TPU v7x, 32 devices: a whole 2x2x4 slice. The times are simulated.
32 devices in a mesh: groups: 2 (over y), tok: 8 (over z, x), head: 2 (over core).
Axes of the slice: x: 2, y: 2, z: 4, core: 2. Of those that a mesh axis runs over, the one named last changes fastest.
Arguments:
- interior_element_embedding: bfloat16 [2048, 1024], P(('groups', 'tok')), parts along dimension 0, may hold values from -70 to 70
- boundary_element_embedding: bfloat16 [512, 1024], P(('groups', 'tok')), parts along dimension 0, may hold values from -70 to 70
- interior_landmark_position: int32 [256], P(('groups', 'tok')), parts along dimension 0, may hold values from 0 to 1023, as said below
- boundary_landmark_position: int32 [128], P(('groups', 'tok')), parts along dimension 0, may hold values from 0 to 255, as said below
- interior_rescaling_factor: float32 [1024], replicated, may hold values from 0.1 to 1.9
- boundary_rescaling_factor: float32 [1024], replicated, may hold values from 0.1 to 1.9
- question_projection_matrix: bfloat16 [1024, 1024], P(None, 'head'), may hold values from -0.1875 to 0.1875
- lookup_projection_matrix: bfloat16 [1024, 1024], P(None, 'head'), may hold values from -0.1875 to 0.1875
- content_projection_matrix: bfloat16 [1024, 1024], P(None, 'head'), may hold values from -0.1875 to 0.1875
- final_projection_matrix: bfloat16 [1024, 1024], P('head'), may hold values from -0.1875 to 0.1875
- channel_logit_divisor: float32 [16], P('head'), may hold values from 0.5 to 96
Outputs:
- update: bfloat16 [2048, 1024], P(('groups', 'tok'), 'head'), parts along dimension 0
There are 2 independent parts, one for each index of `groups`. A program takes and returns all parts, laid end to end along the dimension named above; an argument that names none is the same for every part. Nothing has to cross between parts.
Inputs may be any that keep to these rules, and one draw needn't show every extreme that they name: `interior_landmark_position`: anchor i lies among the 128 cells of block i // 16, that is from (i // 16) * 128 on; no cell is named twice; cell 0 and the last cell of the last block are always anchors. `boundary_landmark_position`: anchor i lies among the 32 cells of block i // 8, that is from (i // 8) * 32 on; no cell is named twice; cell 0 and the last cell of the last block are always anchors.
All inputs are finite; a program needn't handle non-finite values.
Results may differ from a plain program's by a relative error of at most 0.012.
The roundings to bfloat16 on the way count: a program that leaves them out, or rounds other values in their place, can miss the bound.
Values may be sent and summed in bfloat16 or wider, within the bound.
No kernel may reach another device: no remote copies, remote signals or barrier semaphores. Data moves between devices by JAX's collectives and lax.ppermute only.
A program may use at most 64 MiB of HBM per device.

v0:
```python
import math

import jax
import jax.numpy as jnp
from jax import lax
from jax.sharding import PartitionSpec as P

epsilon = 1e-06
key_block = 512


def rms_rows(cells, gain):
    values = cells.astype(jnp.float32)
    mean_square = jnp.mean(values * values, axis=1, keepdims=True)
    return (values * lax.rsqrt(mean_square + epsilon) * gain).astype(jnp.bfloat16)


def absorb(running, key_rows, value_rows, queries, logit_multiplier):
    run_max, denominator, accumulated = running
    parallel_channel_total, channel_dimension, cell_count = queries.shape
    key_heads = key_rows.reshape(key_rows.shape[0], parallel_channel_total, channel_dimension)
    value_heads = value_rows.reshape(value_rows.shape[0], parallel_channel_total, channel_dimension)
    scores = (
        jnp.einsum("jhd,hdc->hjc", key_heads, queries, preferred_element_type=jnp.float32)
        * logit_multiplier
    )
    new_max = jnp.maximum(run_max, jnp.max(scores, axis=1))
    shrink = jnp.exp(run_max - new_max)
    exp_scores = jnp.exp(scores - new_max[:, None, :])
    denominator = denominator * shrink + jnp.sum(exp_scores, axis=1)
    added = jnp.einsum(
        "jhd,hjc->hdc",
        value_heads,
        exp_scores.astype(jnp.bfloat16),
        preferred_element_type=jnp.float32,
    )
    accumulated = accumulated * shrink[:, None, :] + added
    return (new_max, denominator, accumulated)


def make_folder(queries, logit_multiplier):

    def folder(running, shard_rows, offset):
        key_rows, value_rows = shard_rows
        row_count = key_rows.shape[0]
        if row_count > key_block and row_count % key_block == 0:
            row_width = key_rows.shape[1]

            def scan_step(state, key_pair):
                return (absorb(state, key_pair[0], key_pair[1], queries, logit_multiplier), None)

            stacked = (
                key_rows.reshape(row_count // key_block, key_block, row_width),
                value_rows.reshape(row_count // key_block, key_block, row_width),
            )
            running, unused = lax.scan(scan_step, running, stacked)
            return running
        return absorb(running, key_rows, value_rows, queries, logit_multiplier)

    return folder


def project_pair(rows_in, lookup_projection_matrix, content_projection_matrix):
    key_rows = jnp.dot(
        rows_in, lookup_projection_matrix, preferred_element_type=jnp.float32
    ).astype(jnp.bfloat16)
    value_rows = jnp.dot(
        rows_in, content_projection_matrix, preferred_element_type=jnp.float32
    ).astype(jnp.bfloat16)
    return (key_rows, value_rows)


def body(
    interior_element_embedding,
    boundary_element_embedding,
    interior_landmark_position,
    boundary_landmark_position,
    interior_rescaling_factor,
    boundary_rescaling_factor,
    question_projection_matrix,
    lookup_projection_matrix,
    content_projection_matrix,
    final_projection_matrix,
    channel_logit_divisor,
):
    block_index = lax.axis_index("tok")
    vol_normed = rms_rows(interior_element_embedding, interior_rescaling_factor)
    vol_local = interior_landmark_position - block_index * interior_element_embedding.shape[0]
    surf_local = boundary_landmark_position - block_index * boundary_element_embedding.shape[0]
    vol_picked = jnp.take(vol_normed, vol_local, axis=0)
    surf_picked = rms_rows(
        jnp.take(boundary_element_embedding, surf_local, axis=0), boundary_rescaling_factor
    )
    parallel_channel_total = channel_logit_divisor.shape[0]
    local_width = question_projection_matrix.shape[1]
    channel_dimension = local_width // parallel_channel_total
    cell_count = interior_element_embedding.shape[0]
    query_cols = lax.dot_general(
        question_projection_matrix,
        vol_normed,
        (((0,), (1,)), ((), ())),
        preferred_element_type=jnp.float32,
    )
    queries = query_cols.astype(jnp.bfloat16).reshape(
        parallel_channel_total, channel_dimension, cell_count
    )
    logit_multiplier = (channel_logit_divisor * (1.0 / math.sqrt(channel_dimension)))[:, None, None]
    start_state = (
        jnp.full((parallel_channel_total, cell_count), -1e30, jnp.float32),
        jnp.zeros((parallel_channel_total, cell_count), jnp.float32),
        jnp.zeros((parallel_channel_total, channel_dimension, cell_count), jnp.float32),
    )
    folder = make_folder(queries, logit_multiplier)
    anchors = jnp.concatenate([vol_picked, surf_picked], axis=0)
    anchor_keys, anchor_values = project_pair(
        anchors, lookup_projection_matrix, content_projection_matrix
    )
    final_state = folder(
        start_state,
        (
            lax.all_gather(anchor_keys, "tok", axis=0, tiled=True),
            lax.all_gather(anchor_values, "tok", axis=0, tiled=True),
        ),
        jnp.int32(0),
    )
    run_max, denominator, accumulated = final_state
    context = (
        (accumulated / denominator[:, None, :])
        .astype(jnp.bfloat16)
        .reshape(local_width, cell_count)
    )
    head_terms = lax.dot_general(
        context,
        final_projection_matrix,
        (((0,), (0,)), ((), ())),
        preferred_element_type=jnp.float32,
    )
    full_width = head_terms.shape[1]
    share = lax.psum_scatter(
        head_terms.astype(jnp.bfloat16), "head", scatter_dimension=1, tiled=True
    ).astype(jnp.float32)
    squares = lax.psum(jnp.sum(share * share, axis=1), "head")
    return (share * lax.rsqrt(squares[:, None] / full_width + epsilon)).astype(jnp.bfloat16)


def solution(mesh):
    placed = (
        P(("groups", "tok"), None),
        P(("groups", "tok"), None),
        P(("groups", "tok")),
        P(("groups", "tok")),
        P(),
        P(),
        P(None, "head"),
        P(None, "head"),
        P(None, "head"),
        P("head", None),
        P("head"),
    )
    return jax.shard_map(
        body, mesh=mesh, in_specs=placed, out_specs=P(("groups", "tok"), "head"), check_vma=False
    )
```

profile of v0, /device:TPU:0, one launch (start us, length us, event | category | flops | bytes accessed | tf_op | source)
XLA Modules:
  0.0 101.6 jit_solution(5933496600620693102)
XLA Ops:
  6.6 0.8 compare_and_fusion
  7.4 1.4 %gather_fusion.1 = bf16[8,1024]{1,0:T(8,128)(2,1)S(1)} fusion(bf16[32,1024]{1,0:T(8,128)(2,1)} %param.12, s32[1024]{0:T(1024)S(1)} %pad_clamp_fusion), kind=kCustom, calls=%fused_computation.1 | custom fusion | bytes 32800 | tf_op jit(solution)/shard_map/jit(_take)/gather | solution.py:92
  8.8 0.2 fusion.12
  9.0 0.7 compare_and_fusion.1
  9.7 1.1 %fusion.5 = f32[128]{0:T(128)S(1)} fusion(bf16[128,1024]{1,0:T(8,128)(2,1)} %param.11), kind=kLoop, calls=%fused_computation.16 | loop fusion | flops 393088 | bytes 262656 | tf_op jit(solution)/shard_map/reduce_sum | solution.py:14
  10.8 0.8 fusion.14
  11.6 0.8 fusion.7
  12.4 0.6 gather_fusion
  13.1 0.2 convolution_convert_fusion.3
  13.3 32.4 %all_gather.6 = bf16[192,512]{1,0:T(8,128)(2,1)S(1)} all-gather(bf16[24,512]{1,0:T(8,128)(2,1)S(1)} %convolution_convert_fusion.3), channel_id=1, replica_groups=mesh['groups'=2,'tok'=8,'head'=2] {'tok'}, dimensions={0}, use_global_device_ids=true | all-gather | bytes 221184 | tf_op jit(solution)/shard_map/all_gather | solution.py:121
  45.7 0.1 copy.15
  45.9 1.5 %fusion.2 = bf16[512,128]{0,1:T(8,128)(2,1)S(1)} fusion(bf16[128,1024]{1,0:T(8,128)(2,1)S(1)} %fusion.7, bf16[1024,512]{1,0:T(8,128)(2,1)} %param.17), kind=kOutput, calls=%fused_computation.8 | convolution fusion | flops 134283264 | bytes 1441792 | tf_op jit(solution)/shard_map/dot_general | solution.py:98
  47.5 0.5 copy-done.5
  48.1 0.4 fusion.18
  48.6 0.7 copy-done.3
  49.3 0.2 convolution_convert_fusion.2
  49.5 30.6 %all_gather.7 = bf16[192,512]{1,0:T(8,128)(2,1)S(1)} all-gather(bf16[24,512]{1,0:T(8,128)(2,1)S(1)} %convolution_convert_fusion.2), channel_id=1, replica_groups=mesh['groups'=2,'tok'=8,'head'=2] {'tok'}, dimensions={0}, use_global_device_ids=true | all-gather | bytes 221184 | tf_op jit(solution)/shard_map/all_gather | solution.py:122
  80.2 0.1 copy.17
  80.3 0.3 fusion.1
  80.6 1.0 %convolution_convert_fusion = bf16[128,1024]{1,0:T(8,128)(2,1)} fusion(bf16[512,128]{1,0:T(8,128)(2,1)S(1)} %bitcast.18, bf16[512,1024]{1,0:T(8,128)(2,1)S(1)} %copy-done), kind=kOutput, calls=%fused_computation.3 | convolution fusion | flops 134348800 | bytes 1441792 | tf_op jit(solution)/shard_map/dot_general | solution.py:132
  81.6 8.8 %reduce-scatter.2.cloned.1.call-done = bf16[128,512]{1,0:T(8,128)(2,1)} async-done(((bf16[128,1024]{1,0:T(8,128)(2,1)}), bf16[128,512]{1,0:T(8,128)(2,1)}) %reduce-scatter.2.cloned.1.call-update) | async-done | bytes 131088 | tf_op jit(solution)/shard_map/reduce_scatter | solution.py:139
  90.4 1.1 %fusion.10 = f32[128]{0:T(128)S(1)} fusion(bf16[128,512]{1,0:T(8,128)(2,1)} %reduce-scatter.2.cloned.1.call-done), kind=kLoop, calls=%fused_computation.22 | loop fusion | flops 196480 | bytes 131584 | tf_op jit(solution)/shard_map/reduce_sum | solution.py:142
  91.5 2.5 %psum.7 = f32[128]{0:T(128)S(1)} all-reduce(f32[128]{0:T(128)S(1)} %fusion.10), channel_id=1, replica_groups=mesh['groups'=2,'tok'=8,'head'=2] {'head'}, use_global_device_ids=true, to_apply=%region_6.7 | all-reduce | flops 128 | bytes 1024 | tf_op jit(solution)/shard_map/psum | solution.py:142
  94.0 0.7 fusion.11
  (23 shorter events, 0.4 us)
Async XLA Ops:
  6.5 74.0 %copy-start = (bf16[512,1024]{1,0:T(8,128)(2,1)S(1)}, bf16[512,1024]{1,0:T(8,128)(2,1)}, u32[]{:S(2)}) copy-start(bf16[512,1024]{1,0:T(8,128)(2,1)} %param.20) | copy-start | bytes 3145732
  6.5 5.0 %copy-start.1 = (bf16[128,1024]{1,0:T(8,128)(2,1)S(1)}, bf16[128,1024]{1,0:T(8,128)(2,1)}, u32[]{:S(2)}) copy-start(bf16[128,1024]{1,0:T(8,128)(2,1)} %param.11) | copy-start | bytes 786436
  6.5 6.5 %copy-start.2 = (bf16[1024,512]{1,0:T(8,128)(2,1)S(1)}, bf16[1024,512]{1,0:T(8,128)(2,1)}, u32[]{:S(2)}) copy-start(bf16[1024,512]{1,0:T(8,128)(2,1)} %param.18) | copy-start | bytes 3145732
  6.5 83.9 %reduce-scatter.2.cloned.1.call-start = ((), (), s32[]{:S(2)}) async-start(), calls=%async_computation.1 | async-start | bytes 393216 | tf_op jit(solution)/shard_map/reduce_scatter | solution.py:139
  47.4 0.7 copy-start.5
  48.1 1.2 %copy-start.3 = (bf16[1024,512]{1,0:T(8,128)(2,1)S(1)}, bf16[1024,512]{1,0:T(8,128)(2,1)}, u32[]{:S(2)}) copy-start(bf16[1024,512]{1,0:T(8,128)(2,1)} %param.19) | copy-start | bytes 3145732
  90.4 3.6 %copy-start.4 = (bf16[128,512]{1,0:T(8,128)(2,1)S(1)}, bf16[128,512]{1,0:T(8,128)(2,1)}, u32[]{:S(2)}) copy-start(bf16[128,512]{1,0:T(8,128)(2,1)} %reduce-scatter.2.cloned.1.call-done) | copy-start | bytes 393220
Sparse Core Ops, SparseCore 0:
  81.8 8.5 reduce-scatter.1
where the time goes:
time: 102 us
  blocking collectives  65.5 us (64%)
  between operations  13.5 us (13%)
  waiting for transfers between devices  8.78 us (9%)
  other arithmetic  6.43 us (6%)
  matrix products  3.67 us (4%)
  local copies, waits for them, and re-layouts  3.66 us (4%)
    all_gather x1, blocking collectives, body(): lax.all_gather(anchor_keys, 'tok', axis=0, tiled=True)  32.4 us
    all_gather x1, blocking collectives, body(): lax.all_gather(anchor_values, 'tok', axis=0, tiled=True)  30.6 us
    reduce_scatter x1, waiting for transfers between devices, body(): lax.psum_scatter(head_terms.astype(jnp.bfloat16), 'head', scatter_dimensi...  8.76 us
    psum x1, blocking collectives, body(): squares = lax.psum(jnp.sum(share * share, axis=1), 'head')  2.47 us
  transfers between devices with their start and end apart: 1, of which 1 were waited for; matrix products, arithmetic and copies ran while one was open for 0% of the time, Pallas kernels for 0%

commit v1 on v0

--- a/solution.py
+++ b/solution.py
@@ -1,8 +1,11 @@
+import functools
 import math
 
 import jax
 import jax.numpy as jnp
 from jax import lax
+from jax.experimental import pallas as pl
+from jax.experimental.pallas import tpu as pltpu
 from jax.sharding import PartitionSpec as P
 
 epsilon = 1e-06
@@ -70,7 +73,7 @@
     return (key_rows, value_rows)
 
 
-def body(
+def gathered_body(
     interior_element_embedding,
     boundary_element_embedding,
     interior_landmark_position,
@@ -143,6 +146,189 @@
     return (share * lax.rsqrt(squares[:, None] / full_width + epsilon)).astype(jnp.bfloat16)
 
 
+def in_vmem(array):
+    return pltpu.with_memory_space_constraint(array, pltpu.VMEM)
+
+
+def normed(values, gain):
+    mean_square = jnp.mean(values * values, axis=1, keepdims=True)
+    return (values * lax.rsqrt(mean_square + epsilon) * gain).astype(jnp.bfloat16)
+
+
+def pick_rows(positions, first, cells):
+    picks, rows = positions.shape[0], cells.shape[0]
+    row = lax.broadcasted_iota(jnp.int32, (picks, rows), 0)
+    column = lax.broadcasted_iota(jnp.int32, (picks, rows), 1)
+    chosen = jnp.zeros((picks, rows), jnp.int32)
+    for pick in range(picks):
+        chosen = jnp.where(row == pick, positions[pick] - first, chosen)
+    one_hot = jnp.where(chosen == column, 1.0, 0.0).astype(jnp.bfloat16)
+    return jnp.dot(one_hot, cells, preferred_element_type=jnp.float32)
+
+
+def anchor_kernel(vol_position, surf_position, vol, surf, vol_gain, surf_gain, anchors):
+    block_index = lax.axis_index("tok")
+    vol_rows = pick_rows(vol_position, block_index * vol.shape[0], vol[...])
+    surf_rows = pick_rows(surf_position, block_index * surf.shape[0], surf[...])
+    parts = [normed(vol_rows, vol_gain[...]), normed(surf_rows, surf_gain[...])]
+    stacked = jnp.concatenate([part.astype(jnp.float32) for part in parts], axis=0)
+    anchors[...] = stacked.astype(jnp.bfloat16)
+
+
+def query_kernel(vol, gain, projection, value_projection, queries, value_turned):
+    vol_normed = normed(vol[...].astype(jnp.float32), gain[...])
+    cells = vol.shape[0]
+    columns = lax.dot_general(
+        projection[...], vol_normed, (((0,), (1,)), ((), ())), preferred_element_type=jnp.float32
+    ).astype(jnp.bfloat16)
+    pairs, pair_width, _ = queries.shape
+    half = pair_width // 2
+    upper = lax.broadcasted_iota(jnp.int32, (pair_width, cells), 0) < half
+    for pair in range(pairs):
+        block = columns[pair * pair_width : (pair + 1) * pair_width, :].astype(jnp.float32)
+        queries[pair, :, :cells] = jnp.where(upper, block, 0.0).astype(jnp.bfloat16)
+        queries[pair, :, cells:] = jnp.where(upper, 0.0, block).astype(jnp.bfloat16)
+    value_turned[...] = value_projection[...].T
+
+
+def attention_kernel(block_count, divisor, queries, lookup, value_turned, final, *rest):
+    blocks, terms, context = rest[:block_count], rest[block_count], rest[block_count + 1]
+    pairs, pair_width, wide = queries.shape
+    half, cells = pair_width // 2, wide // 2
+    rows = [block[...].astype(jnp.float32) for block in blocks[:-2]]
+    rows.append(blocks[-2][...].astype(jnp.float32) + blocks[-1][...].astype(jnp.float32))
+    anchors = jnp.concatenate(rows, axis=0).astype(jnp.bfloat16)
+    keys = jnp.dot(anchors, lookup[...], preferred_element_type=jnp.float32).astype(jnp.bfloat16)
+    values = lax.dot_general(
+        value_turned[...], anchors, (((1,), (1,)), ((), ())), preferred_element_type=jnp.float32
+    ).astype(jnp.bfloat16)
+    left = lax.broadcasted_iota(jnp.int32, (1, wide), 1) < cells
+    scale = 1.0 / math.sqrt(half)
+    for pair in range(pairs):
+        span = slice(pair * pair_width, (pair + 1) * pair_width)
+        multiplier = jnp.where(left, divisor[2 * pair] * scale, divisor[2 * pair + 1] * scale)
+        scores = jnp.dot(keys[:, span], queries[pair], preferred_element_type=jnp.float32) * multiplier
+        exp_scores = jnp.exp(scores - jnp.max(scores, axis=0, keepdims=True))
+        denominator = jnp.sum(exp_scores, axis=0, keepdims=True)
+        added = jnp.dot(
+            values[span, :], exp_scores.astype(jnp.bfloat16), preferred_element_type=jnp.float32
+        )
+        added = added / denominator
+        context[span, :] = jnp.concatenate(
+            [added[:half, :cells], added[half:, cells:]], axis=0
+        ).astype(jnp.bfloat16)
+    terms[...] = lax.dot_general(
+        context[...], final[...], (((0,), (0,)), ((), ())), preferred_element_type=jnp.float32
+    ).astype(jnp.bfloat16)
+
+
+def finish_kernel(own, other, update):
+    mixed = own[...].astype(jnp.float32) + other[...].astype(jnp.float32)
+    factor = lax.rsqrt(jnp.mean(mixed * mixed, axis=1, keepdims=True) + epsilon)
+    width = update.shape[1]
+    for part in range(mixed.shape[1] // width):
+
+        @pl.when(lax.axis_index("head") == part)
+        def _():
+            update[...] = (mixed[:, part * width : (part + 1) * width] * factor).astype(update.dtype)
+
+
+SMEM = pl.BlockSpec(memory_space=pltpu.SMEM)
+VMEM = pl.BlockSpec(memory_space=pltpu.VMEM)
+PARAMS = pltpu.CompilerParams(vmem_limit_bytes=32 * 1024 * 1024)
+
+
+def direct_body(
+    shards,
+    interior_element_embedding,
+    boundary_element_embedding,
+    interior_landmark_position,
+    boundary_landmark_position,
+    interior_rescaling_factor,
+    boundary_rescaling_factor,
+    question_projection_matrix,
+    lookup_projection_matrix,
+    content_projection_matrix,
+    final_projection_matrix,
+    channel_logit_divisor,
+):
+    cells, width = interior_element_embedding.shape
+    local_width = question_projection_matrix.shape[1]
+    heads = channel_logit_divisor.shape[0]
+    pair_width = 2 * (local_width // heads)
+    picks = interior_landmark_position.shape[0] + boundary_landmark_position.shape[0]
+    vol_gain = interior_rescaling_factor.reshape(1, width)
+    surf_gain = boundary_rescaling_factor.reshape(1, width)
+    anchors = pl.pallas_call(
+        anchor_kernel,
+        out_shape=jax.ShapeDtypeStruct((picks, width), jnp.bfloat16),
+        in_specs=[SMEM, SMEM, VMEM, VMEM, VMEM, VMEM],
+        out_specs=VMEM,
+        compiler_params=PARAMS,
+        name="anchors",
+    )(
+        interior_landmark_position,
+        boundary_landmark_position,
+        interior_element_embedding,
+        boundary_element_embedding,
+        vol_gain,
+        surf_gain,
+    )
+    arrived = []
+    for odd in range(1, shards, 2):
+        pairs = [(2 * t, 2 * ((t + odd) % shards)) for t in range(shards)]
+        if odd + 1 < shards:
+            pairs += [(2 * t + 1, 2 * ((t + odd + 1) % shards) + 1) for t in range(shards)]
+        arrived.append(lax.ppermute(anchors, ("tok", "head"), pairs))
+    swapped = [lax.ppermute(block, "head", [(0, 1), (1, 0)]) for block in arrived[:-1]]
+    swapped.append(lax.ppermute(arrived[-1], "head", [(0, 1)]))
+    queries, value_turned = pl.pallas_call(
+        query_kernel,
+        out_shape=(
+            jax.ShapeDtypeStruct((heads // 2, pair_width, 2 * cells), jnp.bfloat16),
+            jax.ShapeDtypeStruct((local_width, width), jnp.bfloat16),
+        ),
+        in_specs=[VMEM] * 4,
+        out_specs=(VMEM, VMEM),
+        compiler_params=PARAMS,
+        cost_estimate=pl.CostEstimate(
+            flops=2 * cells * width * local_width, bytes_accessed=4 * width * local_width, transcendentals=0
+        ),
+        name="queries",
+    )(
+        interior_element_embedding,
+        vol_gain,
+        in_vmem(question_projection_matrix),
+        in_vmem(content_projection_matrix),
+    )
+    blocks = [anchors, *arrived[:-1], *swapped[:-1], arrived[-1], swapped[-1]]
+    terms = pl.pallas_call(
+        functools.partial(attention_kernel, len(blocks)),
+        out_shape=jax.ShapeDtypeStruct((cells, width), jnp.bfloat16),
+        in_specs=[SMEM] + [VMEM] * (4 + len(blocks)),
+        out_specs=VMEM,
+        scratch_shapes=[pltpu.VMEM((local_width, cells), jnp.bfloat16)],
+        compiler_params=PARAMS,
+        name="attention",
+    )(
+        channel_logit_divisor,
+        in_vmem(queries),
+        in_vmem(lookup_projection_matrix),
+        in_vmem(value_turned),
+        in_vmem(final_projection_matrix),
+        *[in_vmem(block) for block in blocks],
+    )
+    other = lax.ppermute(terms, "head", [(0, 1), (1, 0)])
+    return pl.pallas_call(
+        finish_kernel,
+        out_shape=jax.ShapeDtypeStruct((cells, local_width), jnp.bfloat16),
+        in_specs=[VMEM, VMEM],
+        out_specs=VMEM,
+        compiler_params=PARAMS,
+        name="finish",
+    )(in_vmem(terms), in_vmem(other))
+
+
 def solution(mesh):
     placed = (
         P(("groups", "tok"), None),
@@ -157,6 +343,9 @@
         P("head", None),
         P("head"),
     )
+    shards = mesh.shape["tok"]
+    small = shards % 2 == 0 and shards <= 16 and mesh.shape["head"] == 2
+    body = functools.partial(direct_body, shards) if small else gathered_body
     return jax.shard_map(
         body, mesh=mesh, in_specs=placed, out_specs=P(("groups", "tok"), "head"), check_vma=False
     )

time: 102 us -> 31.9 us (0.31)
  blocking collectives: 65.5 us -> 0 us
  between operations: 13.5 us -> 0.1 us
  starting transfers between devices: 0.01 us -> 12.7 us
  other arithmetic: 6.43 us -> 0 us
  Pallas kernels: 0 us -> 4.91 us
  matrix products: 3.67 us -> 0 us
  local copies, waits for them, and re-layouts: 3.66 us -> 7.06 us
  waiting for transfers between devices: 8.78 us -> 6.66 us
    all_gather x2 -> x0, blocking collectives: 63.1 us -> none  [the longest x1 32.4 us: body(): lax.all_gather(anchor_keys, 'tok', axis=0, tiled=True)]
    ppermute x0 -> x9, starting transfers between devices: none -> 12.7 us  [the longest x4 10.9 us: direct_body(): arrived.append(lax.ppermute(anchors, ('tok', 'head'), pairs))]
    reduce_scatter x1 -> x0, waiting for transfers between devices: 8.76 us -> none  [body(): lax.psum_scatter(head_terms.astype(jnp.bfloat16), 'head', scatter_dimensi...]
    ppermute x0 -> x9, waiting for transfers between devices: none -> 6.66 us  [the longest x4 5.49 us: direct_body(): arrived.append(lax.ppermute(anchors, ('tok', 'head'), pairs))]
    unnamed x12 -> x22, local copies, waits for them, and re-layouts: 1.25 us -> 7.06 us
    pallas_call x0 -> x4, Pallas kernels: none -> 4.91 us  [the longest x1 2.57 us: direct_body(): pl.pallas_call(functools.partial(attention_kernel, len(blocks)), out_shap...]
    dot_general x6 -> x0, matrix products: 3.67 us -> none  [the longest x1 1.53 us: body(): lax.dot_general(question_projection_matrix, vol_normed, (((0,), (1,)), ((...]
    reduce_sum x4 -> x0, other arithmetic: 2.48 us -> none  [the longest x2 1.28 us: rms_rows(): mean_square = jnp.mean(values * values, axis=1, keepdims=True)]
  transfers between devices with their start and end apart: 1 -> 9, of which waited for: 1 -> 4; matrix products, arithmetic and copies ran while one was open for 0% -> 0% of each run, Pallas kernels for 0% -> 2%
where the time goes in v1:
time: 31.9 us; the launch traced here: 31.5 us
  starting transfers between devices  12.7 us (40%)
  local copies, waits for them, and re-layouts  7.06 us (22%)
  waiting for transfers between devices  6.66 us (21%)
  Pallas kernels  4.91 us (15%)
    ppermute x4, starting transfers between devices, direct_body(): arrived.append(lax.ppermute(anchors, ('tok', 'head'), pairs))  10.9 us
    unnamed x22, local copies, waits for them, and re-layouts  7.06 us
    ppermute x4, waiting for transfers between devices, direct_body(): arrived.append(lax.ppermute(anchors, ('tok', 'head'), pairs))  5.49 us
    pallas_call x1, Pallas kernels, direct_body(): pl.pallas_call(functools.partial(attention_kernel, len(blocks)), out_shap...  2.57 us
    ppermute x1, starting transfers between devices, direct_body(): swapped.append(lax.ppermute(arrived[-1], 'head', [(0, 1)]))  1.28 us
    ppermute x1, waiting for transfers between devices, direct_body(): other = lax.ppermute(terms, 'head', [(0, 1), (1, 0)])  1.16 us
    pallas_call x1, Pallas kernels, direct_body(): pl.pallas_call(finish_kernel, out_shape=jax.ShapeDtypeStruct((cells, loca...  0.83 us
    pallas_call x1, Pallas kernels, direct_body(): pl.pallas_call(anchor_kernel, out_shape=jax.ShapeDtypeStruct((picks, widt...  0.79 us
  transfers between devices with their start and end apart: 9, of which 4 were waited for; matrix products, arithmetic and copies ran while one was open for 0% of the time, Pallas kernels for 2%

profile of v1, /device:TPU:0, one launch (start us, length us, event | category | flops | bytes accessed | tf_op | source)
XLA Modules:
  0.0 31.5 jit_solution(12655090432623457236)
XLA Ops:
  0.0 0.7 %copy-done.8 = s32[16]{0:T(128)S(1)} copy-done((s32[16]{0:T(128)S(1)}, s32[16]{0:T(128)}, u32[]{:S(2)}) %copy-start.8) | copy-done | bytes 88
  0.7 0.0 copy-done.9
  0.7 0.9 %copy-done = bf16[128,1024]{1,0:T(8,128)(2,1)S(1)} copy-done((bf16[128,1024]{1,0:T(8,128)(2,1)S(1)}, bf16[128,1024]{1,0:T(8,128)(2,1)}, u32[]{:S(2)}) %copy-start) | copy-done | bytes 262168
  1.6 0.8 %copy-done.5 = bf16[32,1024]{1,0:T(8,128)(2,1)S(1)} copy-done((bf16[32,1024]{1,0:T(8,128)(2,1)S(1)}, bf16[32,1024]{1,0:T(8,128)(2,1)}, u32[]{:S(2)}) %copy-start.5) | copy-done | bytes 65560
  2.5 0.7 %copy-done.6 = f32[1024]{0:T(1024)S(1)} copy-done((f32[1024]{0:T(1024)S(1)}, f32[1024]{0:T(1024)}, u32[]{:S(2)}) %copy-start.6) | copy-done | bytes 4120
  3.2 0.7 %copy-done.7 = f32[1024]{0:T(1024)S(1)} copy-done((f32[1024]{0:T(1024)S(1)}, f32[1024]{0:T(1024)}, u32[]{:S(2)}) %copy-start.7) | copy-done | bytes 4120
  3.8 0.8 %anchors.1.rest_0_ = bf16[24,1024]{1,0:T(8,128)(2,1)S(1)} custom-call(s32[16]{0:T(128)S(1)} %copy-done.8, s32[8]{0:T(128)S(1)} %copy-done.9, bf16[128,1024]{1,0:T(8,128)(2,1)S(1)} %copy-done, bf16[32,1024]{1,0:T(8,128)(2,1)S(1)} %copy-done.5, f32[1,1024]{1,0:T(1,128)S(1)} %bitcast.2, f32[1,1024]{1,0:T(1,128)S(1)} %bitcast.4), custom_call_target="tpu_custom_call" | custom-call | tf_op jit(solution)/shard_map/anchors/pallas_call | solution.py:262
  4.6 7.9 %collective-permute-start.6 = (bf16[24,1024]{1,0:T(8,128)(2,1)S(1)}, bf16[24,1024]{1,0:T(8,128)(2,1)S(1)}, u32[]{:S(2)}, u32[]{:S(2)}) collective-permute-start(bf16[24,1024]{1,0:T(8,128)(2,1)S(1)} %anchors.1.rest_0_), channel_id=1, source_target_pairs={{0,14},{2,0},{4,2},{6,4},{8,6},{10,8},{12,10},{14,12},{16,30},{18,... | collective-permute-start | bytes 147464 | tf_op jit(solution)/shard_map/ppermute | solution.py:282
  12.5 0.1 collective-permute-start.2
  12.6 2.9 %collective-permute-start.1 = (bf16[24,1024]{1,0:T(8,128)(2,1)S(1)}, bf16[24,1024]{1,0:T(8,128)(2,1)S(1)}, u32[]{:S(2)}, u32[]{:S(2)}) collective-permute-start(bf16[24,1024]{1,0:T(8,128)(2,1)S(1)} %anchors.1.rest_0_), channel_id=1, source_target_pairs={{0,6},{2,8},{4,10},{6,12},{8,14},{10,0},{12,2},{14,4},{1,9},{3,11}... | collective-permute-start | bytes 147464 | tf_op jit(solution)/shard_map/ppermute | solution.py:282
  15.5 1.3 %collective-permute-start.7 = (bf16[24,1024]{1,0:T(8,128)(2,1)S(1)}, bf16[24,1024]{1,0:T(8,128)(2,1)S(1)}, u32[]{:S(2)}, u32[]{:S(2)}) collective-permute-start(bf16[24,1024]{1,0:T(8,128)(2,1)S(1)} %collective-permute-done.6.rest_7_), channel_id=1, source_target_pairs={{0,1},{2,3},{4,5},{6,7},{8,9},{10,11},{12,13},{14,15},{16,17},{18,... | collective-permute-start | bytes 147464 | tf_op jit(solution)/shard_map/ppermute | solution.py:284
  16.8 0.8 %collective-permute-done.2.rest_3_ = bf16[24,1024]{1,0:T(8,128)(2,1)S(1)} collective-permute-done((bf16[24,1024]{1,0:T(8,128)(2,1)S(1)}, bf16[24,1024]{1,0:T(8,128)(2,1)S(1)}, u32[]{:S(2)}, u32[]{:S(2)}) %collective-permute-start.2) | collective-permute-done | bytes 49184 | tf_op jit(solution)/shard_map/ppermute | solution.py:282
  17.6 1.0 %collective-permute-done.1.rest_2_ = bf16[24,1024]{1,0:T(8,128)(2,1)S(1)} collective-permute-done((bf16[24,1024]{1,0:T(8,128)(2,1)S(1)}, bf16[24,1024]{1,0:T(8,128)(2,1)S(1)}, u32[]{:S(2)}, u32[]{:S(2)}) %collective-permute-start.1) | collective-permute-done | bytes 49184 | tf_op jit(solution)/shard_map/ppermute | solution.py:282
  18.5 3.7 %collective-permute-done.rest_1_ = bf16[24,1024]{1,0:T(8,128)(2,1)S(1)} collective-permute-done((bf16[24,1024]{1,0:T(8,128)(2,1)S(1)}, bf16[24,1024]{1,0:T(8,128)(2,1)S(1)}, u32[]{:S(2)}, u32[]{:S(2)}) %collective-permute-start) | collective-permute-done | bytes 49184 | tf_op jit(solution)/shard_map/ppermute | solution.py:282
  22.3 1.2 %copy-done.1 = bf16[1024,512]{1,0:T(8,128)(2,1)S(1)} copy-done((bf16[1024,512]{1,0:T(8,128)(2,1)S(1)}, bf16[1024,512]{1,0:T(8,128)(2,1)}, u32[]{:S(2)}) %copy-start.1) | copy-done | bytes 1048600
  23.5 1.2 %copy-done.2 = bf16[1024,512]{1,0:T(8,128)(2,1)S(1)} copy-done((bf16[1024,512]{1,0:T(8,128)(2,1)S(1)}, bf16[1024,512]{1,0:T(8,128)(2,1)}, u32[]{:S(2)}) %copy-start.2) | copy-done | bytes 1048600
  24.8 0.7 %queries.1 = (bf16[4,128,256]{2,1,0:T(8,128)(2,1)S(1)}, bf16[512,1024]{1,0:T(8,128)(2,1)S(1)}) custom-call(bf16[128,1024]{1,0:T(8,128)(2,1)S(1)} %copy-done, f32[1,1024]{1,0:T(1,128)S(1)} %bitcast.3, bf16[1024,512]{1,0:T(8,128)(2,1)S(1)} %copy-done.1, bf16[1024,512]{1,0:T(8,128)(2,1)S(1)} %copy-done.2), custom_call_target="tpu_custom_call" | custom-call | flops 134217728 | bytes 2097152 | tf_op jit(solution)/shard_map/queries/pallas_call | solution.py:285
  25.5 0.4 %copy-done.3 = bf16[1024,512]{1,0:T(8,128)(2,1)S(1)} copy-done((bf16[1024,512]{1,0:T(8,128)(2,1)S(1)}, bf16[1024,512]{1,0:T(8,128)(2,1)}, u32[]{:S(2)}) %copy-start.3) | copy-done | bytes 1048600
  26.0 0.3 %copy-done.4 = bf16[512,1024]{1,0:T(8,128)(2,1)S(1)} copy-done((bf16[512,1024]{1,0:T(8,128)(2,1)S(1)}, bf16[512,1024]{1,0:T(8,128)(2,1)}, u32[]{:S(2)}) %copy-start.4) | copy-done | bytes 1048600
  26.3 0.0 copy-done.10
  26.3 2.6 %attention.1.own = bf16[128,1024]{1,0:T(8,128)(2,1)S(1)} custom-call(f32[8]{0:T(128)S(1)} %copy-done.10, bf16[4,128,256]{2,1,0:T(8,128)(2,1)S(1)} %get-tuple-element.7.queries, bf16[1024,512]{1,0:T(8,128)(2,1)S(1)} %copy-done.3, bf16[512,1024]{1,0:T(8,128)(2,1)S(1)} %get-tuple-element.8.value_turned, bf16[512,1024]{1,0:T(8,128)(2,1)S(1)} %copy-done.4, ...), custom_call_target="tpu_custom_call" | custom-call | tf_op jit(solution)/shard_map/attention/pallas_call | solution.py:305
  28.9 0.6 %collective-permute-start.8 = (bf16[128,1024]{1,0:T(8,128)(2,1)S(1)}, bf16[128,1024]{1,0:T(8,128)(2,1)S(1)}, u32[]{:S(2)}, u32[]{:S(2)}) collective-permute-start(bf16[128,1024]{1,0:T(8,128)(2,1)S(1)} %attention.1.own), channel_id=1, source_target_pairs={{0,1},{1,0},{2,3},{3,2},{4,5},{5,4},{6,7},{7,6},{8,9},{9,8},{10,11... | collective-permute-start | bytes 786440 | tf_op jit(solution)/shard_map/ppermute | solution.py:321
  29.5 1.2 %collective-permute-done.8.other = bf16[128,1024]{1,0:T(8,128)(2,1)S(1)} collective-permute-done((bf16[128,1024]{1,0:T(8,128)(2,1)S(1)}, bf16[128,1024]{1,0:T(8,128)(2,1)S(1)}, u32[]{:S(2)}, u32[]{:S(2)}) %collective-permute-start.8) | collective-permute-done | bytes 262176 | tf_op jit(solution)/shard_map/ppermute | solution.py:321
  30.6 0.8 %finish.1 = bf16[128,512]{1,0:T(8,128)(2,1)} custom-call(bf16[128,1024]{1,0:T(8,128)(2,1)S(1)} %attention.1.own, bf16[128,1024]{1,0:T(8,128)(2,1)S(1)} %collective-permute-done.8.other), custom_call_target="tpu_custom_call" | custom-call | tf_op jit(solution)/shard_map/finish/pallas_call | solution.py:322
  (20 shorter events, 0.0 us)
Async XLA Ops:
  0.0 0.7 %copy-start.8 = (s32[16]{0:T(128)S(1)}, s32[16]{0:T(128)}, u32[]{:S(2)}) copy-start(s32[16]{0:T(128)} %vol_position.1) | copy-start | bytes 196
  0.0 0.7 %copy-start.9 = (s32[8]{0:T(128)S(1)}, s32[8]{0:T(128)}, u32[]{:S(2)}) copy-start(s32[8]{0:T(128)} %surf_position.1) | copy-start | bytes 100
  0.7 0.9 %copy-start = (bf16[128,1024]{1,0:T(8,128)(2,1)S(1)}, bf16[128,1024]{1,0:T(8,128)(2,1)}, u32[]{:S(2)}) copy-start(bf16[128,1024]{1,0:T(8,128)(2,1)} %vol.3) | copy-start | bytes 786436
  1.6 0.8 %copy-start.5 = (bf16[32,1024]{1,0:T(8,128)(2,1)S(1)}, bf16[32,1024]{1,0:T(8,128)(2,1)}, u32[]{:S(2)}) copy-start(bf16[32,1024]{1,0:T(8,128)(2,1)} %surf.1) | copy-start | bytes 196612
  2.5 0.7 %copy-start.6 = (f32[1024]{0:T(1024)S(1)}, f32[1024]{0:T(1024)}, u32[]{:S(2)}) copy-start(f32[1024]{0:T(1024)} %param.15) | copy-start | bytes 12292
  3.1 0.7 %copy-start.7 = (f32[1024]{0:T(1024)S(1)}, f32[1024]{0:T(1024)}, u32[]{:S(2)}) copy-start(f32[1024]{0:T(1024)} %param.16) | copy-start | bytes 12292
  4.6 10.9 %collective-permute-start.6 = (bf16[24,1024]{1,0:T(8,128)(2,1)S(1)}, bf16[24,1024]{1,0:T(8,128)(2,1)S(1)}, u32[]{:S(2)}, u32[]{:S(2)}) collective-permute-start(bf16[24,1024]{1,0:T(8,128)(2,1)S(1)} %anchors.1.rest_0_), channel_id=1, source_target_pairs={{0,14},{2,0},{4,2},{6,4},{8,6},{10,8},{12,10},{14,12},{16,30},{18,... | collective-permute-start | bytes 147464 | tf_op jit(solution)/shard_map/ppermute | solution.py:282
  12.5 5.0 %collective-permute-start.2 = (bf16[24,1024]{1,0:T(8,128)(2,1)S(1)}, bf16[24,1024]{1,0:T(8,128)(2,1)S(1)}, u32[]{:S(2)}, u32[]{:S(2)}) collective-permute-start(bf16[24,1024]{1,0:T(8,128)(2,1)S(1)} %anchors.1.rest_0_), channel_id=1, source_target_pairs={{0,10},{2,12},{4,14},{6,0},{8,2},{10,4},{12,6},{14,8},{1,13},{3,15... | collective-permute-start | bytes 147464 | tf_op jit(solution)/shard_map/ppermute | solution.py:282
  12.6 6.0 %collective-permute-start.1 = (bf16[24,1024]{1,0:T(8,128)(2,1)S(1)}, bf16[24,1024]{1,0:T(8,128)(2,1)S(1)}, u32[]{:S(2)}, u32[]{:S(2)}) collective-permute-start(bf16[24,1024]{1,0:T(8,128)(2,1)S(1)} %anchors.1.rest_0_), channel_id=1, source_target_pairs={{0,6},{2,8},{4,10},{6,12},{8,14},{10,0},{12,2},{14,4},{1,9},{3,11}... | collective-permute-start | bytes 147464 | tf_op jit(solution)/shard_map/ppermute | solution.py:282
  15.5 6.8 %collective-permute-start = (bf16[24,1024]{1,0:T(8,128)(2,1)S(1)}, bf16[24,1024]{1,0:T(8,128)(2,1)S(1)}, u32[]{:S(2)}, u32[]{:S(2)}) collective-permute-start(bf16[24,1024]{1,0:T(8,128)(2,1)S(1)} %anchors.1.rest_0_), channel_id=1, source_target_pairs={{0,2},{2,4},{4,6},{6,8},{8,10},{10,12},{12,14},{14,0},{1,5},{3,7},... | collective-permute-start | bytes 147464 | tf_op jit(solution)/shard_map/ppermute | solution.py:282
  15.5 10.0 %collective-permute-start.7 = (bf16[24,1024]{1,0:T(8,128)(2,1)S(1)}, bf16[24,1024]{1,0:T(8,128)(2,1)S(1)}, u32[]{:S(2)}, u32[]{:S(2)}) collective-permute-start(bf16[24,1024]{1,0:T(8,128)(2,1)S(1)} %collective-permute-done.6.rest_7_), channel_id=1, source_target_pairs={{0,1},{2,3},{4,5},{6,7},{8,9},{10,11},{12,13},{14,15},{16,17},{18,... | collective-permute-start | bytes 147464 | tf_op jit(solution)/shard_map/ppermute | solution.py:284
  17.6 7.9 %collective-permute-start.5 = (bf16[24,1024]{1,0:T(8,128)(2,1)S(1)}, bf16[24,1024]{1,0:T(8,128)(2,1)S(1)}, u32[]{:S(2)}, u32[]{:S(2)}) collective-permute-start(bf16[24,1024]{1,0:T(8,128)(2,1)S(1)} %collective-permute-done.2.rest_3_), channel_id=1, source_target_pairs={{0,1},{1,0},{2,3},{3,2},{4,5},{5,4},{6,7},{7,6},{8,9},{9,8},{10,11... | collective-permute-start | bytes 147464 | tf_op jit(solution)/shard_map/ppermute | solution.py:283
  18.5 7.0 %collective-permute-start.4 = (bf16[24,1024]{1,0:T(8,128)(2,1)S(1)}, bf16[24,1024]{1,0:T(8,128)(2,1)S(1)}, u32[]{:S(2)}, u32[]{:S(2)}) collective-permute-start(bf16[24,1024]{1,0:T(8,128)(2,1)S(1)} %collective-permute-done.1.rest_2_), channel_id=1, source_target_pairs={{0,1},{1,0},{2,3},{3,2},{4,5},{5,4},{6,7},{7,6},{8,9},{9,8},{10,11... | collective-permute-start | bytes 147464 | tf_op jit(solution)/shard_map/ppermute | solution.py:283
  22.3 3.2 %collective-permute-start.3 = (bf16[24,1024]{1,0:T(8,128)(2,1)S(1)}, bf16[24,1024]{1,0:T(8,128)(2,1)S(1)}, u32[]{:S(2)}, u32[]{:S(2)}) collective-permute-start(bf16[24,1024]{1,0:T(8,128)(2,1)S(1)} %collective-permute-done.rest_1_), channel_id=1, source_target_pairs={{0,1},{1,0},{2,3},{3,2},{4,5},{5,4},{6,7},{7,6},{8,9},{9,8},{10,11... | collective-permute-start | bytes 147464 | tf_op jit(solution)/shard_map/ppermute | solution.py:283
  22.3 1.2 %copy-start.1 = (bf16[1024,512]{1,0:T(8,128)(2,1)S(1)}, bf16[1024,512]{1,0:T(8,128)(2,1)}, u32[]{:S(2)}) copy-start(bf16[1024,512]{1,0:T(8,128)(2,1)} %projection.1) | copy-start | bytes 3145732
  23.5 1.2 %copy-start.2 = (bf16[1024,512]{1,0:T(8,128)(2,1)S(1)}, bf16[1024,512]{1,0:T(8,128)(2,1)}, u32[]{:S(2)}) copy-start(bf16[1024,512]{1,0:T(8,128)(2,1)} %value_projection.1) | copy-start | bytes 3145732
  24.7 1.2 %copy-start.3 = (bf16[1024,512]{1,0:T(8,128)(2,1)S(1)}, bf16[1024,512]{1,0:T(8,128)(2,1)}, u32[]{:S(2)}) copy-start(bf16[1024,512]{1,0:T(8,128)(2,1)} %lookup.1) | copy-start | bytes 3145732
  24.7 1.5 %copy-start.4 = (bf16[512,1024]{1,0:T(8,128)(2,1)S(1)}, bf16[512,1024]{1,0:T(8,128)(2,1)}, u32[]{:S(2)}) copy-start(bf16[512,1024]{1,0:T(8,128)(2,1)} %final.1) | copy-start | bytes 3145732
  25.5 0.8 %copy-start.10 = (f32[8]{0:T(128)S(1)}, f32[8]{0:T(128)}, u32[]{:S(2)}) copy-start(f32[8]{0:T(128)} %divisor.1) | copy-start | bytes 100
  28.9 1.7 %collective-permute-start.8 = (bf16[128,1024]{1,0:T(8,128)(2,1)S(1)}, bf16[128,1024]{1,0:T(8,128)(2,1)S(1)}, u32[]{:S(2)}, u32[]{:S(2)}) collective-permute-start(bf16[128,1024]{1,0:T(8,128)(2,1)S(1)} %attention.1.own), channel_id=1, source_target_pairs={{0,1},{1,0},{2,3},{3,2},{4,5},{5,4},{6,7},{7,6},{8,9},{9,8},{10,11... | collective-permute-start | bytes 786440 | tf_op jit(solution)/shard_map/ppermute | solution.py:321

commit v2 on v1

--- a/solution.py
+++ b/solution.py
@@ -146,8 +146,12 @@
     return (share * lax.rsqrt(squares[:, None] / full_width + epsilon)).astype(jnp.bfloat16)
 
 
-def in_vmem(array):
-    return pltpu.with_memory_space_constraint(array, pltpu.VMEM)
+def in_vmem(*arrays):
+    return [pltpu.with_memory_space_constraint(array, pltpu.VMEM) for array in arrays]
+
+
+def in_hbm(*arrays):
+    return [pltpu.with_memory_space_constraint(array, pltpu.HBM) for array in arrays]
 
 
 def normed(values, gain):
@@ -166,7 +170,21 @@
     return jnp.dot(one_hot, cells, preferred_element_type=jnp.float32)
 
 
-def anchor_kernel(vol_position, surf_position, vol, surf, vol_gain, surf_gain, anchors):
+def fetch(sources, targets, semaphores):
+    copies = [
+        pltpu.make_async_copy(source, target, semaphores.at[number])
+        for number, (source, target) in enumerate(zip(sources, targets))
+    ]
+    for copy in copies:
+        copy.start()
+    return copies
+
+
+def anchor_kernel(*refs):
+    sources, anchors, targets, semaphores = refs[:6], refs[6], refs[7:13], refs[13]
+    vol_position, surf_position, vol, surf, vol_gain, surf_gain = targets
+    for copy in fetch(sources, targets, semaphores):
+        copy.wait()
     block_index = lax.axis_index("tok")
     vol_rows = pick_rows(vol_position, block_index * vol.shape[0], vol[...])
     surf_rows = pick_rows(surf_position, block_index * surf.shape[0], surf[...])
@@ -175,7 +193,13 @@
     anchors[...] = stacked.astype(jnp.bfloat16)
 
 
-def query_kernel(vol, gain, projection, value_projection, queries, value_turned):
+def query_kernel(*refs):
+    sources, (queries, lookup, value_turned, final) = refs[:6], refs[6:10]
+    (vol, gain, projection, value_projection), semaphores = refs[10:14], refs[14]
+    targets = (vol, gain, projection, value_projection, lookup, final)
+    copies = fetch(sources, targets, semaphores)
+    for copy in copies[:3]:
+        copy.wait()
     vol_normed = normed(vol[...].astype(jnp.float32), gain[...])
     cells = vol.shape[0]
     columns = lax.dot_general(
@@ -188,7 +212,10 @@
         block = columns[pair * pair_width : (pair + 1) * pair_width, :].astype(jnp.float32)
         queries[pair, :, :cells] = jnp.where(upper, block, 0.0).astype(jnp.bfloat16)
         queries[pair, :, cells:] = jnp.where(upper, 0.0, block).astype(jnp.bfloat16)
+    copies[3].wait()
     value_turned[...] = value_projection[...].T
+    for copy in copies[4:]:
+        copy.wait()
 
 
 def attention_kernel(block_count, divisor, queries, lookup, value_turned, final, *rest):
@@ -196,7 +223,12 @@
     pairs, pair_width, wide = queries.shape
     half, cells = pair_width // 2, wide // 2
     rows = [block[...].astype(jnp.float32) for block in blocks[:-2]]
-    rows.append(blocks[-2][...].astype(jnp.float32) + blocks[-1][...].astype(jnp.float32))
+    first_core = lax.axis_index("head") == 0
+    rows.append(
+        jnp.where(
+            first_core, blocks[-2][...].astype(jnp.float32), blocks[-1][...].astype(jnp.float32)
+        )
+    )
     anchors = jnp.concatenate(rows, axis=0).astype(jnp.bfloat16)
     keys = jnp.dot(anchors, lookup[...], preferred_element_type=jnp.float32).astype(jnp.bfloat16)
     values = lax.dot_general(
@@ -235,6 +267,7 @@
 
 SMEM = pl.BlockSpec(memory_space=pltpu.SMEM)
 VMEM = pl.BlockSpec(memory_space=pltpu.VMEM)
+HBM = pl.BlockSpec(memory_space=pltpu.HBM)
 PARAMS = pltpu.CompilerParams(vmem_limit_bytes=32 * 1024 * 1024)
 
 
@@ -262,46 +295,75 @@
     anchors = pl.pallas_call(
         anchor_kernel,
         out_shape=jax.ShapeDtypeStruct((picks, width), jnp.bfloat16),
-        in_specs=[SMEM, SMEM, VMEM, VMEM, VMEM, VMEM],
+        in_specs=[HBM] * 6,
         out_specs=VMEM,
+        scratch_shapes=[
+            pltpu.SMEM(interior_landmark_position.shape, jnp.int32),
+            pltpu.SMEM(boundary_landmark_position.shape, jnp.int32),
+            pltpu.VMEM(interior_element_embedding.shape, jnp.bfloat16),
+            pltpu.VMEM(boundary_element_embedding.shape, jnp.bfloat16),
+            pltpu.VMEM((1, width), jnp.float32),
+            pltpu.VMEM((1, width), jnp.float32),
+            pltpu.SemaphoreType.DMA((6,)),
+        ],
         compiler_params=PARAMS,
         name="anchors",
     )(
-        interior_landmark_position,
-        boundary_landmark_position,
-        interior_element_embedding,
-        boundary_element_embedding,
-        vol_gain,
-        surf_gain,
-    )
-    arrived = []
-    for odd in range(1, shards, 2):
-        pairs = [(2 * t, 2 * ((t + odd) % shards)) for t in range(shards)]
-        if odd + 1 < shards:
-            pairs += [(2 * t + 1, 2 * ((t + odd + 1) % shards) + 1) for t in range(shards)]
-        arrived.append(lax.ppermute(anchors, ("tok", "head"), pairs))
-    swapped = [lax.ppermute(block, "head", [(0, 1), (1, 0)]) for block in arrived[:-1]]
-    swapped.append(lax.ppermute(arrived[-1], "head", [(0, 1)]))
-    queries, value_turned = pl.pallas_call(
+        *in_hbm(
+            interior_landmark_position,
+            boundary_landmark_position,
+            interior_element_embedding,
+            boundary_element_embedding,
+            vol_gain,
+            surf_gain,
+        )
+    )
+    evens = list(range(2, shards, 2))
+    order = [evens.pop(0 if turn % 2 == 0 else -1) for turn in range(len(evens))] + [shards - 1]
+    rounds = list(zip(order, [*range(1, shards - 1, 2), 0]))
+    arrived = [
+        lax.ppermute(
+            anchors,
+            ("tok", "head"),
+            [(2 * t + core, 2 * ((t + hop[core]) % shards) + core) for t in range(shards) for core in (0, 1)],
+        )
+        for hop in rounds[::-1]
+    ]
+    queries, *weights = pl.pallas_call(
         query_kernel,
         out_shape=(
             jax.ShapeDtypeStruct((heads // 2, pair_width, 2 * cells), jnp.bfloat16),
+            jax.ShapeDtypeStruct((width, local_width), jnp.bfloat16),
+            jax.ShapeDtypeStruct((local_width, width), jnp.bfloat16),
             jax.ShapeDtypeStruct((local_width, width), jnp.bfloat16),
         ),
-        in_specs=[VMEM] * 4,
-        out_specs=(VMEM, VMEM),
+        in_specs=[HBM] * 6,
+        out_specs=(VMEM,) * 4,
+        scratch_shapes=[
+            pltpu.VMEM((cells, width), jnp.bfloat16),
+            pltpu.VMEM((1, width), jnp.float32),
+            pltpu.VMEM((width, local_width), jnp.bfloat16),
+            pltpu.VMEM((width, local_width), jnp.bfloat16),
+            pltpu.SemaphoreType.DMA((6,)),
+        ],
         compiler_params=PARAMS,
         cost_estimate=pl.CostEstimate(
-            flops=2 * cells * width * local_width, bytes_accessed=4 * width * local_width, transcendentals=0
+            flops=2 * cells * width * local_width, bytes_accessed=8 * width * local_width, transcendentals=0
         ),
         name="queries",
     )(
-        interior_element_embedding,
-        vol_gain,
-        in_vmem(question_projection_matrix),
-        in_vmem(content_projection_matrix),
-    )
-    blocks = [anchors, *arrived[:-1], *swapped[:-1], arrived[-1], swapped[-1]]
+        *in_hbm(
+            interior_element_embedding,
+            vol_gain,
+            question_projection_matrix,
+            content_projection_matrix,
+            lookup_projection_matrix,
+            final_projection_matrix,
+        )
+    )
+    *arrived, queries = lax.optimization_barrier((*arrived, queries))
+    swapped = [lax.ppermute(block, "head", [(0, 1), (1, 0)]) for block in arrived]
+    blocks = [anchors, *arrived[1:], *swapped[1:], arrived[0], swapped[0]]
     terms = pl.pallas_call(
         functools.partial(attention_kernel, len(blocks)),
         out_shape=jax.ShapeDtypeStruct((cells, width), jnp.bfloat16),
@@ -312,11 +374,7 @@
         name="attention",
     )(
         channel_logit_divisor,
-        in_vmem(queries),
-        in_vmem(lookup_projection_matrix),
-        in_vmem(value_turned),
-        in_vmem(final_projection_matrix),
-        *[in_vmem(block) for block in blocks],
+        *in_vmem(queries, *weights, *blocks),
     )
     other = lax.ppermute(terms, "head", [(0, 1), (1, 0)])
     return pl.pallas_call(
@@ -326,7 +384,7 @@
         out_specs=VMEM,
         compiler_params=PARAMS,
         name="finish",
-    )(in_vmem(terms), in_vmem(other))
+    )(*in_vmem(terms, other))
 
 
 def solution(mesh):

time: 31.9 us -> 21.8 us (0.68)
  local copies, waits for them, and re-layouts: 7.06 us -> 0.65 us
  waiting for transfers between devices: 6.66 us -> 2.08 us
  Pallas kernels: 4.91 us -> 6.99 us
  starting transfers between devices: 12.7 us -> 11.8 us
    unnamed x22 -> x2, local copies, waits for them, and re-layouts: 7.06 us -> 0.65 us
    ppermute x5 -> x4, waiting for transfers between devices: 5.49 us -> 0.01 us  [direct_body(): lax.ppermute(anchors, ('tok', 'head'), [(2 * t + core, 2 * ((t + hop[core...]
    ppermute x5 -> x4, starting transfers between devices: 12.1 us -> 10.3 us  [direct_body(): lax.ppermute(anchors, ('tok', 'head'), [(2 * t + core, 2 * ((t + hop[core...]
    pallas_call x1, Pallas kernels: 0.72 us -> 2.33 us  [direct_body(): pl.pallas_call(query_kernel, out_shape=(jax.ShapeDtypeStruct((heads // 2,...]
    ppermute x3 -> x4, starting transfers between devices: 0.01 us -> 1.08 us  [direct_body(): lax.ppermute(block, 'head', [(0, 1), (1, 0)])]
    ppermute x3 -> x4, waiting for transfers between devices: 0.01 us -> 0.88 us  [direct_body(): lax.ppermute(block, 'head', [(0, 1), (1, 0)])]
    pallas_call x1, Pallas kernels: 0.79 us -> 1.26 us  [direct_body(): pl.pallas_call(anchor_kernel, out_shape=jax.ShapeDtypeStruct((picks, widt...]
  transfers between devices with their start and end apart: 9 -> 9, of which waited for: 4 -> 5; matrix products, arithmetic and copies ran while one was open for 0% -> 0% of each run, Pallas kernels for 2% -> 11%
where the time goes in v2:
time: 21.8 us; the launch traced here: 21.6 us
  starting transfers between devices  11.8 us (54%)
  Pallas kernels  6.99 us (32%)
  waiting for transfers between devices  2.08 us (10%)
  local copies, waits for them, and re-layouts  0.65 us (3%)
    ppermute x4, starting transfers between devices, direct_body(): lax.ppermute(anchors, ('tok', 'head'), [(2 * t + core, 2 * ((t + hop[core...  10.3 us
    pallas_call x1, Pallas kernels, direct_body(): pl.pallas_call(functools.partial(attention_kernel, len(blocks)), out_shap...  2.56 us
    pallas_call x1, Pallas kernels, direct_body(): pl.pallas_call(query_kernel, out_shape=(jax.ShapeDtypeStruct((heads // 2,...  2.33 us
    pallas_call x1, Pallas kernels, direct_body(): pl.pallas_call(anchor_kernel, out_shape=jax.ShapeDtypeStruct((picks, widt...  1.26 us
    ppermute x1, waiting for transfers between devices, direct_body(): other = lax.ppermute(terms, 'head', [(0, 1), (1, 0)])  1.19 us
    ppermute x4, starting transfers between devices, direct_body(): lax.ppermute(block, 'head', [(0, 1), (1, 0)])  1.08 us
    ppermute x4, waiting for transfers between devices, direct_body(): lax.ppermute(block, 'head', [(0, 1), (1, 0)])  0.88 us
    pallas_call x1, Pallas kernels, direct_body(): pl.pallas_call(finish_kernel, out_shape=jax.ShapeDtypeStruct((cells, loca...  0.83 us
  transfers between devices with their start and end apart: 9, of which 5 were waited for; matrix products, arithmetic and copies ran while one was open for 0% of the time, Pallas kernels for 11%

profile of v2, /device:TPU:0, one launch (start us, length us, event | category | flops | bytes accessed | tf_op | source)
XLA Modules:
  0.0 21.6 jit_solution(14959966264330918951)
XLA Ops:
  0.0 1.3 %anchors.1.rest_0_ = bf16[24,1024]{1,0:T(8,128)(2,1)S(1)} custom-call(s32[16]{0:T(128)} %refs_0_.2, s32[8]{0:T(128)} %refs_1_.1, bf16[128,1024]{1,0:T(8,128)(2,1)} %refs_0_.3, bf16[32,1024]{1,0:T(8,128)(2,1)} %refs_3_.2, f32[1,1024]{1,0:T(1,128)} %bitcast.2, f32[1,1024]{1,0:T(1,128)} %bitcast.4), custom_call_target="tpu_custom_call" | custom-call | tf_op jit(solution)/shard_map/anchors/pallas_call | solution.py:295
  1.3 3.1 %collective-permute-start.3 = (bf16[24,1024]{1,0:T(8,128)(2,1)S(1)}, bf16[24,1024]{1,0:T(8,128)(2,1)S(1)}, u32[]{:S(2)}, u32[]{:S(2)}) collective-permute-start(bf16[24,1024]{1,0:T(8,128)(2,1)S(1)} %anchors.1.rest_0_), channel_id=1, source_target_pairs={{0,4},{1,3},{2,6},{3,5},{4,8},{5,7},{6,10},{7,9},{8,12},{9,11},{10... | collective-permute-start | bytes 147464 | tf_op jit(solution)/shard_map/ppermute | solution.py:325
  4.3 2.1 %collective-permute-start.2 = (bf16[24,1024]{1,0:T(8,128)(2,1)S(1)}, bf16[24,1024]{1,0:T(8,128)(2,1)S(1)}, u32[]{:S(2)}, u32[]{:S(2)}) collective-permute-start(bf16[24,1024]{1,0:T(8,128)(2,1)S(1)} %anchors.1.rest_0_), channel_id=1, source_target_pairs={{0,12},{1,7},{2,14},{3,9},{4,0},{5,11},{6,2},{7,13},{8,4},{9,15},{... | collective-permute-start | bytes 147464 | tf_op jit(solution)/shard_map/ppermute | solution.py:325
  6.4 0.9 %collective-permute-start.1 = (bf16[24,1024]{1,0:T(8,128)(2,1)S(1)}, bf16[24,1024]{1,0:T(8,128)(2,1)S(1)}, u32[]{:S(2)}, u32[]{:S(2)}) collective-permute-start(bf16[24,1024]{1,0:T(8,128)(2,1)S(1)} %anchors.1.rest_0_), channel_id=1, source_target_pairs={{0,8},{1,11},{2,10},{3,13},{4,12},{5,15},{6,14},{7,1},{8,0},{9,3},... | collective-permute-start | bytes 147464 | tf_op jit(solution)/shard_map/ppermute | solution.py:325
  7.4 4.2 %collective-permute-start = (bf16[24,1024]{1,0:T(8,128)(2,1)S(1)}, bf16[24,1024]{1,0:T(8,128)(2,1)S(1)}, u32[]{:S(2)}, u32[]{:S(2)}) collective-permute-start(bf16[24,1024]{1,0:T(8,128)(2,1)S(1)} %anchors.1.rest_0_), channel_id=1, source_target_pairs={{0,14},{1,1},{2,0},{3,3},{4,2},{5,5},{6,4},{7,7},{8,6},{9,9},{10,8... | collective-permute-start | bytes 147464 | tf_op jit(solution)/shard_map/ppermute | solution.py:325
  11.6 2.3 %queries.1 = (bf16[4,128,256]{2,1,0:T(8,128)(2,1)S(1)}, bf16[1024,512]{1,0:T(8,128)(2,1)S(1)}, bf16[512,1024]{1,0:T(8,128)(2,1)S(1)}, bf16[512,1024]{1,0:T(8,128)(2,1)S(1)}) custom-call(bf16[128,1024]{1,0:T(8,128)(2,1)} %refs_0_.3, f32[1,1024]{1,0:T(1,128)} %bitcast.3, bf16[1024,512]{1,0:T(8,128)(2,1)} %refs_2_.3, bf16[1024,512]{1,0:T(8,128)(2,1)} %refs_3_.3, ...), custom_call_target="tpu_custom_call" | custom-call | flops 134217728 | bytes 4194304 | tf_op jit(solution)/shard_map/queries/pallas_call | solution.py:332
  13.9 0.0 collective-permute-done.3.rest_3_
  13.9 0.0 collective-permute-done.2.rest_2_
  13.9 0.0 collective-permute-done.1.rest_1_
  13.9 0.0 collective-permute-done.rest_7_
  13.9 0.1 collective-permute-start.4
  14.0 0.5 %collective-permute-start.5 = (bf16[24,1024]{1,0:T(8,128)(2,1)S(1)}, bf16[24,1024]{1,0:T(8,128)(2,1)S(1)}, u32[]{:S(2)}, u32[]{:S(2)}) collective-permute-start(bf16[24,1024]{1,0:T(8,128)(2,1)S(1)} %collective-permute-done.2.rest_2_), channel_id=1, source_target_pairs={{0,1},{1,0},{2,3},{3,2},{4,5},{5,4},{6,7},{7,6},{8,9},{9,8},{10,11... | collective-permute-start | bytes 147464 | tf_op jit(solution)/shard_map/ppermute | solution.py:365
  14.5 0.1 collective-permute-start.6
  14.6 0.4 %collective-permute-start.7 = (bf16[24,1024]{1,0:T(8,128)(2,1)S(1)}, bf16[24,1024]{1,0:T(8,128)(2,1)S(1)}, u32[]{:S(2)}, u32[]{:S(2)}) collective-permute-start(bf16[24,1024]{1,0:T(8,128)(2,1)S(1)} %collective-permute-done.rest_7_), channel_id=1, source_target_pairs={{0,1},{1,0},{2,3},{3,2},{4,5},{5,4},{6,7},{7,6},{8,9},{9,8},{10,11... | collective-permute-start | bytes 147464 | tf_op jit(solution)/shard_map/ppermute | solution.py:365
  15.0 0.2 collective-permute-done.4.rest_4_
  15.2 0.2 collective-permute-done.5.rest_5_
  15.4 0.3 %collective-permute-done.6.rest_6_ = bf16[24,1024]{1,0:T(8,128)(2,1)S(1)} collective-permute-done((bf16[24,1024]{1,0:T(8,128)(2,1)S(1)}, bf16[24,1024]{1,0:T(8,128)(2,1)S(1)}, u32[]{:S(2)}, u32[]{:S(2)}) %collective-permute-start.6) | collective-permute-done | bytes 49184 | tf_op jit(solution)/shard_map/ppermute | solution.py:365
  15.8 0.2 collective-permute-done.7.rest_8_
  15.9 0.0 copy-start
  15.9 0.7 %copy-done = f32[8]{0:T(128)S(1)} copy-done((f32[8]{0:T(128)S(1)}, f32[8]{0:T(128)}, u32[]{:S(2)}) %copy-start) | copy-done | bytes 56
  16.6 2.6 %attention.1.own = bf16[128,1024]{1,0:T(8,128)(2,1)S(1)} custom-call(f32[8]{0:T(128)S(1)} %copy-done, bf16[4,128,256]{2,1,0:T(8,128)(2,1)S(1)} %get-tuple-element.15.queries, bf16[1024,512]{1,0:T(8,128)(2,1)S(1)} %get-tuple-element.16.lookup, bf16[512,1024]{1,0:T(8,128)(2,1)S(1)} %get-tuple-element.17.value_turned, ...), custom_call_target="tpu_custom_call" | custom-call | tf_op jit(solution)/shard_map/attention/pallas_call | solution.py:367
  19.1 0.4 %collective-permute-start.8 = (bf16[128,1024]{1,0:T(8,128)(2,1)S(1)}, bf16[128,1024]{1,0:T(8,128)(2,1)S(1)}, u32[]{:S(2)}, u32[]{:S(2)}) collective-permute-start(bf16[128,1024]{1,0:T(8,128)(2,1)S(1)} %attention.1.own), channel_id=1, source_target_pairs={{0,1},{1,0},{2,3},{3,2},{4,5},{5,4},{6,7},{7,6},{8,9},{9,8},{10,11... | collective-permute-start | bytes 786440 | tf_op jit(solution)/shard_map/ppermute | solution.py:379
  19.6 1.2 %collective-permute-done.8.other = bf16[128,1024]{1,0:T(8,128)(2,1)S(1)} collective-permute-done((bf16[128,1024]{1,0:T(8,128)(2,1)S(1)}, bf16[128,1024]{1,0:T(8,128)(2,1)S(1)}, u32[]{:S(2)}, u32[]{:S(2)}) %collective-permute-start.8) | collective-permute-done | bytes 262176 | tf_op jit(solution)/shard_map/ppermute | solution.py:379
  20.7 0.8 %finish.1 = bf16[128,512]{1,0:T(8,128)(2,1)} custom-call(bf16[128,1024]{1,0:T(8,128)(2,1)S(1)} %attention.1.own, bf16[128,1024]{1,0:T(8,128)(2,1)S(1)} %collective-permute-done.8.other), custom_call_target="tpu_custom_call" | custom-call | tf_op jit(solution)/shard_map/finish/pallas_call | solution.py:380
Async XLA Ops:
  1.3 12.6 %collective-permute-start.3 = (bf16[24,1024]{1,0:T(8,128)(2,1)S(1)}, bf16[24,1024]{1,0:T(8,128)(2,1)S(1)}, u32[]{:S(2)}, u32[]{:S(2)}) collective-permute-start(bf16[24,1024]{1,0:T(8,128)(2,1)S(1)} %anchors.1.rest_0_), channel_id=1, source_target_pairs={{0,4},{1,3},{2,6},{3,5},{4,8},{5,7},{6,10},{7,9},{8,12},{9,11},{10... | collective-permute-start | bytes 147464 | tf_op jit(solution)/shard_map/ppermute | solution.py:325
  4.3 9.6 %collective-permute-start.2 = (bf16[24,1024]{1,0:T(8,128)(2,1)S(1)}, bf16[24,1024]{1,0:T(8,128)(2,1)S(1)}, u32[]{:S(2)}, u32[]{:S(2)}) collective-permute-start(bf16[24,1024]{1,0:T(8,128)(2,1)S(1)} %anchors.1.rest_0_), channel_id=1, source_target_pairs={{0,12},{1,7},{2,14},{3,9},{4,0},{5,11},{6,2},{7,13},{8,4},{9,15},{... | collective-permute-start | bytes 147464 | tf_op jit(solution)/shard_map/ppermute | solution.py:325
  6.4 7.5 %collective-permute-start.1 = (bf16[24,1024]{1,0:T(8,128)(2,1)S(1)}, bf16[24,1024]{1,0:T(8,128)(2,1)S(1)}, u32[]{:S(2)}, u32[]{:S(2)}) collective-permute-start(bf16[24,1024]{1,0:T(8,128)(2,1)S(1)} %anchors.1.rest_0_), channel_id=1, source_target_pairs={{0,8},{1,11},{2,10},{3,13},{4,12},{5,15},{6,14},{7,1},{8,0},{9,3},... | collective-permute-start | bytes 147464 | tf_op jit(solution)/shard_map/ppermute | solution.py:325
  7.4 6.6 %collective-permute-start = (bf16[24,1024]{1,0:T(8,128)(2,1)S(1)}, bf16[24,1024]{1,0:T(8,128)(2,1)S(1)}, u32[]{:S(2)}, u32[]{:S(2)}) collective-permute-start(bf16[24,1024]{1,0:T(8,128)(2,1)S(1)} %anchors.1.rest_0_), channel_id=1, source_target_pairs={{0,14},{1,1},{2,0},{3,3},{4,2},{5,5},{6,4},{7,7},{8,6},{9,9},{10,8... | collective-permute-start | bytes 147464 | tf_op jit(solution)/shard_map/ppermute | solution.py:325
  13.9 1.3 %collective-permute-start.4 = (bf16[24,1024]{1,0:T(8,128)(2,1)S(1)}, bf16[24,1024]{1,0:T(8,128)(2,1)S(1)}, u32[]{:S(2)}, u32[]{:S(2)}) collective-permute-start(bf16[24,1024]{1,0:T(8,128)(2,1)S(1)} %collective-permute-done.1.rest_1_), channel_id=1, source_target_pairs={{0,1},{1,0},{2,3},{3,2},{4,5},{5,4},{6,7},{7,6},{8,9},{9,8},{10,11... | collective-permute-start | bytes 147464 | tf_op jit(solution)/shard_map/ppermute | solution.py:365
  14.0 1.4 %collective-permute-start.5 = (bf16[24,1024]{1,0:T(8,128)(2,1)S(1)}, bf16[24,1024]{1,0:T(8,128)(2,1)S(1)}, u32[]{:S(2)}, u32[]{:S(2)}) collective-permute-start(bf16[24,1024]{1,0:T(8,128)(2,1)S(1)} %collective-permute-done.2.rest_2_), channel_id=1, source_target_pairs={{0,1},{1,0},{2,3},{3,2},{4,5},{5,4},{6,7},{7,6},{8,9},{9,8},{10,11... | collective-permute-start | bytes 147464 | tf_op jit(solution)/shard_map/ppermute | solution.py:365
  14.5 1.2 %collective-permute-start.6 = (bf16[24,1024]{1,0:T(8,128)(2,1)S(1)}, bf16[24,1024]{1,0:T(8,128)(2,1)S(1)}, u32[]{:S(2)}, u32[]{:S(2)}) collective-permute-start(bf16[24,1024]{1,0:T(8,128)(2,1)S(1)} %collective-permute-done.3.rest_3_), channel_id=1, source_target_pairs={{0,1},{1,0},{2,3},{3,2},{4,5},{5,4},{6,7},{7,6},{8,9},{9,8},{10,11... | collective-permute-start | bytes 147464 | tf_op jit(solution)/shard_map/ppermute | solution.py:365
  14.6 1.3 %collective-permute-start.7 = (bf16[24,1024]{1,0:T(8,128)(2,1)S(1)}, bf16[24,1024]{1,0:T(8,128)(2,1)S(1)}, u32[]{:S(2)}, u32[]{:S(2)}) collective-permute-start(bf16[24,1024]{1,0:T(8,128)(2,1)S(1)} %collective-permute-done.rest_7_), channel_id=1, source_target_pairs={{0,1},{1,0},{2,3},{3,2},{4,5},{5,4},{6,7},{7,6},{8,9},{9,8},{10,11... | collective-permute-start | bytes 147464 | tf_op jit(solution)/shard_map/ppermute | solution.py:365
  15.9 0.7 %copy-start = (f32[8]{0:T(128)S(1)}, f32[8]{0:T(128)}, u32[]{:S(2)}) copy-start(f32[8]{0:T(128)} %divisor.1) | copy-start | bytes 100
  19.1 1.6 %collective-permute-start.8 = (bf16[128,1024]{1,0:T(8,128)(2,1)S(1)}, bf16[128,1024]{1,0:T(8,128)(2,1)S(1)}, u32[]{:S(2)}, u32[]{:S(2)}) collective-permute-start(bf16[128,1024]{1,0:T(8,128)(2,1)S(1)} %attention.1.own), channel_id=1, source_target_pairs={{0,1},{1,0},{2,3},{3,2},{4,5},{5,4},{6,7},{7,6},{8,9},{9,8},{10,11... | collective-permute-start | bytes 786440 | tf_op jit(solution)/shard_map/ppermute | solution.py:379

commit v3 on v2

--- a/solution.py
+++ b/solution.py
@@ -194,11 +194,11 @@
 
 
 def query_kernel(*refs):
-    sources, (queries, lookup, value_turned, final) = refs[:6], refs[6:10]
-    (vol, gain, projection, value_projection), semaphores = refs[10:14], refs[14]
-    targets = (vol, gain, projection, value_projection, lookup, final)
+    sources, (queries, multiplier, lookup, value_turned, final) = refs[:7], refs[7:12]
+    (vol, gain, projection, divisor, value_projection), semaphores = refs[12:17], refs[17]
+    targets = (vol, gain, projection, divisor, value_projection, lookup, final)
     copies = fetch(sources, targets, semaphores)
-    for copy in copies[:3]:
+    for copy in copies[:4]:
         copy.wait()
     vol_normed = normed(vol[...].astype(jnp.float32), gain[...])
     cells = vol.shape[0]
@@ -207,39 +207,37 @@
     ).astype(jnp.bfloat16)
     pairs, pair_width, _ = queries.shape
     half = pair_width // 2
+    left = lax.broadcasted_iota(jnp.int32, (1, 2 * cells), 1) < cells
+    scale = 1.0 / math.sqrt(half)
+    for pair in range(pairs):
+        multiplier[pair : pair + 1, :] = jnp.where(
+            left, divisor[2 * pair] * scale, divisor[2 * pair + 1] * scale
+        )
     upper = lax.broadcasted_iota(jnp.int32, (pair_width, cells), 0) < half
     for pair in range(pairs):
         block = columns[pair * pair_width : (pair + 1) * pair_width, :].astype(jnp.float32)
         queries[pair, :, :cells] = jnp.where(upper, block, 0.0).astype(jnp.bfloat16)
         queries[pair, :, cells:] = jnp.where(upper, 0.0, block).astype(jnp.bfloat16)
-    copies[3].wait()
+    copies[4].wait()
     value_turned[...] = value_projection[...].T
-    for copy in copies[4:]:
+    for copy in copies[5:]:
         copy.wait()
 
 
-def attention_kernel(block_count, divisor, queries, lookup, value_turned, final, *rest):
+def attention_kernel(block_count, queries, multiplier, lookup, value_turned, final, *rest):
     blocks, terms, context = rest[:block_count], rest[block_count], rest[block_count + 1]
     pairs, pair_width, wide = queries.shape
     half, cells = pair_width // 2, wide // 2
-    rows = [block[...].astype(jnp.float32) for block in blocks[:-2]]
-    first_core = lax.axis_index("head") == 0
-    rows.append(
-        jnp.where(
-            first_core, blocks[-2][...].astype(jnp.float32), blocks[-1][...].astype(jnp.float32)
-        )
-    )
+    rows = [block[...].astype(jnp.float32) for block in blocks]
     anchors = jnp.concatenate(rows, axis=0).astype(jnp.bfloat16)
     keys = jnp.dot(anchors, lookup[...], preferred_element_type=jnp.float32).astype(jnp.bfloat16)
     values = lax.dot_general(
         value_turned[...], anchors, (((1,), (1,)), ((), ())), preferred_element_type=jnp.float32
     ).astype(jnp.bfloat16)
-    left = lax.broadcasted_iota(jnp.int32, (1, wide), 1) < cells
-    scale = 1.0 / math.sqrt(half)
     for pair in range(pairs):
         span = slice(pair * pair_width, (pair + 1) * pair_width)
-        multiplier = jnp.where(left, divisor[2 * pair] * scale, divisor[2 * pair + 1] * scale)
-        scores = jnp.dot(keys[:, span], queries[pair], preferred_element_type=jnp.float32) * multiplier
+        scores = jnp.dot(keys[:, span], queries[pair], preferred_element_type=jnp.float32)
+        scores = scores * multiplier[pair : pair + 1, :]
         exp_scores = jnp.exp(scores - jnp.max(scores, axis=0, keepdims=True))
         denominator = jnp.sum(exp_scores, axis=0, keepdims=True)
         added = jnp.dot(
@@ -265,7 +263,6 @@
             update[...] = (mixed[:, part * width : (part + 1) * width] * factor).astype(update.dtype)
 
 
-SMEM = pl.BlockSpec(memory_space=pltpu.SMEM)
 VMEM = pl.BlockSpec(memory_space=pltpu.VMEM)
 HBM = pl.BlockSpec(memory_space=pltpu.HBM)
 PARAMS = pltpu.CompilerParams(vmem_limit_bytes=32 * 1024 * 1024)
@@ -318,9 +315,7 @@
             surf_gain,
         )
     )
-    evens = list(range(2, shards, 2))
-    order = [evens.pop(0 if turn % 2 == 0 else -1) for turn in range(len(evens))] + [shards - 1]
-    rounds = list(zip(order, [*range(1, shards - 1, 2), 0]))
+    rounds = [(hop + 1, hop) for hop in range(1, shards - 1, 2)] + [(shards - 1, shards - 1)]
     arrived = [
         lax.ppermute(
             anchors,
@@ -333,18 +328,20 @@
         query_kernel,
         out_shape=(
             jax.ShapeDtypeStruct((heads // 2, pair_width, 2 * cells), jnp.bfloat16),
+            jax.ShapeDtypeStruct((heads // 2, 2 * cells), jnp.float32),
             jax.ShapeDtypeStruct((width, local_width), jnp.bfloat16),
             jax.ShapeDtypeStruct((local_width, width), jnp.bfloat16),
             jax.ShapeDtypeStruct((local_width, width), jnp.bfloat16),
         ),
-        in_specs=[HBM] * 6,
-        out_specs=(VMEM,) * 4,
+        in_specs=[HBM] * 7,
+        out_specs=(VMEM,) * 5,
         scratch_shapes=[
             pltpu.VMEM((cells, width), jnp.bfloat16),
             pltpu.VMEM((1, width), jnp.float32),
             pltpu.VMEM((width, local_width), jnp.bfloat16),
+            pltpu.SMEM((heads,), jnp.float32),
             pltpu.VMEM((width, local_width), jnp.bfloat16),
-            pltpu.SemaphoreType.DMA((6,)),
+            pltpu.SemaphoreType.DMA((7,)),
         ],
         compiler_params=PARAMS,
         cost_estimate=pl.CostEstimate(
@@ -356,24 +353,23 @@
             interior_element_embedding,
             vol_gain,
             question_projection_matrix,
+            channel_logit_divisor,
             content_projection_matrix,
             lookup_projection_matrix,
             final_projection_matrix,
         )
     )
-    *arrived, queries = lax.optimization_barrier((*arrived, queries))
-    swapped = [lax.ppermute(block, "head", [(0, 1), (1, 0)]) for block in arrived]
-    blocks = [anchors, *arrived[1:], *swapped[1:], arrived[0], swapped[0]]
+    swapped = [lax.ppermute(block, "head", [(0, 1), (1, 0)]) for block in arrived[1:]]
+    blocks = [anchors, *arrived, *swapped]
     terms = pl.pallas_call(
         functools.partial(attention_kernel, len(blocks)),
         out_shape=jax.ShapeDtypeStruct((cells, width), jnp.bfloat16),
-        in_specs=[SMEM] + [VMEM] * (4 + len(blocks)),
+        in_specs=[VMEM] * (5 + len(blocks)),
         out_specs=VMEM,
         scratch_shapes=[pltpu.VMEM((local_width, cells), jnp.bfloat16)],
         compiler_params=PARAMS,
         name="attention",
     )(
-        channel_logit_divisor,
         *in_vmem(queries, *weights, *blocks),
     )
     other = lax.ppermute(terms, "head", [(0, 1), (1, 0)])

time: 21.8 us -> 18.7 us (0.86)
  starting transfers between devices: 11.8 us -> 8.97 us
  waiting for transfers between devices: 2.08 us -> 3.06 us
  local copies, waits for them, and re-layouts: 0.65 us -> 0 us
  Pallas kernels: 6.99 us -> 6.46 us
    ppermute x4, starting transfers between devices: 10.3 us -> 8.39 us  [direct_body(): lax.ppermute(anchors, ('tok', 'head'), [(2 * t + core, 2 * ((t + hop[core...]
    ppermute x4, waiting for transfers between devices: 0.01 us -> 1.89 us  [direct_body(): lax.ppermute(anchors, ('tok', 'head'), [(2 * t + core, 2 * ((t + hop[core...]
    ppermute x4 -> x3, starting transfers between devices: 1.08 us -> 0.01 us  [direct_body(): lax.ppermute(block, 'head', [(0, 1), (1, 0)])]
    ppermute x4 -> x3, waiting for transfers between devices: 0.88 us -> 0.01 us  [direct_body(): lax.ppermute(block, 'head', [(0, 1), (1, 0)])]
    unnamed x2 -> x0, local copies, waits for them, and re-layouts: 0.65 us -> none
    pallas_call x1, Pallas kernels: 2.56 us -> 2.03 us  [direct_body(): pl.pallas_call(functools.partial(attention_kernel, len(blocks)), out_shap...]
  transfers between devices with their start and end apart: 9 -> 8, of which waited for: 5 -> 3; matrix products, arithmetic and copies ran while one was open for 0% -> 0% of each run, Pallas kernels for 11% -> 13%
where the time goes in v3:
time: 18.7 us; the launch traced here: 18.6 us
  starting transfers between devices  8.97 us (48%)
  Pallas kernels  6.46 us (35%)
  waiting for transfers between devices  3.06 us (16%)
    ppermute x4, starting transfers between devices, direct_body(): lax.ppermute(anchors, ('tok', 'head'), [(2 * t + core, 2 * ((t + hop[core...  8.39 us
    pallas_call x1, Pallas kernels, direct_body(): pl.pallas_call(query_kernel, out_shape=(jax.ShapeDtypeStruct((heads // 2,...  2.34 us
    pallas_call x1, Pallas kernels, direct_body(): pl.pallas_call(functools.partial(attention_kernel, len(blocks)), out_shap...  2.03 us
    ppermute x4, waiting for transfers between devices, direct_body(): lax.ppermute(anchors, ('tok', 'head'), [(2 * t + core, 2 * ((t + hop[core...  1.89 us
    pallas_call x1, Pallas kernels, direct_body(): pl.pallas_call(anchor_kernel, out_shape=jax.ShapeDtypeStruct((picks, widt...  1.26 us
    ppermute x1, waiting for transfers between devices, direct_body(): other = lax.ppermute(terms, 'head', [(0, 1), (1, 0)])  1.16 us
    pallas_call x1, Pallas kernels, direct_body(): pl.pallas_call(finish_kernel, out_shape=jax.ShapeDtypeStruct((cells, loca...  0.83 us
    ppermute x1, starting transfers between devices, direct_body(): other = lax.ppermute(terms, 'head', [(0, 1), (1, 0)])  0.57 us
  transfers between devices with their start and end apart: 8, of which 3 were waited for; matrix products, arithmetic and copies ran while one was open for 0% of the time, Pallas kernels for 13%

profile of v3, /device:TPU:0, one launch (start us, length us, event | category | flops | bytes accessed | tf_op | source)
XLA Modules:
  0.0 18.6 jit_solution(10717452879319601742)
XLA Ops:
  0.0 1.3 %anchors.1.rest_0_ = bf16[24,1024]{1,0:T(8,128)(2,1)S(1)} custom-call(s32[16]{0:T(128)} %refs_0_.3, s32[8]{0:T(128)} %refs_1_.1, bf16[128,1024]{1,0:T(8,128)(2,1)} %refs_2_.3, bf16[32,1024]{1,0:T(8,128)(2,1)} %refs_3_.3, f32[1,1024]{1,0:T(1,128)} %bitcast.2, f32[1,1024]{1,0:T(1,128)} %bitcast.4), custom_call_target="tpu_custom_call" | custom-call | tf_op jit(solution)/shard_map/anchors/pallas_call | solution.py:292
  1.3 3.1 %collective-permute-start.3 = (bf16[24,1024]{1,0:T(8,128)(2,1)S(1)}, bf16[24,1024]{1,0:T(8,128)(2,1)S(1)}, u32[]{:S(2)}, u32[]{:S(2)}) collective-permute-start(bf16[24,1024]{1,0:T(8,128)(2,1)S(1)} %anchors.1.rest_0_), channel_id=1, source_target_pairs={{0,4},{1,3},{2,6},{3,5},{4,8},{5,7},{6,10},{7,9},{8,12},{9,11},{10... | collective-permute-start | bytes 147464 | tf_op jit(solution)/shard_map/ppermute | solution.py:320
  4.3 2.6 %collective-permute-start.2 = (bf16[24,1024]{1,0:T(8,128)(2,1)S(1)}, bf16[24,1024]{1,0:T(8,128)(2,1)S(1)}, u32[]{:S(2)}, u32[]{:S(2)}) collective-permute-start(bf16[24,1024]{1,0:T(8,128)(2,1)S(1)} %anchors.1.rest_0_), channel_id=1, source_target_pairs={{0,8},{1,7},{2,10},{3,9},{4,12},{5,11},{6,14},{7,13},{8,0},{9,15},... | collective-permute-start | bytes 147464 | tf_op jit(solution)/shard_map/ppermute | solution.py:320
  6.9 1.3 %collective-permute-start.1 = (bf16[24,1024]{1,0:T(8,128)(2,1)S(1)}, bf16[24,1024]{1,0:T(8,128)(2,1)S(1)}, u32[]{:S(2)}, u32[]{:S(2)}) collective-permute-start(bf16[24,1024]{1,0:T(8,128)(2,1)S(1)} %anchors.1.rest_0_), channel_id=1, source_target_pairs={{0,12},{1,11},{2,14},{3,13},{4,0},{5,15},{6,2},{7,1},{8,4},{9,3},{... | collective-permute-start | bytes 147464 | tf_op jit(solution)/shard_map/ppermute | solution.py:320
  8.3 1.4 %collective-permute-start = (bf16[24,1024]{1,0:T(8,128)(2,1)S(1)}, bf16[24,1024]{1,0:T(8,128)(2,1)S(1)}, u32[]{:S(2)}, u32[]{:S(2)}) collective-permute-start(bf16[24,1024]{1,0:T(8,128)(2,1)S(1)} %anchors.1.rest_0_), channel_id=1, source_target_pairs={{0,14},{1,15},{2,0},{3,1},{4,2},{5,3},{6,4},{7,5},{8,6},{9,7},{10,... | collective-permute-start | bytes 147464 | tf_op jit(solution)/shard_map/ppermute | solution.py:320
  9.7 0.0 collective-permute-done.3.rest_4_
  9.7 0.0 collective-permute-start.6
  9.7 0.7 %collective-permute-done.2.rest_3_ = bf16[24,1024]{1,0:T(8,128)(2,1)S(1)} collective-permute-done((bf16[24,1024]{1,0:T(8,128)(2,1)S(1)}, bf16[24,1024]{1,0:T(8,128)(2,1)S(1)}, u32[]{:S(2)}, u32[]{:S(2)}) %collective-permute-start.2) | collective-permute-done | bytes 49184 | tf_op jit(solution)/shard_map/ppermute | solution.py:320
  10.4 0.0 collective-permute-start.5
  10.4 1.2 %collective-permute-done.1.rest_2_ = bf16[24,1024]{1,0:T(8,128)(2,1)S(1)} collective-permute-done((bf16[24,1024]{1,0:T(8,128)(2,1)S(1)}, bf16[24,1024]{1,0:T(8,128)(2,1)S(1)}, u32[]{:S(2)}, u32[]{:S(2)}) %collective-permute-start.1) | collective-permute-done | bytes 49184 | tf_op jit(solution)/shard_map/ppermute | solution.py:320
  11.6 0.0 collective-permute-start.4
  11.6 2.3 %queries.1 = (bf16[4,128,256]{2,1,0:T(8,128)(2,1)S(1)}, f32[4,256]{1,0:T(4,128)S(1)}, bf16[1024,512]{1,0:T(8,128)(2,1)S(1)}, bf16[512,1024]{1,0:T(8,128)(2,1)S(1)}, bf16[512,1024]{1,0:T(8,128)(2,1)S(1)}) custom-call(bf16[128,1024]{1,0:T(8,128)(2,1)} %refs_2_.3, f32[1,1024]{1,0:T(1,128)} %bitcast.3, bf16[1024,512]{1,0:T(8,128)(2,1)} %refs_2_.2, f32[8]{0:T(128)} %refs_3_.2, ...), custom_call_target="tpu_custom_call" | custom-call | flops 134217728 | bytes 4194304 | tf_op jit(solution)/shard_map/queries/pallas_call | solution.py:327
  13.9 0.0 collective-permute-done.rest_1_
  13.9 0.0 collective-permute-done.6.rest_7_
  13.9 0.0 collective-permute-done.5.rest_6_
  13.9 0.0 collective-permute-done.4.rest_5_
  13.9 2.0 %attention.1.own = bf16[128,1024]{1,0:T(8,128)(2,1)S(1)} custom-call(bf16[4,128,256]{2,1,0:T(8,128)(2,1)S(1)} %get-tuple-element.10.queries, f32[4,256]{1,0:T(4,128)S(1)} %get-tuple-element.11.multiplier, bf16[1024,512]{1,0:T(8,128)(2,1)S(1)} %get-tuple-element.12.lookup, bf16[512,1024]{1,0:T(8,128)(2,1)S(1)} %get-tuple-element.13.value_turned, ...), custom_call_target="tpu_custom_call" | custom-call | tf_op jit(solution)/shard_map/attention/pallas_call | solution.py:364
  16.0 0.6 %collective-permute-start.7 = (bf16[128,1024]{1,0:T(8,128)(2,1)S(1)}, bf16[128,1024]{1,0:T(8,128)(2,1)S(1)}, u32[]{:S(2)}, u32[]{:S(2)}) collective-permute-start(bf16[128,1024]{1,0:T(8,128)(2,1)S(1)} %attention.1.own), channel_id=1, source_target_pairs={{0,1},{1,0},{2,3},{3,2},{4,5},{5,4},{6,7},{7,6},{8,9},{9,8},{10,11... | collective-permute-start | bytes 786440 | tf_op jit(solution)/shard_map/ppermute | solution.py:375
  16.6 1.2 %collective-permute-done.7.other = bf16[128,1024]{1,0:T(8,128)(2,1)S(1)} collective-permute-done((bf16[128,1024]{1,0:T(8,128)(2,1)S(1)}, bf16[128,1024]{1,0:T(8,128)(2,1)S(1)}, u32[]{:S(2)}, u32[]{:S(2)}) %collective-permute-start.7) | collective-permute-done | bytes 262176 | tf_op jit(solution)/shard_map/ppermute | solution.py:375
  17.7 0.8 %finish.1 = bf16[128,512]{1,0:T(8,128)(2,1)} custom-call(bf16[128,1024]{1,0:T(8,128)(2,1)S(1)} %attention.1.own, bf16[128,1024]{1,0:T(8,128)(2,1)S(1)} %collective-permute-done.7.other), custom_call_target="tpu_custom_call" | custom-call | tf_op jit(solution)/shard_map/finish/pallas_call | solution.py:376
Async XLA Ops:
  1.3 8.4 %collective-permute-start.3 = (bf16[24,1024]{1,0:T(8,128)(2,1)S(1)}, bf16[24,1024]{1,0:T(8,128)(2,1)S(1)}, u32[]{:S(2)}, u32[]{:S(2)}) collective-permute-start(bf16[24,1024]{1,0:T(8,128)(2,1)S(1)} %anchors.1.rest_0_), channel_id=1, source_target_pairs={{0,4},{1,3},{2,6},{3,5},{4,8},{5,7},{6,10},{7,9},{8,12},{9,11},{10... | collective-permute-start | bytes 147464 | tf_op jit(solution)/shard_map/ppermute | solution.py:320
  4.3 6.0 %collective-permute-start.2 = (bf16[24,1024]{1,0:T(8,128)(2,1)S(1)}, bf16[24,1024]{1,0:T(8,128)(2,1)S(1)}, u32[]{:S(2)}, u32[]{:S(2)}) collective-permute-start(bf16[24,1024]{1,0:T(8,128)(2,1)S(1)} %anchors.1.rest_0_), channel_id=1, source_target_pairs={{0,8},{1,7},{2,10},{3,9},{4,12},{5,11},{6,14},{7,13},{8,0},{9,15},... | collective-permute-start | bytes 147464 | tf_op jit(solution)/shard_map/ppermute | solution.py:320
  6.9 4.6 %collective-permute-start.1 = (bf16[24,1024]{1,0:T(8,128)(2,1)S(1)}, bf16[24,1024]{1,0:T(8,128)(2,1)S(1)}, u32[]{:S(2)}, u32[]{:S(2)}) collective-permute-start(bf16[24,1024]{1,0:T(8,128)(2,1)S(1)} %anchors.1.rest_0_), channel_id=1, source_target_pairs={{0,12},{1,11},{2,14},{3,13},{4,0},{5,15},{6,2},{7,1},{8,4},{9,3},{... | collective-permute-start | bytes 147464 | tf_op jit(solution)/shard_map/ppermute | solution.py:320
  8.3 5.6 %collective-permute-start = (bf16[24,1024]{1,0:T(8,128)(2,1)S(1)}, bf16[24,1024]{1,0:T(8,128)(2,1)S(1)}, u32[]{:S(2)}, u32[]{:S(2)}) collective-permute-start(bf16[24,1024]{1,0:T(8,128)(2,1)S(1)} %anchors.1.rest_0_), channel_id=1, source_target_pairs={{0,14},{1,15},{2,0},{3,1},{4,2},{5,3},{6,4},{7,5},{8,6},{9,7},{10,... | collective-permute-start | bytes 147464 | tf_op jit(solution)/shard_map/ppermute | solution.py:320
  9.7 4.3 %collective-permute-start.6 = (bf16[24,1024]{1,0:T(8,128)(2,1)S(1)}, bf16[24,1024]{1,0:T(8,128)(2,1)S(1)}, u32[]{:S(2)}, u32[]{:S(2)}) collective-permute-start(bf16[24,1024]{1,0:T(8,128)(2,1)S(1)} %collective-permute-done.3.rest_4_), channel_id=1, source_target_pairs={{0,1},{1,0},{2,3},{3,2},{4,5},{5,4},{6,7},{7,6},{8,9},{9,8},{10,11... | collective-permute-start | bytes 147464 | tf_op jit(solution)/shard_map/ppermute | solution.py:362
  10.4 3.5 %collective-permute-start.5 = (bf16[24,1024]{1,0:T(8,128)(2,1)S(1)}, bf16[24,1024]{1,0:T(8,128)(2,1)S(1)}, u32[]{:S(2)}, u32[]{:S(2)}) collective-permute-start(bf16[24,1024]{1,0:T(8,128)(2,1)S(1)} %collective-permute-done.2.rest_3_), channel_id=1, source_target_pairs={{0,1},{1,0},{2,3},{3,2},{4,5},{5,4},{6,7},{7,6},{8,9},{9,8},{10,11... | collective-permute-start | bytes 147464 | tf_op jit(solution)/shard_map/ppermute | solution.py:362
  11.6 2.4 %collective-permute-start.4 = (bf16[24,1024]{1,0:T(8,128)(2,1)S(1)}, bf16[24,1024]{1,0:T(8,128)(2,1)S(1)}, u32[]{:S(2)}, u32[]{:S(2)}) collective-permute-start(bf16[24,1024]{1,0:T(8,128)(2,1)S(1)} %collective-permute-done.1.rest_2_), channel_id=1, source_target_pairs={{0,1},{1,0},{2,3},{3,2},{4,5},{5,4},{6,7},{7,6},{8,9},{9,8},{10,11... | collective-permute-start | bytes 147464 | tf_op jit(solution)/shard_map/ppermute | solution.py:362
  16.0 1.7 %collective-permute-start.7 = (bf16[128,1024]{1,0:T(8,128)(2,1)S(1)}, bf16[128,1024]{1,0:T(8,128)(2,1)S(1)}, u32[]{:S(2)}, u32[]{:S(2)}) collective-permute-start(bf16[128,1024]{1,0:T(8,128)(2,1)S(1)} %attention.1.own), channel_id=1, source_target_pairs={{0,1},{1,0},{2,3},{3,2},{4,5},{5,4},{6,7},{7,6},{8,9},{9,8},{10,11... | collective-permute-start | bytes 786440 | tf_op jit(solution)/shard_map/ppermute | solution.py:375

commit v4 on v3

--- a/solution.py
+++ b/solution.py
@@ -181,8 +181,9 @@
 
 
 def anchor_kernel(*refs):
-    sources, anchors, targets, semaphores = refs[:6], refs[6], refs[7:13], refs[13]
-    vol_position, surf_position, vol, surf, vol_gain, surf_gain = targets
+    sources, (anchors, vol, vol_gain, multiplier), rest = refs[:7], refs[7:11], refs[11:]
+    vol_position, surf_position, surf, surf_gain, divisor, semaphores = rest
+    targets = (vol_position, surf_position, vol, surf, vol_gain, surf_gain, divisor)
     for copy in fetch(sources, targets, semaphores):
         copy.wait()
     block_index = lax.axis_index("tok")
@@ -191,37 +192,25 @@
     parts = [normed(vol_rows, vol_gain[...]), normed(surf_rows, surf_gain[...])]
     stacked = jnp.concatenate([part.astype(jnp.float32) for part in parts], axis=0)
     anchors[...] = stacked.astype(jnp.bfloat16)
-
-
-def query_kernel(*refs):
-    sources, (queries, multiplier, lookup, value_turned, final) = refs[:7], refs[7:12]
-    (vol, gain, projection, divisor, value_projection), semaphores = refs[12:17], refs[17]
-    targets = (vol, gain, projection, divisor, value_projection, lookup, final)
-    copies = fetch(sources, targets, semaphores)
-    for copy in copies[:4]:
-        copy.wait()
+    pairs, wide = multiplier.shape
+    left = lax.broadcasted_iota(jnp.int32, (1, wide), 1) < wide // 2
+    for pair in range(pairs):
+        multiplier[pair : pair + 1, :] = jnp.where(left, divisor[2 * pair], divisor[2 * pair + 1])
+
+
+def query_kernel(vol, gain, projection, value_projection, lookup, final, queries, value_turned):
     vol_normed = normed(vol[...].astype(jnp.float32), gain[...])
     cells = vol.shape[0]
     columns = lax.dot_general(
         projection[...], vol_normed, (((0,), (1,)), ((), ())), preferred_element_type=jnp.float32
     ).astype(jnp.bfloat16)
     pairs, pair_width, _ = queries.shape
-    half = pair_width // 2
-    left = lax.broadcasted_iota(jnp.int32, (1, 2 * cells), 1) < cells
-    scale = 1.0 / math.sqrt(half)
-    for pair in range(pairs):
-        multiplier[pair : pair + 1, :] = jnp.where(
-            left, divisor[2 * pair] * scale, divisor[2 * pair + 1] * scale
-        )
-    upper = lax.broadcasted_iota(jnp.int32, (pair_width, cells), 0) < half
+    upper = lax.broadcasted_iota(jnp.int32, (pair_width, cells), 0) < pair_width // 2
     for pair in range(pairs):
         block = columns[pair * pair_width : (pair + 1) * pair_width, :].astype(jnp.float32)
         queries[pair, :, :cells] = jnp.where(upper, block, 0.0).astype(jnp.bfloat16)
         queries[pair, :, cells:] = jnp.where(upper, 0.0, block).astype(jnp.bfloat16)
-    copies[4].wait()
     value_turned[...] = value_projection[...].T
-    for copy in copies[5:]:
-        copy.wait()
 
 
 def attention_kernel(block_count, queries, multiplier, lookup, value_turned, final, *rest):
@@ -234,10 +223,11 @@
     values = lax.dot_general(
         value_turned[...], anchors, (((1,), (1,)), ((), ())), preferred_element_type=jnp.float32
     ).astype(jnp.bfloat16)
+    scale = 1.0 / math.sqrt(half)
     for pair in range(pairs):
         span = slice(pair * pair_width, (pair + 1) * pair_width)
         scores = jnp.dot(keys[:, span], queries[pair], preferred_element_type=jnp.float32)
-        scores = scores * multiplier[pair : pair + 1, :]
+        scores = scores * (multiplier[pair : pair + 1, :] * scale)
         exp_scores = jnp.exp(scores - jnp.max(scores, axis=0, keepdims=True))
         denominator = jnp.sum(exp_scores, axis=0, keepdims=True)
         added = jnp.dot(
@@ -287,23 +277,26 @@
     heads = channel_logit_divisor.shape[0]
     pair_width = 2 * (local_width // heads)
     picks = interior_landmark_position.shape[0] + boundary_landmark_position.shape[0]
-    vol_gain = interior_rescaling_factor.reshape(1, width)
-    surf_gain = boundary_rescaling_factor.reshape(1, width)
-    anchors = pl.pallas_call(
+    anchors, vol, vol_gain, multiplier = pl.pallas_call(
         anchor_kernel,
-        out_shape=jax.ShapeDtypeStruct((picks, width), jnp.bfloat16),
-        in_specs=[HBM] * 6,
-        out_specs=VMEM,
+        out_shape=(
+            jax.ShapeDtypeStruct((picks, width), jnp.bfloat16),
+            jax.ShapeDtypeStruct((cells, width), jnp.bfloat16),
+            jax.ShapeDtypeStruct((1, width), jnp.float32),
+            jax.ShapeDtypeStruct((heads // 2, 2 * cells), jnp.float32),
+        ),
+        in_specs=[HBM] * 7,
+        out_specs=(VMEM,) * 4,
         scratch_shapes=[
             pltpu.SMEM(interior_landmark_position.shape, jnp.int32),
             pltpu.SMEM(boundary_landmark_position.shape, jnp.int32),
-            pltpu.VMEM(interior_element_embedding.shape, jnp.bfloat16),
             pltpu.VMEM(boundary_element_embedding.shape, jnp.bfloat16),
             pltpu.VMEM((1, width), jnp.float32),
-            pltpu.VMEM((1, width), jnp.float32),
-            pltpu.SemaphoreType.DMA((6,)),
+            pltpu.SMEM((heads,), jnp.float32),
+            pltpu.SemaphoreType.DMA((7,)),
         ],
         compiler_params=PARAMS,
+        cost_estimate=pl.CostEstimate(flops=2*10**10, bytes_accessed=2**20, transcendentals=0),
         name="anchors",
     )(
         *in_hbm(
@@ -311,8 +304,9 @@
             boundary_landmark_position,
             interior_element_embedding,
             boundary_element_embedding,
-            vol_gain,
-            surf_gain,
+            interior_rescaling_factor.reshape(1, width),
+            boundary_rescaling_factor.reshape(1, width),
+            channel_logit_divisor,
         )
     )
     rounds = [(hop + 1, hop) for hop in range(1, shards - 1, 2)] + [(shards - 1, shards - 1)]
@@ -322,43 +316,22 @@
             ("tok", "head"),
             [(2 * t + core, 2 * ((t + hop[core]) % shards) + core) for t in range(shards) for core in (0, 1)],
         )
-        for hop in rounds[::-1]
+        for hop in rounds[-1:] + rounds[:-1]
     ]
-    queries, *weights = pl.pallas_call(
+    queries, value_turned = pl.pallas_call(
         query_kernel,
         out_shape=(
             jax.ShapeDtypeStruct((heads // 2, pair_width, 2 * cells), jnp.bfloat16),
-            jax.ShapeDtypeStruct((heads // 2, 2 * cells), jnp.float32),
-            jax.ShapeDtypeStruct((width, local_width), jnp.bfloat16),
-            jax.ShapeDtypeStruct((local_width, width), jnp.bfloat16),
             jax.ShapeDtypeStruct((local_width, width), jnp.bfloat16),
         ),
-        in_specs=[HBM] * 7,
-        out_specs=(VMEM,) * 5,
-        scratch_shapes=[
-            pltpu.VMEM((cells, width), jnp.bfloat16),
-            pltpu.VMEM((1, width), jnp.float32),
-            pltpu.VMEM((width, local_width), jnp.bfloat16),
-            pltpu.SMEM((heads,), jnp.float32),
-            pltpu.VMEM((width, local_width), jnp.bfloat16),
-            pltpu.SemaphoreType.DMA((7,)),
-        ],
+        in_specs=[VMEM] * 6,
+        out_specs=(VMEM, VMEM),
         compiler_params=PARAMS,
         cost_estimate=pl.CostEstimate(
             flops=2 * cells * width * local_width, bytes_accessed=8 * width * local_width, transcendentals=0
         ),
         name="queries",
-    )(
-        *in_hbm(
-            interior_element_embedding,
-            vol_gain,
-            question_projection_matrix,
-            channel_logit_divisor,
-            content_projection_matrix,
-            lookup_projection_matrix,
-            final_projection_matrix,
-        )
-    )
+    )(*in_vmem(vol, vol_gain, question_projection_matrix, content_projection_matrix, lookup_projection_matrix, final_projection_matrix))
     swapped = [lax.ppermute(block, "head", [(0, 1), (1, 0)]) for block in arrived[1:]]
     blocks = [anchors, *arrived, *swapped]
     terms = pl.pallas_call(
@@ -370,7 +343,7 @@
         compiler_params=PARAMS,
         name="attention",
     )(
-        *in_vmem(queries, *weights, *blocks),
+        *in_vmem(queries, multiplier, lookup_projection_matrix, value_turned, final_projection_matrix, *blocks),
     )
     other = lax.ppermute(terms, "head", [(0, 1), (1, 0)])
     return pl.pallas_call(

time: 18.7 us -> 17.6 us (0.941)
  Pallas kernels: 6.46 us -> 5.02 us
  waiting for transfers between devices: 3.06 us -> 3.73 us
  starting transfers between devices: 8.97 us -> 8.63 us
    pallas_call x1, Pallas kernels: 2.34 us -> 0.72 us  [direct_body(): pl.pallas_call(query_kernel, out_shape=(jax.ShapeDtypeStruct((heads // 2,...]
    ppermute x3, waiting for transfers between devices: 0.01 us -> 0.41 us  [direct_body(): lax.ppermute(block, 'head', [(0, 1), (1, 0)])]
    ppermute x1, starting transfers between devices: 0.57 us -> 0.22 us  [direct_body(): other = lax.ppermute(terms, 'head', [(0, 1), (1, 0)])]
    ppermute x1, waiting for transfers between devices: 1.16 us -> 1.38 us  [direct_body(): other = lax.ppermute(terms, 'head', [(0, 1), (1, 0)])]
  transfers between devices with their start and end apart: 8 -> 8, of which waited for: 3 -> 5; matrix products, arithmetic and copies ran while one was open for 0% -> 0% of each run, Pallas kernels for 13% -> 4%
where the time goes in v4:
time: 17.6 us; the launch traced here: 17.5 us
  starting transfers between devices  8.63 us (49%)
  Pallas kernels  5.02 us (29%)
  waiting for transfers between devices  3.73 us (21%)
    ppermute x4, starting transfers between devices, direct_body(): lax.ppermute(anchors, ('tok', 'head'), [(2 * t + core, 2 * ((t + hop[core...  8.4 us
    pallas_call x1, Pallas kernels, direct_body(): pl.pallas_call(functools.partial(attention_kernel, len(blocks)), out_shap...  2.04 us
    ppermute x4, waiting for transfers between devices, direct_body(): lax.ppermute(anchors, ('tok', 'head'), [(2 * t + core, 2 * ((t + hop[core...  1.95 us
    pallas_call x1, Pallas kernels, direct_body(): pl.pallas_call(anchor_kernel, out_shape=(jax.ShapeDtypeStruct((picks, wid...  1.43 us
    ppermute x1, waiting for transfers between devices, direct_body(): other = lax.ppermute(terms, 'head', [(0, 1), (1, 0)])  1.38 us
    pallas_call x1, Pallas kernels, direct_body(): pl.pallas_call(finish_kernel, out_shape=jax.ShapeDtypeStruct((cells, loca...  0.83 us
    pallas_call x1, Pallas kernels, direct_body(): pl.pallas_call(query_kernel, out_shape=(jax.ShapeDtypeStruct((heads // 2,...  0.72 us
    ppermute x3, waiting for transfers between devices, direct_body(): lax.ppermute(block, 'head', [(0, 1), (1, 0)])  0.41 us
  transfers between devices with their start and end apart: 8, of which 5 were waited for; matrix products, arithmetic and copies ran while one was open for 0% of the time, Pallas kernels for 4%

profile of v4, /device:TPU:0, one launch (start us, length us, event | category | flops | bytes accessed | tf_op | source)
XLA Modules:
  0.0 17.5 jit_solution(13803445248378600436)
XLA Ops:
  0.0 1.4 %anchors.1 = (bf16[24,1024]{1,0:T(8,128)(2,1)S(1)}, bf16[128,1024]{1,0:T(8,128)(2,1)S(1)}, f32[1,1024]{1,0:T(1,128)S(1)}, f32[4,256]{1,0:T(4,128)S(1)}) custom-call(s32[16]{0:T(128)} %refs_0_.1, s32[8]{0:T(128)} %refs_1_.1, bf16[128,1024]{1,0:T(8,128)(2,1)} %refs_2_.1, bf16[32,1024]{1,0:T(8,128)(2,1)} %refs_3_.1, f32[1,1024]{1,0:T(1,128)} %bitcast.2, ...), custom_call_target="tpu_custom_call" | custom-call | flops 20000000000 | bytes 1048576 | tf_op jit(solution)/shard_map/anchors/pallas_call | solution.py:280
  1.4 3.1 %collective-permute-start.1 = (bf16[24,1024]{1,0:T(8,128)(2,1)S(1)}, bf16[24,1024]{1,0:T(8,128)(2,1)S(1)}, u32[]{:S(2)}, u32[]{:S(2)}) collective-permute-start(bf16[24,1024]{1,0:T(8,128)(2,1)S(1)} %get-tuple-element.16.rest_0_), channel_id=1, source_target_pairs={{0,4},{1,3},{2,6},{3,5},{4,8},{5,7},{6,10},{7,9},{8,12},{9,11},{10... | collective-permute-start | bytes 147464 | tf_op jit(solution)/shard_map/ppermute | solution.py:314
  4.5 2.6 %collective-permute-start.2 = (bf16[24,1024]{1,0:T(8,128)(2,1)S(1)}, bf16[24,1024]{1,0:T(8,128)(2,1)S(1)}, u32[]{:S(2)}, u32[]{:S(2)}) collective-permute-start(bf16[24,1024]{1,0:T(8,128)(2,1)S(1)} %get-tuple-element.16.rest_0_), channel_id=1, source_target_pairs={{0,8},{1,7},{2,10},{3,9},{4,12},{5,11},{6,14},{7,13},{8,0},{9,15},... | collective-permute-start | bytes 147464 | tf_op jit(solution)/shard_map/ppermute | solution.py:314
  7.1 1.3 %collective-permute-start.3 = (bf16[24,1024]{1,0:T(8,128)(2,1)S(1)}, bf16[24,1024]{1,0:T(8,128)(2,1)S(1)}, u32[]{:S(2)}, u32[]{:S(2)}) collective-permute-start(bf16[24,1024]{1,0:T(8,128)(2,1)S(1)} %get-tuple-element.16.rest_0_), channel_id=1, source_target_pairs={{0,12},{1,11},{2,14},{3,13},{4,0},{5,15},{6,2},{7,1},{8,4},{9,3},{... | collective-permute-start | bytes 147464 | tf_op jit(solution)/shard_map/ppermute | solution.py:314
  8.5 1.4 %collective-permute-start = (bf16[24,1024]{1,0:T(8,128)(2,1)S(1)}, bf16[24,1024]{1,0:T(8,128)(2,1)S(1)}, u32[]{:S(2)}, u32[]{:S(2)}) collective-permute-start(bf16[24,1024]{1,0:T(8,128)(2,1)S(1)} %get-tuple-element.16.rest_0_), channel_id=1, source_target_pairs={{0,14},{1,15},{2,0},{3,1},{4,2},{5,3},{6,4},{7,5},{8,6},{9,7},{10,... | collective-permute-start | bytes 147464 | tf_op jit(solution)/shard_map/ppermute | solution.py:314
  9.9 0.0 collective-permute-done.1.rest_2_
  9.9 0.0 collective-permute-start.4
  9.9 0.7 %collective-permute-done.2.rest_3_ = bf16[24,1024]{1,0:T(8,128)(2,1)S(1)} collective-permute-done((bf16[24,1024]{1,0:T(8,128)(2,1)S(1)}, bf16[24,1024]{1,0:T(8,128)(2,1)S(1)}, u32[]{:S(2)}, u32[]{:S(2)}) %collective-permute-start.2) | collective-permute-done | bytes 49184 | tf_op jit(solution)/shard_map/ppermute | solution.py:314
  10.6 0.0 collective-permute-start.5
  10.6 1.2 %collective-permute-done.3.rest_4_ = bf16[24,1024]{1,0:T(8,128)(2,1)S(1)} collective-permute-done((bf16[24,1024]{1,0:T(8,128)(2,1)S(1)}, bf16[24,1024]{1,0:T(8,128)(2,1)S(1)}, u32[]{:S(2)}, u32[]{:S(2)}) %collective-permute-start.3) | collective-permute-done | bytes 49184 | tf_op jit(solution)/shard_map/ppermute | solution.py:314
  11.7 0.0 collective-permute-start.6
  11.7 0.0 copy-done
  11.7 0.0 copy-done.1
  11.8 0.0 copy-done.2
  11.8 0.0 copy-done.3
  11.8 0.7 %queries.1 = (bf16[4,128,256]{2,1,0:T(8,128)(2,1)S(1)}, bf16[512,1024]{1,0:T(8,128)(2,1)S(1)}) custom-call(bf16[128,1024]{1,0:T(8,128)(2,1)S(1)} %get-tuple-element.11.vol, f32[1,1024]{1,0:T(1,128)S(1)} %get-tuple-element.12.gain, bf16[1024,512]{1,0:T(8,128)(2,1)S(1)} %copy-done.2, bf16[1024,512]{1,0:T(8,128)(2,1)S(1)} %copy-done.3, ...), custom_call_target="tpu_custom_call" | custom-call | flops 134217728 | bytes 4194304 | tf_op jit(solution)/shard_map/queries/pallas_call | solution.py:321
  12.5 0.1 collective-permute-done.rest_1_
  12.6 0.0 collective-permute-done.4.rest_5_
  12.6 0.0 collective-permute-done.5.rest_6_
  12.6 0.4 %collective-permute-done.6.rest_7_ = bf16[24,1024]{1,0:T(8,128)(2,1)S(1)} collective-permute-done((bf16[24,1024]{1,0:T(8,128)(2,1)S(1)}, bf16[24,1024]{1,0:T(8,128)(2,1)S(1)}, u32[]{:S(2)}, u32[]{:S(2)}) %collective-permute-start.6) | collective-permute-done | bytes 49184 | tf_op jit(solution)/shard_map/ppermute | solution.py:335
  13.0 2.0 %attention.1.own = bf16[128,1024]{1,0:T(8,128)(2,1)S(1)} custom-call(bf16[4,128,256]{2,1,0:T(8,128)(2,1)S(1)} %get-tuple-element.13.queries, f32[4,256]{1,0:T(4,128)S(1)} %get-tuple-element.14.multiplier, bf16[1024,512]{1,0:T(8,128)(2,1)S(1)} %copy-done, bf16[512,1024]{1,0:T(8,128)(2,1)S(1)} %get-tuple-element.15.value_turned, ...), custom_call_target="tpu_custom_call" | custom-call | tf_op jit(solution)/shard_map/attention/pallas_call | solution.py:337
  15.0 0.2 %collective-permute-start.7 = (bf16[128,1024]{1,0:T(8,128)(2,1)S(1)}, bf16[128,1024]{1,0:T(8,128)(2,1)S(1)}, u32[]{:S(2)}, u32[]{:S(2)}) collective-permute-start(bf16[128,1024]{1,0:T(8,128)(2,1)S(1)} %attention.1.own), channel_id=1, source_target_pairs={{0,1},{1,0},{2,3},{3,2},{4,5},{5,4},{6,7},{7,6},{8,9},{9,8},{10,11... | collective-permute-start | bytes 786440 | tf_op jit(solution)/shard_map/ppermute | solution.py:348
  15.2 1.4 %collective-permute-done.7.other = bf16[128,1024]{1,0:T(8,128)(2,1)S(1)} collective-permute-done((bf16[128,1024]{1,0:T(8,128)(2,1)S(1)}, bf16[128,1024]{1,0:T(8,128)(2,1)S(1)}, u32[]{:S(2)}, u32[]{:S(2)}) %collective-permute-start.7) | collective-permute-done | bytes 262176 | tf_op jit(solution)/shard_map/ppermute | solution.py:348
  16.6 0.8 %finish.1 = bf16[128,512]{1,0:T(8,128)(2,1)} custom-call(bf16[128,1024]{1,0:T(8,128)(2,1)S(1)} %attention.1.own, bf16[128,1024]{1,0:T(8,128)(2,1)S(1)} %collective-permute-done.7.other), custom_call_target="tpu_custom_call" | custom-call | tf_op jit(solution)/shard_map/finish/pallas_call | solution.py:349
  (4 shorter events, 0.0 us)
Async XLA Ops:
  0.0 11.7 %copy-start = (bf16[1024,512]{1,0:T(8,128)(2,1)S(1)}, bf16[1024,512]{1,0:T(8,128)(2,1)}, u32[]{:S(2)}) copy-start(bf16[1024,512]{1,0:T(8,128)(2,1)} %lookup.3) | copy-start | bytes 3145732
  0.0 11.7 %copy-start.1 = (bf16[512,1024]{1,0:T(8,128)(2,1)S(1)}, bf16[512,1024]{1,0:T(8,128)(2,1)}, u32[]{:S(2)}) copy-start(bf16[512,1024]{1,0:T(8,128)(2,1)} %final.3) | copy-start | bytes 3145732
  0.0 11.8 %copy-start.2 = (bf16[1024,512]{1,0:T(8,128)(2,1)S(1)}, bf16[1024,512]{1,0:T(8,128)(2,1)}, u32[]{:S(2)}) copy-start(bf16[1024,512]{1,0:T(8,128)(2,1)} %projection.1) | copy-start | bytes 3145732
  0.0 11.8 %copy-start.3 = (bf16[1024,512]{1,0:T(8,128)(2,1)S(1)}, bf16[1024,512]{1,0:T(8,128)(2,1)}, u32[]{:S(2)}) copy-start(bf16[1024,512]{1,0:T(8,128)(2,1)} %value_projection.1) | copy-start | bytes 3145732
  1.4 8.4 %collective-permute-start.1 = (bf16[24,1024]{1,0:T(8,128)(2,1)S(1)}, bf16[24,1024]{1,0:T(8,128)(2,1)S(1)}, u32[]{:S(2)}, u32[]{:S(2)}) collective-permute-start(bf16[24,1024]{1,0:T(8,128)(2,1)S(1)} %get-tuple-element.16.rest_0_), channel_id=1, source_target_pairs={{0,4},{1,3},{2,6},{3,5},{4,8},{5,7},{6,10},{7,9},{8,12},{9,11},{10... | collective-permute-start | bytes 147464 | tf_op jit(solution)/shard_map/ppermute | solution.py:314
  4.5 6.0 %collective-permute-start.2 = (bf16[24,1024]{1,0:T(8,128)(2,1)S(1)}, bf16[24,1024]{1,0:T(8,128)(2,1)S(1)}, u32[]{:S(2)}, u32[]{:S(2)}) collective-permute-start(bf16[24,1024]{1,0:T(8,128)(2,1)S(1)} %get-tuple-element.16.rest_0_), channel_id=1, source_target_pairs={{0,8},{1,7},{2,10},{3,9},{4,12},{5,11},{6,14},{7,13},{8,0},{9,15},... | collective-permute-start | bytes 147464 | tf_op jit(solution)/shard_map/ppermute | solution.py:314
  7.1 4.6 %collective-permute-start.3 = (bf16[24,1024]{1,0:T(8,128)(2,1)S(1)}, bf16[24,1024]{1,0:T(8,128)(2,1)S(1)}, u32[]{:S(2)}, u32[]{:S(2)}) collective-permute-start(bf16[24,1024]{1,0:T(8,128)(2,1)S(1)} %get-tuple-element.16.rest_0_), channel_id=1, source_target_pairs={{0,12},{1,11},{2,14},{3,13},{4,0},{5,15},{6,2},{7,1},{8,4},{9,3},{... | collective-permute-start | bytes 147464 | tf_op jit(solution)/shard_map/ppermute | solution.py:314
  8.5 4.1 %collective-permute-start = (bf16[24,1024]{1,0:T(8,128)(2,1)S(1)}, bf16[24,1024]{1,0:T(8,128)(2,1)S(1)}, u32[]{:S(2)}, u32[]{:S(2)}) collective-permute-start(bf16[24,1024]{1,0:T(8,128)(2,1)S(1)} %get-tuple-element.16.rest_0_), channel_id=1, source_target_pairs={{0,14},{1,15},{2,0},{3,1},{4,2},{5,3},{6,4},{7,5},{8,6},{9,7},{10,... | collective-permute-start | bytes 147464 | tf_op jit(solution)/shard_map/ppermute | solution.py:314
  9.9 2.7 %collective-permute-start.4 = (bf16[24,1024]{1,0:T(8,128)(2,1)S(1)}, bf16[24,1024]{1,0:T(8,128)(2,1)S(1)}, u32[]{:S(2)}, u32[]{:S(2)}) collective-permute-start(bf16[24,1024]{1,0:T(8,128)(2,1)S(1)} %collective-permute-done.1.rest_2_), channel_id=1, source_target_pairs={{0,1},{1,0},{2,3},{3,2},{4,5},{5,4},{6,7},{7,6},{8,9},{9,8},{10,11... | collective-permute-start | bytes 147464 | tf_op jit(solution)/shard_map/ppermute | solution.py:335
  10.6 2.0 %collective-permute-start.5 = (bf16[24,1024]{1,0:T(8,128)(2,1)S(1)}, bf16[24,1024]{1,0:T(8,128)(2,1)S(1)}, u32[]{:S(2)}, u32[]{:S(2)}) collective-permute-start(bf16[24,1024]{1,0:T(8,128)(2,1)S(1)} %collective-permute-done.2.rest_3_), channel_id=1, source_target_pairs={{0,1},{1,0},{2,3},{3,2},{4,5},{5,4},{6,7},{7,6},{8,9},{9,8},{10,11... | collective-permute-start | bytes 147464 | tf_op jit(solution)/shard_map/ppermute | solution.py:335
  11.7 1.2 %collective-permute-start.6 = (bf16[24,1024]{1,0:T(8,128)(2,1)S(1)}, bf16[24,1024]{1,0:T(8,128)(2,1)S(1)}, u32[]{:S(2)}, u32[]{:S(2)}) collective-permute-start(bf16[24,1024]{1,0:T(8,128)(2,1)S(1)} %collective-permute-done.3.rest_4_), channel_id=1, source_target_pairs={{0,1},{1,0},{2,3},{3,2},{4,5},{5,4},{6,7},{7,6},{8,9},{9,8},{10,11... | collective-permute-start | bytes 147464 | tf_op jit(solution)/shard_map/ppermute | solution.py:335
  15.0 1.6 %collective-permute-start.7 = (bf16[128,1024]{1,0:T(8,128)(2,1)S(1)}, bf16[128,1024]{1,0:T(8,128)(2,1)S(1)}, u32[]{:S(2)}, u32[]{:S(2)}) collective-permute-start(bf16[128,1024]{1,0:T(8,128)(2,1)S(1)} %attention.1.own), channel_id=1, source_target_pairs={{0,1},{1,0},{2,3},{3,2},{4,5},{5,4},{6,7},{7,6},{8,9},{9,8},{10,11... | collective-permute-start | bytes 786440 | tf_op jit(solution)/shard_map/ppermute | solution.py:348

commit v5 on v4

--- a/solution.py
+++ b/solution.py
@@ -214,31 +214,37 @@
 
 
 def attention_kernel(block_count, queries, multiplier, lookup, value_turned, final, *rest):
-    blocks, terms, context = rest[:block_count], rest[block_count], rest[block_count + 1]
+    blocks, terms = rest[:block_count], rest[block_count]
     pairs, pair_width, wide = queries.shape
     half, cells = pair_width // 2, wide // 2
     rows = [block[...].astype(jnp.float32) for block in blocks]
     anchors = jnp.concatenate(rows, axis=0).astype(jnp.bfloat16)
-    keys = jnp.dot(anchors, lookup[...], preferred_element_type=jnp.float32).astype(jnp.bfloat16)
     values = lax.dot_general(
         value_turned[...], anchors, (((1,), (1,)), ((), ())), preferred_element_type=jnp.float32
     ).astype(jnp.bfloat16)
+    keys = jnp.dot(anchors, lookup[...], preferred_element_type=jnp.float32).astype(jnp.bfloat16)
     scale = 1.0 / math.sqrt(half)
-    for pair in range(pairs):
-        span = slice(pair * pair_width, (pair + 1) * pair_width)
-        scores = jnp.dot(keys[:, span], queries[pair], preferred_element_type=jnp.float32)
-        scores = scores * (multiplier[pair : pair + 1, :] * scale)
-        exp_scores = jnp.exp(scores - jnp.max(scores, axis=0, keepdims=True))
-        denominator = jnp.sum(exp_scores, axis=0, keepdims=True)
-        added = jnp.dot(
-            values[span, :], exp_scores.astype(jnp.bfloat16), preferred_element_type=jnp.float32
-        )
-        added = added / denominator
-        context[span, :] = jnp.concatenate(
-            [added[:half, :cells], added[half:, cells:]], axis=0
-        ).astype(jnp.bfloat16)
+    spans = [slice(pair * pair_width, (pair + 1) * pair_width) for pair in range(pairs)]
+    scores = [
+        jnp.dot(keys[:, span], queries[pair], preferred_element_type=jnp.float32)
+        for pair, span in enumerate(spans)
+    ]
+    scores = [score * (multiplier[pair : pair + 1, :] * scale) for pair, score in enumerate(scores)]
+    exp_scores = [jnp.exp(score - jnp.max(score, axis=0, keepdims=True)) for score in scores]
+    denominators = [jnp.sum(exp_score, axis=0, keepdims=True) for exp_score in exp_scores]
+    added = [
+        jnp.dot(values[span, :], exp_score.astype(jnp.bfloat16), preferred_element_type=jnp.float32)
+        for span, exp_score in zip(spans, exp_scores)
+    ]
+    context = []
+    for pair_added, denominator in zip(added, denominators):
+        context.append(pair_added[:half, :cells] / denominator[:, :cells])
+        context.append(pair_added[half:, cells:] / denominator[:, cells:])
     terms[...] = lax.dot_general(
-        context[...], final[...], (((0,), (0,)), ((), ())), preferred_element_type=jnp.float32
+        jnp.concatenate(context, axis=0).astype(jnp.bfloat16),
+        final[...],
+        (((0,), (0,)), ((), ())),
+        preferred_element_type=jnp.float32,
     ).astype(jnp.bfloat16)
 
 
@@ -339,7 +345,6 @@
         out_shape=jax.ShapeDtypeStruct((cells, width), jnp.bfloat16),
         in_specs=[VMEM] * (5 + len(blocks)),
         out_specs=VMEM,
-        scratch_shapes=[pltpu.VMEM((local_width, cells), jnp.bfloat16)],
         compiler_params=PARAMS,
         name="attention",
     )(

time: 17.6 us -> 16.9 us (0.960)
  Pallas kernels: 5.02 us -> 4.29 us
    pallas_call x1, Pallas kernels: 2.04 us -> 1.3 us  [direct_body(): pl.pallas_call(functools.partial(attention_kernel, len(blocks)), out_shap...]
where the time goes in v5:
time: 16.9 us; the launch traced here: 16.7 us
  starting transfers between devices  8.64 us (51%)
  Pallas kernels  4.29 us (25%)
  waiting for transfers between devices  3.73 us (22%)
    ppermute x4, starting transfers between devices, direct_body(): lax.ppermute(anchors, ('tok', 'head'), [(2 * t + core, 2 * ((t + hop[core...  8.4 us
    ppermute x4, waiting for transfers between devices, direct_body(): lax.ppermute(anchors, ('tok', 'head'), [(2 * t + core, 2 * ((t + hop[core...  1.95 us
    pallas_call x1, Pallas kernels, direct_body(): pl.pallas_call(anchor_kernel, out_shape=(jax.ShapeDtypeStruct((picks, wid...  1.43 us
    ppermute x1, waiting for transfers between devices, direct_body(): other = lax.ppermute(terms, 'head', [(0, 1), (1, 0)])  1.38 us
    pallas_call x1, Pallas kernels, direct_body(): pl.pallas_call(functools.partial(attention_kernel, len(blocks)), out_shap...  1.3 us
    pallas_call x1, Pallas kernels, direct_body(): pl.pallas_call(finish_kernel, out_shape=jax.ShapeDtypeStruct((cells, loca...  0.83 us
    pallas_call x1, Pallas kernels, direct_body(): pl.pallas_call(query_kernel, out_shape=(jax.ShapeDtypeStruct((heads // 2,...  0.72 us
    ppermute x3, waiting for transfers between devices, direct_body(): lax.ppermute(block, 'head', [(0, 1), (1, 0)])  0.41 us
  transfers between devices with their start and end apart: 8, of which 5 were waited for; matrix products, arithmetic and copies ran while one was open for 0% of the time, Pallas kernels for 4%

profile of v5, /device:TPU:0, one launch (start us, length us, event | category | flops | bytes accessed | tf_op | source)
XLA Modules:
  0.0 16.7 jit_solution(2560010659052177488)
XLA Ops:
  0.0 1.4 %anchors.1 = (bf16[24,1024]{1,0:T(8,128)(2,1)S(1)}, bf16[128,1024]{1,0:T(8,128)(2,1)S(1)}, f32[1,1024]{1,0:T(1,128)S(1)}, f32[4,256]{1,0:T(4,128)S(1)}) custom-call(s32[16]{0:T(128)} %refs_0_.1, s32[8]{0:T(128)} %refs_1_.1, bf16[128,1024]{1,0:T(8,128)(2,1)} %refs_2_.1, bf16[32,1024]{1,0:T(8,128)(2,1)} %refs_3_.1, f32[1,1024]{1,0:T(1,128)} %bitcast.2, ...), custom_call_target="tpu_custom_call" | custom-call | flops 20000000000 | bytes 1048576 | tf_op jit(solution)/shard_map/anchors/pallas_call | solution.py:286
  1.4 3.1 %collective-permute-start.1 = (bf16[24,1024]{1,0:T(8,128)(2,1)S(1)}, bf16[24,1024]{1,0:T(8,128)(2,1)S(1)}, u32[]{:S(2)}, u32[]{:S(2)}) collective-permute-start(bf16[24,1024]{1,0:T(8,128)(2,1)S(1)} %get-tuple-element.16.rest_0_), channel_id=1, source_target_pairs={{0,4},{1,3},{2,6},{3,5},{4,8},{5,7},{6,10},{7,9},{8,12},{9,11},{10... | collective-permute-start | bytes 147464 | tf_op jit(solution)/shard_map/ppermute | solution.py:320
  4.5 2.6 %collective-permute-start.2 = (bf16[24,1024]{1,0:T(8,128)(2,1)S(1)}, bf16[24,1024]{1,0:T(8,128)(2,1)S(1)}, u32[]{:S(2)}, u32[]{:S(2)}) collective-permute-start(bf16[24,1024]{1,0:T(8,128)(2,1)S(1)} %get-tuple-element.16.rest_0_), channel_id=1, source_target_pairs={{0,8},{1,7},{2,10},{3,9},{4,12},{5,11},{6,14},{7,13},{8,0},{9,15},... | collective-permute-start | bytes 147464 | tf_op jit(solution)/shard_map/ppermute | solution.py:320
  7.1 1.3 %collective-permute-start.3 = (bf16[24,1024]{1,0:T(8,128)(2,1)S(1)}, bf16[24,1024]{1,0:T(8,128)(2,1)S(1)}, u32[]{:S(2)}, u32[]{:S(2)}) collective-permute-start(bf16[24,1024]{1,0:T(8,128)(2,1)S(1)} %get-tuple-element.16.rest_0_), channel_id=1, source_target_pairs={{0,12},{1,11},{2,14},{3,13},{4,0},{5,15},{6,2},{7,1},{8,4},{9,3},{... | collective-permute-start | bytes 147464 | tf_op jit(solution)/shard_map/ppermute | solution.py:320
  8.5 1.4 %collective-permute-start = (bf16[24,1024]{1,0:T(8,128)(2,1)S(1)}, bf16[24,1024]{1,0:T(8,128)(2,1)S(1)}, u32[]{:S(2)}, u32[]{:S(2)}) collective-permute-start(bf16[24,1024]{1,0:T(8,128)(2,1)S(1)} %get-tuple-element.16.rest_0_), channel_id=1, source_target_pairs={{0,14},{1,15},{2,0},{3,1},{4,2},{5,3},{6,4},{7,5},{8,6},{9,7},{10,... | collective-permute-start | bytes 147464 | tf_op jit(solution)/shard_map/ppermute | solution.py:320
  9.9 0.0 collective-permute-done.1.rest_2_
  9.9 0.0 collective-permute-start.4
  9.9 0.7 %collective-permute-done.2.rest_3_ = bf16[24,1024]{1,0:T(8,128)(2,1)S(1)} collective-permute-done((bf16[24,1024]{1,0:T(8,128)(2,1)S(1)}, bf16[24,1024]{1,0:T(8,128)(2,1)S(1)}, u32[]{:S(2)}, u32[]{:S(2)}) %collective-permute-start.2) | collective-permute-done | bytes 49184 | tf_op jit(solution)/shard_map/ppermute | solution.py:320
  10.6 0.0 collective-permute-start.5
  10.6 1.2 %collective-permute-done.3.rest_4_ = bf16[24,1024]{1,0:T(8,128)(2,1)S(1)} collective-permute-done((bf16[24,1024]{1,0:T(8,128)(2,1)S(1)}, bf16[24,1024]{1,0:T(8,128)(2,1)S(1)}, u32[]{:S(2)}, u32[]{:S(2)}) %collective-permute-start.3) | collective-permute-done | bytes 49184 | tf_op jit(solution)/shard_map/ppermute | solution.py:320
  11.7 0.0 collective-permute-start.6
  11.7 0.0 copy-done
  11.7 0.0 copy-done.1
  11.8 0.0 copy-done.2
  11.8 0.0 copy-done.3
  11.8 0.7 %queries.1 = (bf16[4,128,256]{2,1,0:T(8,128)(2,1)S(1)}, bf16[512,1024]{1,0:T(8,128)(2,1)S(1)}) custom-call(bf16[128,1024]{1,0:T(8,128)(2,1)S(1)} %get-tuple-element.11.vol, f32[1,1024]{1,0:T(1,128)S(1)} %get-tuple-element.12.gain, bf16[1024,512]{1,0:T(8,128)(2,1)S(1)} %copy-done.2, bf16[1024,512]{1,0:T(8,128)(2,1)S(1)} %copy-done.3, ...), custom_call_target="tpu_custom_call" | custom-call | flops 134217728 | bytes 4194304 | tf_op jit(solution)/shard_map/queries/pallas_call | solution.py:327
  12.5 0.1 collective-permute-done.rest_1_
  12.6 0.0 collective-permute-done.4.rest_5_
  12.6 0.0 collective-permute-done.5.rest_6_
  12.6 0.4 %collective-permute-done.6.rest_7_ = bf16[24,1024]{1,0:T(8,128)(2,1)S(1)} collective-permute-done((bf16[24,1024]{1,0:T(8,128)(2,1)S(1)}, bf16[24,1024]{1,0:T(8,128)(2,1)S(1)}, u32[]{:S(2)}, u32[]{:S(2)}) %collective-permute-start.6) | collective-permute-done | bytes 49184 | tf_op jit(solution)/shard_map/ppermute | solution.py:341
  13.0 1.3 %attention.1.own = bf16[128,1024]{1,0:T(8,128)(2,1)S(1)} custom-call(bf16[4,128,256]{2,1,0:T(8,128)(2,1)S(1)} %get-tuple-element.13.queries, f32[4,256]{1,0:T(4,128)S(1)} %get-tuple-element.14.multiplier, bf16[1024,512]{1,0:T(8,128)(2,1)S(1)} %copy-done, bf16[512,1024]{1,0:T(8,128)(2,1)S(1)} %get-tuple-element.15.value_turned, ...), custom_call_target="tpu_custom_call" | custom-call | tf_op jit(solution)/shard_map/attention/pallas_call | solution.py:343
  14.3 0.2 %collective-permute-start.7 = (bf16[128,1024]{1,0:T(8,128)(2,1)S(1)}, bf16[128,1024]{1,0:T(8,128)(2,1)S(1)}, u32[]{:S(2)}, u32[]{:S(2)}) collective-permute-start(bf16[128,1024]{1,0:T(8,128)(2,1)S(1)} %attention.1.own), channel_id=1, source_target_pairs={{0,1},{1,0},{2,3},{3,2},{4,5},{5,4},{6,7},{7,6},{8,9},{9,8},{10,11... | collective-permute-start | bytes 786440 | tf_op jit(solution)/shard_map/ppermute | solution.py:353
  14.5 1.4 %collective-permute-done.7.other = bf16[128,1024]{1,0:T(8,128)(2,1)S(1)} collective-permute-done((bf16[128,1024]{1,0:T(8,128)(2,1)S(1)}, bf16[128,1024]{1,0:T(8,128)(2,1)S(1)}, u32[]{:S(2)}, u32[]{:S(2)}) %collective-permute-start.7) | collective-permute-done | bytes 262176 | tf_op jit(solution)/shard_map/ppermute | solution.py:353
  15.9 0.8 %finish.1 = bf16[128,512]{1,0:T(8,128)(2,1)} custom-call(bf16[128,1024]{1,0:T(8,128)(2,1)S(1)} %attention.1.own, bf16[128,1024]{1,0:T(8,128)(2,1)S(1)} %collective-permute-done.7.other), custom_call_target="tpu_custom_call" | custom-call | tf_op jit(solution)/shard_map/finish/pallas_call | solution.py:354
  (4 shorter events, 0.0 us)
Async XLA Ops:
  0.0 11.7 %copy-start = (bf16[1024,512]{1,0:T(8,128)(2,1)S(1)}, bf16[1024,512]{1,0:T(8,128)(2,1)}, u32[]{:S(2)}) copy-start(bf16[1024,512]{1,0:T(8,128)(2,1)} %lookup.3) | copy-start | bytes 3145732
  0.0 11.7 %copy-start.1 = (bf16[512,1024]{1,0:T(8,128)(2,1)S(1)}, bf16[512,1024]{1,0:T(8,128)(2,1)}, u32[]{:S(2)}) copy-start(bf16[512,1024]{1,0:T(8,128)(2,1)} %final.3) | copy-start | bytes 3145732
  0.0 11.8 %copy-start.2 = (bf16[1024,512]{1,0:T(8,128)(2,1)S(1)}, bf16[1024,512]{1,0:T(8,128)(2,1)}, u32[]{:S(2)}) copy-start(bf16[1024,512]{1,0:T(8,128)(2,1)} %projection.1) | copy-start | bytes 3145732
  0.0 11.8 %copy-start.3 = (bf16[1024,512]{1,0:T(8,128)(2,1)S(1)}, bf16[1024,512]{1,0:T(8,128)(2,1)}, u32[]{:S(2)}) copy-start(bf16[1024,512]{1,0:T(8,128)(2,1)} %value_projection.1) | copy-start | bytes 3145732
  1.4 8.4 %collective-permute-start.1 = (bf16[24,1024]{1,0:T(8,128)(2,1)S(1)}, bf16[24,1024]{1,0:T(8,128)(2,1)S(1)}, u32[]{:S(2)}, u32[]{:S(2)}) collective-permute-start(bf16[24,1024]{1,0:T(8,128)(2,1)S(1)} %get-tuple-element.16.rest_0_), channel_id=1, source_target_pairs={{0,4},{1,3},{2,6},{3,5},{4,8},{5,7},{6,10},{7,9},{8,12},{9,11},{10... | collective-permute-start | bytes 147464 | tf_op jit(solution)/shard_map/ppermute | solution.py:320
  4.5 6.0 %collective-permute-start.2 = (bf16[24,1024]{1,0:T(8,128)(2,1)S(1)}, bf16[24,1024]{1,0:T(8,128)(2,1)S(1)}, u32[]{:S(2)}, u32[]{:S(2)}) collective-permute-start(bf16[24,1024]{1,0:T(8,128)(2,1)S(1)} %get-tuple-element.16.rest_0_), channel_id=1, source_target_pairs={{0,8},{1,7},{2,10},{3,9},{4,12},{5,11},{6,14},{7,13},{8,0},{9,15},... | collective-permute-start | bytes 147464 | tf_op jit(solution)/shard_map/ppermute | solution.py:320
  7.1 4.6 %collective-permute-start.3 = (bf16[24,1024]{1,0:T(8,128)(2,1)S(1)}, bf16[24,1024]{1,0:T(8,128)(2,1)S(1)}, u32[]{:S(2)}, u32[]{:S(2)}) collective-permute-start(bf16[24,1024]{1,0:T(8,128)(2,1)S(1)} %get-tuple-element.16.rest_0_), channel_id=1, source_target_pairs={{0,12},{1,11},{2,14},{3,13},{4,0},{5,15},{6,2},{7,1},{8,4},{9,3},{... | collective-permute-start | bytes 147464 | tf_op jit(solution)/shard_map/ppermute | solution.py:320
  8.5 4.1 %collective-permute-start = (bf16[24,1024]{1,0:T(8,128)(2,1)S(1)}, bf16[24,1024]{1,0:T(8,128)(2,1)S(1)}, u32[]{:S(2)}, u32[]{:S(2)}) collective-permute-start(bf16[24,1024]{1,0:T(8,128)(2,1)S(1)} %get-tuple-element.16.rest_0_), channel_id=1, source_target_pairs={{0,14},{1,15},{2,0},{3,1},{4,2},{5,3},{6,4},{7,5},{8,6},{9,7},{10,... | collective-permute-start | bytes 147464 | tf_op jit(solution)/shard_map/ppermute | solution.py:320
  9.9 2.7 %collective-permute-start.4 = (bf16[24,1024]{1,0:T(8,128)(2,1)S(1)}, bf16[24,1024]{1,0:T(8,128)(2,1)S(1)}, u32[]{:S(2)}, u32[]{:S(2)}) collective-permute-start(bf16[24,1024]{1,0:T(8,128)(2,1)S(1)} %collective-permute-done.1.rest_2_), channel_id=1, source_target_pairs={{0,1},{1,0},{2,3},{3,2},{4,5},{5,4},{6,7},{7,6},{8,9},{9,8},{10,11... | collective-permute-start | bytes 147464 | tf_op jit(solution)/shard_map/ppermute | solution.py:341
  10.6 2.0 %collective-permute-start.5 = (bf16[24,1024]{1,0:T(8,128)(2,1)S(1)}, bf16[24,1024]{1,0:T(8,128)(2,1)S(1)}, u32[]{:S(2)}, u32[]{:S(2)}) collective-permute-start(bf16[24,1024]{1,0:T(8,128)(2,1)S(1)} %collective-permute-done.2.rest_3_), channel_id=1, source_target_pairs={{0,1},{1,0},{2,3},{3,2},{4,5},{5,4},{6,7},{7,6},{8,9},{9,8},{10,11... | collective-permute-start | bytes 147464 | tf_op jit(solution)/shard_map/ppermute | solution.py:341
  11.7 1.2 %collective-permute-start.6 = (bf16[24,1024]{1,0:T(8,128)(2,1)S(1)}, bf16[24,1024]{1,0:T(8,128)(2,1)S(1)}, u32[]{:S(2)}, u32[]{:S(2)}) collective-permute-start(bf16[24,1024]{1,0:T(8,128)(2,1)S(1)} %collective-permute-done.3.rest_4_), channel_id=1, source_target_pairs={{0,1},{1,0},{2,3},{3,2},{4,5},{5,4},{6,7},{7,6},{8,9},{9,8},{10,11... | collective-permute-start | bytes 147464 | tf_op jit(solution)/shard_map/ppermute | solution.py:341
  14.3 1.6 %collective-permute-start.7 = (bf16[128,1024]{1,0:T(8,128)(2,1)S(1)}, bf16[128,1024]{1,0:T(8,128)(2,1)S(1)}, u32[]{:S(2)}, u32[]{:S(2)}) collective-permute-start(bf16[128,1024]{1,0:T(8,128)(2,1)S(1)} %attention.1.own), channel_id=1, source_target_pairs={{0,1},{1,0},{2,3},{3,2},{4,5},{5,4},{6,7},{7,6},{8,9},{9,8},{10,11... | collective-permute-start | bytes 786440 | tf_op jit(solution)/shard_map/ppermute | solution.py:353

commit v6 on v5

--- a/solution.py
+++ b/solution.py
@@ -262,6 +262,23 @@
 VMEM = pl.BlockSpec(memory_space=pltpu.VMEM)
 HBM = pl.BlockSpec(memory_space=pltpu.HBM)
 PARAMS = pltpu.CompilerParams(vmem_limit_bytes=32 * 1024 * 1024)
+
+
+SEARCHED_ROUNDS = [
+    ((4, 2, 5, 6, 1, 7, 0, 3), (2, 6, 4, 7, 3, 0, 1, 5)),
+    ((1, 7, 3, 5, 0, 2, 4, 6), (5, 4, 7, 1, 6, 3, 2, 0)),
+    ((7, 5, 6, 0, 2, 1, 3, 4), (6, 3, 0, 2, 5, 4, 7, 1)),
+    ((3, 0, 1, 4, 7, 6, 5, 2), (3, 0, 1, 4, 7, 6, 5, 2)),
+]
+
+
+def permute_rounds(shards):
+    if shards == len(SEARCHED_ROUNDS[0][0]):
+        return SEARCHED_ROUNDS
+    hops = [(hop + 1, hop) for hop in range(1, shards - 1, 2)] + [(shards - 1, shards - 1)]
+    return [
+        tuple(tuple((t + hop) % shards for t in range(shards)) for hop in pair) for pair in hops
+    ]
 
 
 def direct_body(
@@ -315,14 +332,14 @@
             channel_logit_divisor,
         )
     )
-    rounds = [(hop + 1, hop) for hop in range(1, shards - 1, 2)] + [(shards - 1, shards - 1)]
+    rounds = permute_rounds(shards)
     arrived = [
         lax.ppermute(
             anchors,
             ("tok", "head"),
-            [(2 * t + core, 2 * ((t + hop[core]) % shards) + core) for t in range(shards) for core in (0, 1)],
+            [(2 * t + core, 2 * targets[core][t] + core) for t in range(shards) for core in (0, 1)],
         )
-        for hop in rounds[-1:] + rounds[:-1]
+        for targets in rounds[-1:] + rounds[:-1]
     ]
     queries, value_turned = pl.pallas_call(
         query_kernel,

time: 16.9 us -> 16.2 us (0.959)
  starting transfers between devices: 8.64 us -> 7.82 us
  waiting for transfers between devices: 3.73 us -> 3.95 us
    ppermute x4, starting transfers between devices: 8.4 us -> 7.48 us  [direct_body(): lax.ppermute(anchors, ('tok', 'head'), [(2 * t + core, 2 * targets[core][...]
    ppermute x4, waiting for transfers between devices: 1.95 us -> 2.39 us  [direct_body(): lax.ppermute(anchors, ('tok', 'head'), [(2 * t + core, 2 * targets[core][...]
    ppermute x3, waiting for transfers between devices: 0.41 us -> 0.18 us  [direct_body(): lax.ppermute(block, 'head', [(0, 1), (1, 0)])]
  transfers between devices with their start and end apart: 8 -> 8, of which waited for: 5 -> 6; matrix products, arithmetic and copies ran while one was open for 0% -> 0% of each run, Pallas kernels for 4% -> 4%
where the time goes in v6:
time: 16.2 us; the launch traced here: 16.1 us
  starting transfers between devices  7.82 us (48%)
  Pallas kernels  4.29 us (26%)
  waiting for transfers between devices  3.95 us (24%)
    ppermute x4, starting transfers between devices, direct_body(): lax.ppermute(anchors, ('tok', 'head'), [(2 * t + core, 2 * targets[core][...  7.48 us
    ppermute x4, waiting for transfers between devices, direct_body(): lax.ppermute(anchors, ('tok', 'head'), [(2 * t + core, 2 * targets[core][...  2.39 us
    pallas_call x1, Pallas kernels, direct_body(): pl.pallas_call(anchor_kernel, out_shape=(jax.ShapeDtypeStruct((picks, wid...  1.43 us
    ppermute x1, waiting for transfers between devices, direct_body(): other = lax.ppermute(terms, 'head', [(0, 1), (1, 0)])  1.38 us
    pallas_call x1, Pallas kernels, direct_body(): pl.pallas_call(functools.partial(attention_kernel, len(blocks)), out_shap...  1.3 us
    pallas_call x1, Pallas kernels, direct_body(): pl.pallas_call(finish_kernel, out_shape=jax.ShapeDtypeStruct((cells, loca...  0.83 us
    pallas_call x1, Pallas kernels, direct_body(): pl.pallas_call(query_kernel, out_shape=(jax.ShapeDtypeStruct((heads // 2,...  0.72 us
  transfers between devices with their start and end apart: 8, of which 6 were waited for; matrix products, arithmetic and copies ran while one was open for 0% of the time, Pallas kernels for 4%

profile of v6, /device:TPU:0, one launch (start us, length us, event | category | flops | bytes accessed | tf_op | source)
XLA Modules:
  0.0 16.1 jit_solution(14568132714622254063)
XLA Ops:
  0.0 1.4 %anchors.1 = (bf16[24,1024]{1,0:T(8,128)(2,1)S(1)}, bf16[128,1024]{1,0:T(8,128)(2,1)S(1)}, f32[1,1024]{1,0:T(1,128)S(1)}, f32[4,256]{1,0:T(4,128)S(1)}) custom-call(s32[16]{0:T(128)} %refs_0_.1, s32[8]{0:T(128)} %refs_1_.1, bf16[128,1024]{1,0:T(8,128)(2,1)} %refs_2_.1, bf16[32,1024]{1,0:T(8,128)(2,1)} %refs_3_.1, f32[1,1024]{1,0:T(1,128)} %bitcast.2, ...), custom_call_target="tpu_custom_call" | custom-call | flops 20000000000 | bytes 1048576 | tf_op jit(solution)/shard_map/anchors/pallas_call | solution.py:303
  1.4 4.1 %collective-permute-start.1 = (bf16[24,1024]{1,0:T(8,128)(2,1)S(1)}, bf16[24,1024]{1,0:T(8,128)(2,1)S(1)}, u32[]{:S(2)}, u32[]{:S(2)}) collective-permute-start(bf16[24,1024]{1,0:T(8,128)(2,1)S(1)} %get-tuple-element.16.rest_0_), channel_id=1, source_target_pairs={{0,8},{1,5},{2,4},{3,13},{4,10},{5,9},{6,12},{7,15},{8,2},{9,7},{1... | collective-permute-start | bytes 147464 | tf_op jit(solution)/shard_map/ppermute | solution.py:337
  5.5 0.5 %collective-permute-start.2 = (bf16[24,1024]{1,0:T(8,128)(2,1)S(1)}, bf16[24,1024]{1,0:T(8,128)(2,1)S(1)}, u32[]{:S(2)}, u32[]{:S(2)}) collective-permute-start(bf16[24,1024]{1,0:T(8,128)(2,1)S(1)} %get-tuple-element.16.rest_0_), channel_id=1, source_target_pairs={{0,2},{1,11},{2,14},{3,9},{4,6},{5,15},{6,10},{7,3},{8,0},{9,13},{... | collective-permute-start | bytes 147464 | tf_op jit(solution)/shard_map/ppermute | solution.py:337
  6.0 2.1 %collective-permute-start.3 = (bf16[24,1024]{1,0:T(8,128)(2,1)S(1)}, bf16[24,1024]{1,0:T(8,128)(2,1)S(1)}, u32[]{:S(2)}, u32[]{:S(2)}) collective-permute-start(bf16[24,1024]{1,0:T(8,128)(2,1)S(1)} %get-tuple-element.16.rest_0_), channel_id=1, source_target_pairs={{0,14},{1,13},{2,10},{3,7},{4,12},{5,1},{6,0},{7,5},{8,4},{9,11},{... | collective-permute-start | bytes 147464 | tf_op jit(solution)/shard_map/ppermute | solution.py:337
  8.1 0.8 %collective-permute-start = (bf16[24,1024]{1,0:T(8,128)(2,1)S(1)}, bf16[24,1024]{1,0:T(8,128)(2,1)S(1)}, u32[]{:S(2)}, u32[]{:S(2)}) collective-permute-start(bf16[24,1024]{1,0:T(8,128)(2,1)S(1)} %get-tuple-element.16.rest_0_), channel_id=1, source_target_pairs={{0,6},{1,7},{2,0},{3,1},{4,2},{5,3},{6,8},{7,9},{8,14},{9,15},{10,... | collective-permute-start | bytes 147464 | tf_op jit(solution)/shard_map/ppermute | solution.py:337
  8.9 0.4 %collective-permute-done.1.rest_2_ = bf16[24,1024]{1,0:T(8,128)(2,1)S(1)} collective-permute-done((bf16[24,1024]{1,0:T(8,128)(2,1)S(1)}, bf16[24,1024]{1,0:T(8,128)(2,1)S(1)}, u32[]{:S(2)}, u32[]{:S(2)}) %collective-permute-start.1) | collective-permute-done | bytes 49184 | tf_op jit(solution)/shard_map/ppermute | solution.py:337
  9.3 0.0 collective-permute-start.4
  9.3 1.4 %collective-permute-done.2.rest_3_ = bf16[24,1024]{1,0:T(8,128)(2,1)S(1)} collective-permute-done((bf16[24,1024]{1,0:T(8,128)(2,1)S(1)}, bf16[24,1024]{1,0:T(8,128)(2,1)S(1)}, u32[]{:S(2)}, u32[]{:S(2)}) %collective-permute-start.2) | collective-permute-done | bytes 49184 | tf_op jit(solution)/shard_map/ppermute | solution.py:337
  10.7 0.0 collective-permute-start.5
  10.7 0.4 %collective-permute-done.3.rest_4_ = bf16[24,1024]{1,0:T(8,128)(2,1)S(1)} collective-permute-done((bf16[24,1024]{1,0:T(8,128)(2,1)S(1)}, bf16[24,1024]{1,0:T(8,128)(2,1)S(1)}, u32[]{:S(2)}, u32[]{:S(2)}) %collective-permute-start.3) | collective-permute-done | bytes 49184 | tf_op jit(solution)/shard_map/ppermute | solution.py:337
  11.1 0.1 collective-permute-start.6
  11.3 0.0 copy-done
  11.3 0.0 copy-done.1
  11.3 0.0 copy-done.2
  11.3 0.0 copy-done.3
  11.3 0.7 %queries.1 = (bf16[4,128,256]{2,1,0:T(8,128)(2,1)S(1)}, bf16[512,1024]{1,0:T(8,128)(2,1)S(1)}) custom-call(bf16[128,1024]{1,0:T(8,128)(2,1)S(1)} %get-tuple-element.11.vol, f32[1,1024]{1,0:T(1,128)S(1)} %get-tuple-element.12.gain, bf16[1024,512]{1,0:T(8,128)(2,1)S(1)} %copy-done.2, bf16[1024,512]{1,0:T(8,128)(2,1)S(1)} %copy-done.3, ...), custom_call_target="tpu_custom_call" | custom-call | flops 134217728 | bytes 4194304 | tf_op jit(solution)/shard_map/queries/pallas_call | solution.py:344
  12.0 0.2 %collective-permute-done.rest_1_ = bf16[24,1024]{1,0:T(8,128)(2,1)S(1)} collective-permute-done((bf16[24,1024]{1,0:T(8,128)(2,1)S(1)}, bf16[24,1024]{1,0:T(8,128)(2,1)S(1)}, u32[]{:S(2)}, u32[]{:S(2)}) %collective-permute-start) | collective-permute-done | bytes 49184 | tf_op jit(solution)/shard_map/ppermute | solution.py:337
  12.2 0.0 collective-permute-done.4.rest_5_
  12.2 0.0 collective-permute-done.5.rest_6_
  12.2 0.2 %collective-permute-done.6.rest_7_ = bf16[24,1024]{1,0:T(8,128)(2,1)S(1)} collective-permute-done((bf16[24,1024]{1,0:T(8,128)(2,1)S(1)}, bf16[24,1024]{1,0:T(8,128)(2,1)S(1)}, u32[]{:S(2)}, u32[]{:S(2)}) %collective-permute-start.6) | collective-permute-done | bytes 49184 | tf_op jit(solution)/shard_map/ppermute | solution.py:358
  12.4 1.3 %attention.1.own = bf16[128,1024]{1,0:T(8,128)(2,1)S(1)} custom-call(bf16[4,128,256]{2,1,0:T(8,128)(2,1)S(1)} %get-tuple-element.13.queries, f32[4,256]{1,0:T(4,128)S(1)} %get-tuple-element.14.multiplier, bf16[1024,512]{1,0:T(8,128)(2,1)S(1)} %copy-done, bf16[512,1024]{1,0:T(8,128)(2,1)S(1)} %get-tuple-element.15.value_turned, ...), custom_call_target="tpu_custom_call" | custom-call | tf_op jit(solution)/shard_map/attention/pallas_call | solution.py:360
  13.7 0.2 %collective-permute-start.7 = (bf16[128,1024]{1,0:T(8,128)(2,1)S(1)}, bf16[128,1024]{1,0:T(8,128)(2,1)S(1)}, u32[]{:S(2)}, u32[]{:S(2)}) collective-permute-start(bf16[128,1024]{1,0:T(8,128)(2,1)S(1)} %attention.1.own), channel_id=1, source_target_pairs={{0,1},{1,0},{2,3},{3,2},{4,5},{5,4},{6,7},{7,6},{8,9},{9,8},{10,11... | collective-permute-start | bytes 786440 | tf_op jit(solution)/shard_map/ppermute | solution.py:370
  13.9 1.4 %collective-permute-done.7.other = bf16[128,1024]{1,0:T(8,128)(2,1)S(1)} collective-permute-done((bf16[128,1024]{1,0:T(8,128)(2,1)S(1)}, bf16[128,1024]{1,0:T(8,128)(2,1)S(1)}, u32[]{:S(2)}, u32[]{:S(2)}) %collective-permute-start.7) | collective-permute-done | bytes 262176 | tf_op jit(solution)/shard_map/ppermute | solution.py:370
  15.3 0.8 %finish.1 = bf16[128,512]{1,0:T(8,128)(2,1)} custom-call(bf16[128,1024]{1,0:T(8,128)(2,1)S(1)} %attention.1.own, bf16[128,1024]{1,0:T(8,128)(2,1)S(1)} %collective-permute-done.7.other), custom_call_target="tpu_custom_call" | custom-call | tf_op jit(solution)/shard_map/finish/pallas_call | solution.py:371
  (4 shorter events, 0.0 us)
Async XLA Ops:
  0.0 11.3 %copy-start = (bf16[1024,512]{1,0:T(8,128)(2,1)S(1)}, bf16[1024,512]{1,0:T(8,128)(2,1)}, u32[]{:S(2)}) copy-start(bf16[1024,512]{1,0:T(8,128)(2,1)} %lookup.3) | copy-start | bytes 3145732
  0.0 11.3 %copy-start.1 = (bf16[512,1024]{1,0:T(8,128)(2,1)S(1)}, bf16[512,1024]{1,0:T(8,128)(2,1)}, u32[]{:S(2)}) copy-start(bf16[512,1024]{1,0:T(8,128)(2,1)} %final.3) | copy-start | bytes 3145732
  0.0 11.3 %copy-start.2 = (bf16[1024,512]{1,0:T(8,128)(2,1)S(1)}, bf16[1024,512]{1,0:T(8,128)(2,1)}, u32[]{:S(2)}) copy-start(bf16[1024,512]{1,0:T(8,128)(2,1)} %projection.1) | copy-start | bytes 3145732
  0.0 11.3 %copy-start.3 = (bf16[1024,512]{1,0:T(8,128)(2,1)S(1)}, bf16[1024,512]{1,0:T(8,128)(2,1)}, u32[]{:S(2)}) copy-start(bf16[1024,512]{1,0:T(8,128)(2,1)} %value_projection.1) | copy-start | bytes 3145732
  1.4 7.8 %collective-permute-start.1 = (bf16[24,1024]{1,0:T(8,128)(2,1)S(1)}, bf16[24,1024]{1,0:T(8,128)(2,1)S(1)}, u32[]{:S(2)}, u32[]{:S(2)}) collective-permute-start(bf16[24,1024]{1,0:T(8,128)(2,1)S(1)} %get-tuple-element.16.rest_0_), channel_id=1, source_target_pairs={{0,8},{1,5},{2,4},{3,13},{4,10},{5,9},{6,12},{7,15},{8,2},{9,7},{1... | collective-permute-start | bytes 147464 | tf_op jit(solution)/shard_map/ppermute | solution.py:337
  5.5 5.2 %collective-permute-start.2 = (bf16[24,1024]{1,0:T(8,128)(2,1)S(1)}, bf16[24,1024]{1,0:T(8,128)(2,1)S(1)}, u32[]{:S(2)}, u32[]{:S(2)}) collective-permute-start(bf16[24,1024]{1,0:T(8,128)(2,1)S(1)} %get-tuple-element.16.rest_0_), channel_id=1, source_target_pairs={{0,2},{1,11},{2,14},{3,9},{4,6},{5,15},{6,10},{7,3},{8,0},{9,13},{... | collective-permute-start | bytes 147464 | tf_op jit(solution)/shard_map/ppermute | solution.py:337
  6.0 5.1 %collective-permute-start.3 = (bf16[24,1024]{1,0:T(8,128)(2,1)S(1)}, bf16[24,1024]{1,0:T(8,128)(2,1)S(1)}, u32[]{:S(2)}, u32[]{:S(2)}) collective-permute-start(bf16[24,1024]{1,0:T(8,128)(2,1)S(1)} %get-tuple-element.16.rest_0_), channel_id=1, source_target_pairs={{0,14},{1,13},{2,10},{3,7},{4,12},{5,1},{6,0},{7,5},{8,4},{9,11},{... | collective-permute-start | bytes 147464 | tf_op jit(solution)/shard_map/ppermute | solution.py:337
  8.1 4.1 %collective-permute-start = (bf16[24,1024]{1,0:T(8,128)(2,1)S(1)}, bf16[24,1024]{1,0:T(8,128)(2,1)S(1)}, u32[]{:S(2)}, u32[]{:S(2)}) collective-permute-start(bf16[24,1024]{1,0:T(8,128)(2,1)S(1)} %get-tuple-element.16.rest_0_), channel_id=1, source_target_pairs={{0,6},{1,7},{2,0},{3,1},{4,2},{5,3},{6,8},{7,9},{8,14},{9,15},{10,... | collective-permute-start | bytes 147464 | tf_op jit(solution)/shard_map/ppermute | solution.py:337
  9.3 2.9 %collective-permute-start.4 = (bf16[24,1024]{1,0:T(8,128)(2,1)S(1)}, bf16[24,1024]{1,0:T(8,128)(2,1)S(1)}, u32[]{:S(2)}, u32[]{:S(2)}) collective-permute-start(bf16[24,1024]{1,0:T(8,128)(2,1)S(1)} %collective-permute-done.1.rest_2_), channel_id=1, source_target_pairs={{0,1},{1,0},{2,3},{3,2},{4,5},{5,4},{6,7},{7,6},{8,9},{9,8},{10,11... | collective-permute-start | bytes 147464 | tf_op jit(solution)/shard_map/ppermute | solution.py:358
  10.7 1.4 %collective-permute-start.5 = (bf16[24,1024]{1,0:T(8,128)(2,1)S(1)}, bf16[24,1024]{1,0:T(8,128)(2,1)S(1)}, u32[]{:S(2)}, u32[]{:S(2)}) collective-permute-start(bf16[24,1024]{1,0:T(8,128)(2,1)S(1)} %collective-permute-done.2.rest_3_), channel_id=1, source_target_pairs={{0,1},{1,0},{2,3},{3,2},{4,5},{5,4},{6,7},{7,6},{8,9},{9,8},{10,11... | collective-permute-start | bytes 147464 | tf_op jit(solution)/shard_map/ppermute | solution.py:358
  11.1 1.2 %collective-permute-start.6 = (bf16[24,1024]{1,0:T(8,128)(2,1)S(1)}, bf16[24,1024]{1,0:T(8,128)(2,1)S(1)}, u32[]{:S(2)}, u32[]{:S(2)}) collective-permute-start(bf16[24,1024]{1,0:T(8,128)(2,1)S(1)} %collective-permute-done.3.rest_4_), channel_id=1, source_target_pairs={{0,1},{1,0},{2,3},{3,2},{4,5},{5,4},{6,7},{7,6},{8,9},{9,8},{10,11... | collective-permute-start | bytes 147464 | tf_op jit(solution)/shard_map/ppermute | solution.py:358
  13.7 1.6 %collective-permute-start.7 = (bf16[128,1024]{1,0:T(8,128)(2,1)S(1)}, bf16[128,1024]{1,0:T(8,128)(2,1)S(1)}, u32[]{:S(2)}, u32[]{:S(2)}) collective-permute-start(bf16[128,1024]{1,0:T(8,128)(2,1)S(1)} %attention.1.own), channel_id=1, source_target_pairs={{0,1},{1,0},{2,3},{3,2},{4,5},{5,4},{6,7},{7,6},{8,9},{9,8},{10,11... | collective-permute-start | bytes 786440 | tf_op jit(solution)/shard_map/ppermute | solution.py:370

commit v7 on v6

--- a/solution.py
+++ b/solution.py
@@ -265,19 +265,20 @@
 
 
 SEARCHED_ROUNDS = [
-    ((4, 2, 5, 6, 1, 7, 0, 3), (2, 6, 4, 7, 3, 0, 1, 5)),
-    ((1, 7, 3, 5, 0, 2, 4, 6), (5, 4, 7, 1, 6, 3, 2, 0)),
-    ((7, 5, 6, 0, 2, 1, 3, 4), (6, 3, 0, 2, 5, 4, 7, 1)),
-    ((3, 0, 1, 4, 7, 6, 5, 2), (3, 0, 1, 4, 7, 6, 5, 2)),
+    (7, 2, 11, 8, 9, 6, 10, 13, 5, 14, 15, 0, 4, 3, 12, 1),
+    (11, 8, 15, 4, 13, 2, 14, 9, 0, 3, 7, 12, 1, 10, 6, 5),
+    (5, 12, 7, 0, 11, 14, 1, 2, 13, 6, 4, 9, 8, 15, 3, 10),
+    (14, 15, 13, 12, 1, 0, 4, 5, 10, 11, 3, 2, 6, 7, 9, 8),
 ]
 
 
 def permute_rounds(shards):
-    if shards == len(SEARCHED_ROUNDS[0][0]):
+    if 2 * shards == len(SEARCHED_ROUNDS[0]):
         return SEARCHED_ROUNDS
     hops = [(hop + 1, hop) for hop in range(1, shards - 1, 2)] + [(shards - 1, shards - 1)]
     return [
-        tuple(tuple((t + hop) % shards for t in range(shards)) for hop in pair) for pair in hops
+        tuple(2 * ((t + pair[core]) % shards) + core for t in range(shards) for core in (0, 1))
+        for pair in hops
     ]
 
 
@@ -334,11 +335,7 @@
     )
     rounds = permute_rounds(shards)
     arrived = [
-        lax.ppermute(
-            anchors,
-            ("tok", "head"),
-            [(2 * t + core, 2 * targets[core][t] + core) for t in range(shards) for core in (0, 1)],
-        )
+        lax.ppermute(anchors, ("tok", "head"), list(enumerate(targets)))
         for targets in rounds[-1:] + rounds[:-1]
     ]
     queries, value_turned = pl.pallas_call(

time: 16.2 us -> 16 us (0.988)
  waiting for transfers between devices: 3.95 us -> 2.03 us
  starting transfers between devices: 7.82 us -> 9.48 us
    ppermute x4, waiting for transfers between devices: 2.39 us -> 0.73 us  [direct_body(): lax.ppermute(anchors, ('tok', 'head'), list(enumerate(targets)))]
    ppermute x4, starting transfers between devices: 7.48 us -> 8.55 us  [direct_body(): lax.ppermute(anchors, ('tok', 'head'), list(enumerate(targets)))]
    ppermute x3, starting transfers between devices: 0.12 us -> 0.51 us  [direct_body(): lax.ppermute(block, 'head', [(0, 1), (1, 0)])]
    ppermute x1, starting transfers between devices: 0.22 us -> 0.42 us  [direct_body(): other = lax.ppermute(terms, 'head', [(0, 1), (1, 0)])]
    ppermute x1, waiting for transfers between devices: 1.38 us -> 1.19 us  [direct_body(): other = lax.ppermute(terms, 'head', [(0, 1), (1, 0)])]
  transfers between devices with their start and end apart: 8 -> 8, of which waited for: 6 -> 3; matrix products, arithmetic and copies ran while one was open for 0% -> 0% of each run, Pallas kernels for 4% -> 5%
where the time goes in v7:
time: 16 us; the launch traced here: 15.9 us
  starting transfers between devices  9.48 us (59%)
  Pallas kernels  4.29 us (27%)
  waiting for transfers between devices  2.03 us (13%)
    ppermute x4, starting transfers between devices, direct_body(): lax.ppermute(anchors, ('tok', 'head'), list(enumerate(targets)))  8.55 us
    pallas_call x1, Pallas kernels, direct_body(): pl.pallas_call(anchor_kernel, out_shape=(jax.ShapeDtypeStruct((picks, wid...  1.43 us
    pallas_call x1, Pallas kernels, direct_body(): pl.pallas_call(functools.partial(attention_kernel, len(blocks)), out_shap...  1.3 us
    ppermute x1, waiting for transfers between devices, direct_body(): other = lax.ppermute(terms, 'head', [(0, 1), (1, 0)])  1.19 us
    pallas_call x1, Pallas kernels, direct_body(): pl.pallas_call(finish_kernel, out_shape=jax.ShapeDtypeStruct((cells, loca...  0.83 us
    ppermute x4, waiting for transfers between devices, direct_body(): lax.ppermute(anchors, ('tok', 'head'), list(enumerate(targets)))  0.73 us
    pallas_call x1, Pallas kernels, direct_body(): pl.pallas_call(query_kernel, out_shape=(jax.ShapeDtypeStruct((heads // 2,...  0.72 us
    ppermute x3, starting transfers between devices, direct_body(): lax.ppermute(block, 'head', [(0, 1), (1, 0)])  0.51 us
  transfers between devices with their start and end apart: 8, of which 3 were waited for; matrix products, arithmetic and copies ran while one was open for 0% of the time, Pallas kernels for 5%

profile of v7, /device:TPU:0, one launch (start us, length us, event | category | flops | bytes accessed | tf_op | source)
XLA Modules:
  0.0 15.9 jit_solution(11318524622984288915)
XLA Ops:
  0.0 1.4 %anchors.1 = (bf16[24,1024]{1,0:T(8,128)(2,1)S(1)}, bf16[128,1024]{1,0:T(8,128)(2,1)S(1)}, f32[1,1024]{1,0:T(1,128)S(1)}, f32[4,256]{1,0:T(4,128)S(1)}) custom-call(s32[16]{0:T(128)} %refs_0_.1, s32[8]{0:T(128)} %refs_1_.1, bf16[128,1024]{1,0:T(8,128)(2,1)} %refs_2_.1, bf16[32,1024]{1,0:T(8,128)(2,1)} %refs_3_.1, f32[1,1024]{1,0:T(1,128)} %bitcast.2, ...), custom_call_target="tpu_custom_call" | custom-call | flops 20000000000 | bytes 1048576 | tf_op jit(solution)/shard_map/anchors/pallas_call | solution.py:304
  1.4 3.5 %collective-permute-start.1 = (bf16[24,1024]{1,0:T(8,128)(2,1)S(1)}, bf16[24,1024]{1,0:T(8,128)(2,1)S(1)}, u32[]{:S(2)}, u32[]{:S(2)}) collective-permute-start(bf16[24,1024]{1,0:T(8,128)(2,1)S(1)} %get-tuple-element.16.rest_0_), channel_id=1, source_target_pairs={{0,7},{1,2},{2,11},{3,8},{4,9},{5,6},{6,10},{7,13},{8,5},{9,14},{1... | collective-permute-start | bytes 147464 | tf_op jit(solution)/shard_map/ppermute | solution.py:338
  4.9 1.1 %collective-permute-start.2 = (bf16[24,1024]{1,0:T(8,128)(2,1)S(1)}, bf16[24,1024]{1,0:T(8,128)(2,1)S(1)}, u32[]{:S(2)}, u32[]{:S(2)}) collective-permute-start(bf16[24,1024]{1,0:T(8,128)(2,1)S(1)} %get-tuple-element.16.rest_0_), channel_id=1, source_target_pairs={{0,11},{1,8},{2,15},{3,4},{4,13},{5,2},{6,14},{7,9},{8,0},{9,3},{1... | collective-permute-start | bytes 147464 | tf_op jit(solution)/shard_map/ppermute | solution.py:338
  6.0 1.7 %collective-permute-start.3 = (bf16[24,1024]{1,0:T(8,128)(2,1)S(1)}, bf16[24,1024]{1,0:T(8,128)(2,1)S(1)}, u32[]{:S(2)}, u32[]{:S(2)}) collective-permute-start(bf16[24,1024]{1,0:T(8,128)(2,1)S(1)} %get-tuple-element.16.rest_0_), channel_id=1, source_target_pairs={{0,5},{1,12},{2,7},{3,0},{4,11},{5,14},{6,1},{7,2},{8,13},{9,6},{1... | collective-permute-start | bytes 147464 | tf_op jit(solution)/shard_map/ppermute | solution.py:338
  7.7 2.3 %collective-permute-start = (bf16[24,1024]{1,0:T(8,128)(2,1)S(1)}, bf16[24,1024]{1,0:T(8,128)(2,1)S(1)}, u32[]{:S(2)}, u32[]{:S(2)}) collective-permute-start(bf16[24,1024]{1,0:T(8,128)(2,1)S(1)} %get-tuple-element.16.rest_0_), channel_id=1, source_target_pairs={{0,14},{1,15},{2,13},{3,12},{4,1},{5,0},{6,4},{7,5},{8,10},{9,11},... | collective-permute-start | bytes 147464 | tf_op jit(solution)/shard_map/ppermute | solution.py:338
  10.0 0.0 collective-permute-done.1.rest_2_
  10.0 0.0 collective-permute-start.4
  10.0 0.7 %collective-permute-done.2.rest_3_ = bf16[24,1024]{1,0:T(8,128)(2,1)S(1)} collective-permute-done((bf16[24,1024]{1,0:T(8,128)(2,1)S(1)}, bf16[24,1024]{1,0:T(8,128)(2,1)S(1)}, u32[]{:S(2)}, u32[]{:S(2)}) %collective-permute-start.2) | collective-permute-done | bytes 49184 | tf_op jit(solution)/shard_map/ppermute | solution.py:338
  10.7 0.0 collective-permute-start.5
  10.7 0.0 collective-permute-done.3.rest_4_
  10.7 0.5 %collective-permute-start.6 = (bf16[24,1024]{1,0:T(8,128)(2,1)S(1)}, bf16[24,1024]{1,0:T(8,128)(2,1)S(1)}, u32[]{:S(2)}, u32[]{:S(2)}) collective-permute-start(bf16[24,1024]{1,0:T(8,128)(2,1)S(1)} %collective-permute-done.3.rest_4_), channel_id=1, source_target_pairs={{0,1},{1,0},{2,3},{3,2},{4,5},{5,4},{6,7},{7,6},{8,9},{9,8},{10,11... | collective-permute-start | bytes 147464 | tf_op jit(solution)/shard_map/ppermute | solution.py:355
  11.2 0.0 copy-done
  11.3 0.0 copy-done.1
  11.3 0.0 copy-done.2
  11.3 0.0 copy-done.3
  11.3 0.7 %queries.1 = (bf16[4,128,256]{2,1,0:T(8,128)(2,1)S(1)}, bf16[512,1024]{1,0:T(8,128)(2,1)S(1)}) custom-call(bf16[128,1024]{1,0:T(8,128)(2,1)S(1)} %get-tuple-element.11.vol, f32[1,1024]{1,0:T(1,128)S(1)} %get-tuple-element.12.gain, bf16[1024,512]{1,0:T(8,128)(2,1)S(1)} %copy-done.2, bf16[1024,512]{1,0:T(8,128)(2,1)S(1)} %copy-done.3, ...), custom_call_target="tpu_custom_call" | custom-call | flops 134217728 | bytes 4194304 | tf_op jit(solution)/shard_map/queries/pallas_call | solution.py:341
  12.0 0.0 collective-permute-done.rest_1_
  12.0 0.0 collective-permute-done.4.rest_5_
  12.0 0.0 collective-permute-done.5.rest_6_
  12.0 0.1 collective-permute-done.6.rest_7_
  12.1 1.3 %attention.1.own = bf16[128,1024]{1,0:T(8,128)(2,1)S(1)} custom-call(bf16[4,128,256]{2,1,0:T(8,128)(2,1)S(1)} %get-tuple-element.13.queries, f32[4,256]{1,0:T(4,128)S(1)} %get-tuple-element.14.multiplier, bf16[1024,512]{1,0:T(8,128)(2,1)S(1)} %copy-done, bf16[512,1024]{1,0:T(8,128)(2,1)S(1)} %get-tuple-element.15.value_turned, ...), custom_call_target="tpu_custom_call" | custom-call | tf_op jit(solution)/shard_map/attention/pallas_call | solution.py:357
  13.4 0.4 %collective-permute-start.7 = (bf16[128,1024]{1,0:T(8,128)(2,1)S(1)}, bf16[128,1024]{1,0:T(8,128)(2,1)S(1)}, u32[]{:S(2)}, u32[]{:S(2)}) collective-permute-start(bf16[128,1024]{1,0:T(8,128)(2,1)S(1)} %attention.1.own), channel_id=1, source_target_pairs={{0,1},{1,0},{2,3},{3,2},{4,5},{5,4},{6,7},{7,6},{8,9},{9,8},{10,11... | collective-permute-start | bytes 786440 | tf_op jit(solution)/shard_map/ppermute | solution.py:367
  13.8 1.2 %collective-permute-done.7.other = bf16[128,1024]{1,0:T(8,128)(2,1)S(1)} collective-permute-done((bf16[128,1024]{1,0:T(8,128)(2,1)S(1)}, bf16[128,1024]{1,0:T(8,128)(2,1)S(1)}, u32[]{:S(2)}, u32[]{:S(2)}) %collective-permute-start.7) | collective-permute-done | bytes 262176 | tf_op jit(solution)/shard_map/ppermute | solution.py:367
  15.0 0.8 %finish.1 = bf16[128,512]{1,0:T(8,128)(2,1)} custom-call(bf16[128,1024]{1,0:T(8,128)(2,1)S(1)} %attention.1.own, bf16[128,1024]{1,0:T(8,128)(2,1)S(1)} %collective-permute-done.7.other), custom_call_target="tpu_custom_call" | custom-call | tf_op jit(solution)/shard_map/finish/pallas_call | solution.py:368
  (4 shorter events, 0.0 us)
Async XLA Ops:
  0.0 11.2 %copy-start = (bf16[1024,512]{1,0:T(8,128)(2,1)S(1)}, bf16[1024,512]{1,0:T(8,128)(2,1)}, u32[]{:S(2)}) copy-start(bf16[1024,512]{1,0:T(8,128)(2,1)} %lookup.3) | copy-start | bytes 3145732
  0.0 11.2 %copy-start.1 = (bf16[512,1024]{1,0:T(8,128)(2,1)S(1)}, bf16[512,1024]{1,0:T(8,128)(2,1)}, u32[]{:S(2)}) copy-start(bf16[512,1024]{1,0:T(8,128)(2,1)} %final.3) | copy-start | bytes 3145732
  0.0 11.3 %copy-start.2 = (bf16[1024,512]{1,0:T(8,128)(2,1)S(1)}, bf16[1024,512]{1,0:T(8,128)(2,1)}, u32[]{:S(2)}) copy-start(bf16[1024,512]{1,0:T(8,128)(2,1)} %projection.1) | copy-start | bytes 3145732
  0.0 11.3 %copy-start.3 = (bf16[1024,512]{1,0:T(8,128)(2,1)S(1)}, bf16[1024,512]{1,0:T(8,128)(2,1)}, u32[]{:S(2)}) copy-start(bf16[1024,512]{1,0:T(8,128)(2,1)} %value_projection.1) | copy-start | bytes 3145732
  1.4 8.6 %collective-permute-start.1 = (bf16[24,1024]{1,0:T(8,128)(2,1)S(1)}, bf16[24,1024]{1,0:T(8,128)(2,1)S(1)}, u32[]{:S(2)}, u32[]{:S(2)}) collective-permute-start(bf16[24,1024]{1,0:T(8,128)(2,1)S(1)} %get-tuple-element.16.rest_0_), channel_id=1, source_target_pairs={{0,7},{1,2},{2,11},{3,8},{4,9},{5,6},{6,10},{7,13},{8,5},{9,14},{1... | collective-permute-start | bytes 147464 | tf_op jit(solution)/shard_map/ppermute | solution.py:338
  4.9 5.8 %collective-permute-start.2 = (bf16[24,1024]{1,0:T(8,128)(2,1)S(1)}, bf16[24,1024]{1,0:T(8,128)(2,1)S(1)}, u32[]{:S(2)}, u32[]{:S(2)}) collective-permute-start(bf16[24,1024]{1,0:T(8,128)(2,1)S(1)} %get-tuple-element.16.rest_0_), channel_id=1, source_target_pairs={{0,11},{1,8},{2,15},{3,4},{4,13},{5,2},{6,14},{7,9},{8,0},{9,3},{1... | collective-permute-start | bytes 147464 | tf_op jit(solution)/shard_map/ppermute | solution.py:338
  6.0 4.7 %collective-permute-start.3 = (bf16[24,1024]{1,0:T(8,128)(2,1)S(1)}, bf16[24,1024]{1,0:T(8,128)(2,1)S(1)}, u32[]{:S(2)}, u32[]{:S(2)}) collective-permute-start(bf16[24,1024]{1,0:T(8,128)(2,1)S(1)} %get-tuple-element.16.rest_0_), channel_id=1, source_target_pairs={{0,5},{1,12},{2,7},{3,0},{4,11},{5,14},{6,1},{7,2},{8,13},{9,6},{1... | collective-permute-start | bytes 147464 | tf_op jit(solution)/shard_map/ppermute | solution.py:338
  7.7 4.3 %collective-permute-start = (bf16[24,1024]{1,0:T(8,128)(2,1)S(1)}, bf16[24,1024]{1,0:T(8,128)(2,1)S(1)}, u32[]{:S(2)}, u32[]{:S(2)}) collective-permute-start(bf16[24,1024]{1,0:T(8,128)(2,1)S(1)} %get-tuple-element.16.rest_0_), channel_id=1, source_target_pairs={{0,14},{1,15},{2,13},{3,12},{4,1},{5,0},{6,4},{7,5},{8,10},{9,11},... | collective-permute-start | bytes 147464 | tf_op jit(solution)/shard_map/ppermute | solution.py:338
  10.0 2.0 %collective-permute-start.4 = (bf16[24,1024]{1,0:T(8,128)(2,1)S(1)}, bf16[24,1024]{1,0:T(8,128)(2,1)S(1)}, u32[]{:S(2)}, u32[]{:S(2)}) collective-permute-start(bf16[24,1024]{1,0:T(8,128)(2,1)S(1)} %collective-permute-done.1.rest_2_), channel_id=1, source_target_pairs={{0,1},{1,0},{2,3},{3,2},{4,5},{5,4},{6,7},{7,6},{8,9},{9,8},{10,11... | collective-permute-start | bytes 147464 | tf_op jit(solution)/shard_map/ppermute | solution.py:355
  10.7 1.3 %collective-permute-start.5 = (bf16[24,1024]{1,0:T(8,128)(2,1)S(1)}, bf16[24,1024]{1,0:T(8,128)(2,1)S(1)}, u32[]{:S(2)}, u32[]{:S(2)}) collective-permute-start(bf16[24,1024]{1,0:T(8,128)(2,1)S(1)} %collective-permute-done.2.rest_3_), channel_id=1, source_target_pairs={{0,1},{1,0},{2,3},{3,2},{4,5},{5,4},{6,7},{7,6},{8,9},{9,8},{10,11... | collective-permute-start | bytes 147464 | tf_op jit(solution)/shard_map/ppermute | solution.py:355
  10.7 1.4 %collective-permute-start.6 = (bf16[24,1024]{1,0:T(8,128)(2,1)S(1)}, bf16[24,1024]{1,0:T(8,128)(2,1)S(1)}, u32[]{:S(2)}, u32[]{:S(2)}) collective-permute-start(bf16[24,1024]{1,0:T(8,128)(2,1)S(1)} %collective-permute-done.3.rest_4_), channel_id=1, source_target_pairs={{0,1},{1,0},{2,3},{3,2},{4,5},{5,4},{6,7},{7,6},{8,9},{9,8},{10,11... | collective-permute-start | bytes 147464 | tf_op jit(solution)/shard_map/ppermute | solution.py:355
  13.4 1.6 %collective-permute-start.7 = (bf16[128,1024]{1,0:T(8,128)(2,1)S(1)}, bf16[128,1024]{1,0:T(8,128)(2,1)S(1)}, u32[]{:S(2)}, u32[]{:S(2)}) collective-permute-start(bf16[128,1024]{1,0:T(8,128)(2,1)S(1)} %attention.1.own), channel_id=1, source_target_pairs={{0,1},{1,0},{2,3},{3,2},{4,5},{5,4},{6,7},{7,6},{8,9},{9,8},{10,11... | collective-permute-start | bytes 786440 | tf_op jit(solution)/shard_map/ppermute | solution.py:367

commit v8 on v7

--- a/solution.py
+++ b/solution.py
@@ -196,6 +196,10 @@
     left = lax.broadcasted_iota(jnp.int32, (1, wide), 1) < wide // 2
     for pair in range(pairs):
         multiplier[pair : pair + 1, :] = jnp.where(left, divisor[2 * pair], divisor[2 * pair + 1])
+
+
+def copy_kernel(source, target):
+    target[...] = source[...]
 
 
 def query_kernel(vol, gain, projection, value_projection, lookup, final, queries, value_turned):
@@ -320,7 +324,6 @@
             pltpu.SemaphoreType.DMA((7,)),
         ],
         compiler_params=PARAMS,
-        cost_estimate=pl.CostEstimate(flops=2*10**10, bytes_accessed=2**20, transcendentals=0),
         name="anchors",
     )(
         *in_hbm(
@@ -334,9 +337,18 @@
         )
     )
     rounds = permute_rounds(shards)
+    again = pl.pallas_call(
+        copy_kernel,
+        out_shape=jax.ShapeDtypeStruct(anchors.shape, anchors.dtype),
+        in_specs=[VMEM],
+        out_specs=VMEM,
+        compiler_params=PARAMS,
+        cost_estimate=pl.CostEstimate(flops=2 * 10**10, bytes_accessed=2**16, transcendentals=0),
+        name="again",
+    )(*in_vmem(anchors))
     arrived = [
-        lax.ppermute(anchors, ("tok", "head"), list(enumerate(targets)))
-        for targets in rounds[-1:] + rounds[:-1]
+        lax.ppermute(sent, ("tok", "head"), list(enumerate(targets)))
+        for sent, targets in [(again, rounds[-1])] + [(anchors, targets) for targets in rounds[:-1]]
     ]
     queries, value_turned = pl.pallas_call(
         query_kernel,

time: 16 us -> 15.9 us (level)
  no operation moved by 1% of the time
where the time goes in v8:
time: 15.9 us; the launch traced here: 15.7 us
  starting transfers between devices  9.47 us (60%)
  Pallas kernels  4.14 us (26%)
  waiting for transfers between devices  2.02 us (13%)
    ppermute x4, starting transfers between devices, direct_body(): lax.ppermute(sent, ('tok', 'head'), list(enumerate(targets)))  8.54 us
    pallas_call x1, Pallas kernels, direct_body(): pl.pallas_call(functools.partial(attention_kernel, len(blocks)), out_shap...  1.31 us
    pallas_call x1, Pallas kernels, direct_body(): pl.pallas_call(anchor_kernel, out_shape=(jax.ShapeDtypeStruct((picks, wid...  1.28 us
    ppermute x1, waiting for transfers between devices, direct_body(): other = lax.ppermute(terms, 'head', [(0, 1), (1, 0)])  1.19 us
    pallas_call x1, Pallas kernels, direct_body(): pl.pallas_call(finish_kernel, out_shape=jax.ShapeDtypeStruct((cells, loca...  0.83 us
    ppermute x4, waiting for transfers between devices, direct_body(): lax.ppermute(sent, ('tok', 'head'), list(enumerate(targets)))  0.73 us
    pallas_call x1, Pallas kernels, direct_body(): pl.pallas_call(query_kernel, out_shape=(jax.ShapeDtypeStruct((heads // 2,...  0.72 us
    ppermute x3, starting transfers between devices, direct_body(): lax.ppermute(block, 'head', [(0, 1), (1, 0)])  0.51 us
  transfers between devices with their start and end apart: 8, of which 3 were waited for; matrix products, arithmetic and copies ran while one was open for 0% of the time, Pallas kernels for 5%

profile of v8, /device:TPU:0, one launch (start us, length us, event | category | flops | bytes accessed | tf_op | source)
XLA Modules:
  0.0 15.7 jit_solution(17514837159017562600)
XLA Ops:
  0.0 1.3 %anchors.1 = (bf16[24,1024]{1,0:T(8,128)(2,1)S(1)}, bf16[128,1024]{1,0:T(8,128)(2,1)S(1)}, f32[1,1024]{1,0:T(1,128)S(1)}, f32[4,256]{1,0:T(4,128)S(1)}) custom-call(s32[16]{0:T(128)} %refs_0_.1, s32[8]{0:T(128)} %refs_1_.1, bf16[128,1024]{1,0:T(8,128)(2,1)} %refs_2_.1, bf16[32,1024]{1,0:T(8,128)(2,1)} %refs_3_.1, f32[1,1024]{1,0:T(1,128)} %bitcast.2, ...), custom_call_target="tpu_custom_call" | custom-call | tf_op jit(solution)/shard_map/anchors/pallas_call | solution.py:308
  1.3 0.0 copy-start
  1.3 0.0 copy-start.1
  1.3 0.0 copy-start.2
  1.3 0.0 copy-start.3
  1.3 3.5 %collective-permute-start.1 = (bf16[24,1024]{1,0:T(8,128)(2,1)S(1)}, bf16[24,1024]{1,0:T(8,128)(2,1)S(1)}, u32[]{:S(2)}, u32[]{:S(2)}) collective-permute-start(bf16[24,1024]{1,0:T(8,128)(2,1)S(1)} %get-tuple-element.16.source.rest_0_), channel_id=1, source_target_pairs={{0,7},{1,2},{2,11},{3,8},{4,9},{5,6},{6,10},{7,13},{8,5},{9,14},{1... | collective-permute-start | bytes 147464 | tf_op jit(solution)/shard_map/ppermute | solution.py:350
  4.8 1.1 %collective-permute-start.2 = (bf16[24,1024]{1,0:T(8,128)(2,1)S(1)}, bf16[24,1024]{1,0:T(8,128)(2,1)S(1)}, u32[]{:S(2)}, u32[]{:S(2)}) collective-permute-start(bf16[24,1024]{1,0:T(8,128)(2,1)S(1)} %get-tuple-element.16.source.rest_0_), channel_id=1, source_target_pairs={{0,11},{1,8},{2,15},{3,4},{4,13},{5,2},{6,14},{7,9},{8,0},{9,3},{1... | collective-permute-start | bytes 147464 | tf_op jit(solution)/shard_map/ppermute | solution.py:350
  5.9 1.7 %collective-permute-start.3 = (bf16[24,1024]{1,0:T(8,128)(2,1)S(1)}, bf16[24,1024]{1,0:T(8,128)(2,1)S(1)}, u32[]{:S(2)}, u32[]{:S(2)}) collective-permute-start(bf16[24,1024]{1,0:T(8,128)(2,1)S(1)} %get-tuple-element.16.source.rest_0_), channel_id=1, source_target_pairs={{0,5},{1,12},{2,7},{3,0},{4,11},{5,14},{6,1},{7,2},{8,13},{9,6},{1... | collective-permute-start | bytes 147464 | tf_op jit(solution)/shard_map/ppermute | solution.py:350
  7.5 2.3 %collective-permute-start = (bf16[24,1024]{1,0:T(8,128)(2,1)S(1)}, bf16[24,1024]{1,0:T(8,128)(2,1)S(1)}, u32[]{:S(2)}, u32[]{:S(2)}) collective-permute-start(bf16[24,1024]{1,0:T(8,128)(2,1)S(1)} %again.1), channel_id=1, source_target_pairs={{0,14},{1,15},{2,13},{3,12},{4,1},{5,0},{6,4},{7,5},{8,10},{9,11},... | collective-permute-start | bytes 147464 | tf_op jit(solution)/shard_map/ppermute | solution.py:350
  9.9 0.0 collective-permute-done.1.rest_2_
  9.9 0.0 collective-permute-start.4
  9.9 0.7 %collective-permute-done.2.rest_3_ = bf16[24,1024]{1,0:T(8,128)(2,1)S(1)} collective-permute-done((bf16[24,1024]{1,0:T(8,128)(2,1)S(1)}, bf16[24,1024]{1,0:T(8,128)(2,1)S(1)}, u32[]{:S(2)}, u32[]{:S(2)}) %collective-permute-start.2) | collective-permute-done | bytes 49184 | tf_op jit(solution)/shard_map/ppermute | solution.py:350
  10.6 0.0 collective-permute-start.5
  10.6 0.0 collective-permute-done.3.rest_4_
  10.6 0.5 %collective-permute-start.6 = (bf16[24,1024]{1,0:T(8,128)(2,1)S(1)}, bf16[24,1024]{1,0:T(8,128)(2,1)S(1)}, u32[]{:S(2)}, u32[]{:S(2)}) collective-permute-start(bf16[24,1024]{1,0:T(8,128)(2,1)S(1)} %collective-permute-done.3.rest_4_), channel_id=1, source_target_pairs={{0,1},{1,0},{2,3},{3,2},{4,5},{5,4},{6,7},{7,6},{8,9},{9,8},{10,11... | collective-permute-start | bytes 147464 | tf_op jit(solution)/shard_map/ppermute | solution.py:367
  11.1 0.7 %queries.1 = (bf16[4,128,256]{2,1,0:T(8,128)(2,1)S(1)}, bf16[512,1024]{1,0:T(8,128)(2,1)S(1)}) custom-call(bf16[128,1024]{1,0:T(8,128)(2,1)S(1)} %get-tuple-element.11.vol, f32[1,1024]{1,0:T(1,128)S(1)} %get-tuple-element.12.gain, bf16[1024,512]{1,0:T(8,128)(2,1)S(1)} %copy-done.2, bf16[1024,512]{1,0:T(8,128)(2,1)S(1)} %copy-done.3, ...), custom_call_target="tpu_custom_call" | custom-call | flops 134217728 | bytes 4194304 | tf_op jit(solution)/shard_map/queries/pallas_call | solution.py:353
  11.9 0.0 collective-permute-done.rest_1_
  11.9 0.0 collective-permute-done.4.rest_5_
  11.9 0.0 collective-permute-done.5.rest_6_
  11.9 0.1 collective-permute-done.6.rest_7_
  12.0 1.3 %attention.1.own = bf16[128,1024]{1,0:T(8,128)(2,1)S(1)} custom-call(bf16[4,128,256]{2,1,0:T(8,128)(2,1)S(1)} %get-tuple-element.13.queries, f32[4,256]{1,0:T(4,128)S(1)} %get-tuple-element.14.multiplier, bf16[1024,512]{1,0:T(8,128)(2,1)S(1)} %copy-done, bf16[512,1024]{1,0:T(8,128)(2,1)S(1)} %get-tuple-element.15.value_turned, ...), custom_call_target="tpu_custom_call" | custom-call | tf_op jit(solution)/shard_map/attention/pallas_call | solution.py:369
  13.3 0.4 %collective-permute-start.7 = (bf16[128,1024]{1,0:T(8,128)(2,1)S(1)}, bf16[128,1024]{1,0:T(8,128)(2,1)S(1)}, u32[]{:S(2)}, u32[]{:S(2)}) collective-permute-start(bf16[128,1024]{1,0:T(8,128)(2,1)S(1)} %attention.1.own), channel_id=1, source_target_pairs={{0,1},{1,0},{2,3},{3,2},{4,5},{5,4},{6,7},{7,6},{8,9},{9,8},{10,11... | collective-permute-start | bytes 786440 | tf_op jit(solution)/shard_map/ppermute | solution.py:379
  13.7 1.2 %collective-permute-done.7.other = bf16[128,1024]{1,0:T(8,128)(2,1)S(1)} collective-permute-done((bf16[128,1024]{1,0:T(8,128)(2,1)S(1)}, bf16[128,1024]{1,0:T(8,128)(2,1)S(1)}, u32[]{:S(2)}, u32[]{:S(2)}) %collective-permute-start.7) | collective-permute-done | bytes 262176 | tf_op jit(solution)/shard_map/ppermute | solution.py:379
  14.9 0.8 %finish.1 = bf16[128,512]{1,0:T(8,128)(2,1)} custom-call(bf16[128,1024]{1,0:T(8,128)(2,1)S(1)} %attention.1.own, bf16[128,1024]{1,0:T(8,128)(2,1)S(1)} %collective-permute-done.7.other), custom_call_target="tpu_custom_call" | custom-call | tf_op jit(solution)/shard_map/finish/pallas_call | solution.py:380
  (5 shorter events, 0.0 us)
Async XLA Ops:
  1.3 9.8 %copy-start = (bf16[1024,512]{1,0:T(8,128)(2,1)S(1)}, bf16[1024,512]{1,0:T(8,128)(2,1)}, u32[]{:S(2)}) copy-start(bf16[1024,512]{1,0:T(8,128)(2,1)} %lookup.3) | copy-start | bytes 3145732
  1.3 9.8 %copy-start.1 = (bf16[512,1024]{1,0:T(8,128)(2,1)S(1)}, bf16[512,1024]{1,0:T(8,128)(2,1)}, u32[]{:S(2)}) copy-start(bf16[512,1024]{1,0:T(8,128)(2,1)} %final.3) | copy-start | bytes 3145732
  1.3 9.8 %copy-start.2 = (bf16[1024,512]{1,0:T(8,128)(2,1)S(1)}, bf16[1024,512]{1,0:T(8,128)(2,1)}, u32[]{:S(2)}) copy-start(bf16[1024,512]{1,0:T(8,128)(2,1)} %projection.1) | copy-start | bytes 3145732
  1.3 9.8 %copy-start.3 = (bf16[1024,512]{1,0:T(8,128)(2,1)S(1)}, bf16[1024,512]{1,0:T(8,128)(2,1)}, u32[]{:S(2)}) copy-start(bf16[1024,512]{1,0:T(8,128)(2,1)} %value_projection.1) | copy-start | bytes 3145732
  1.3 8.6 %collective-permute-start.1 = (bf16[24,1024]{1,0:T(8,128)(2,1)S(1)}, bf16[24,1024]{1,0:T(8,128)(2,1)S(1)}, u32[]{:S(2)}, u32[]{:S(2)}) collective-permute-start(bf16[24,1024]{1,0:T(8,128)(2,1)S(1)} %get-tuple-element.16.source.rest_0_), channel_id=1, source_target_pairs={{0,7},{1,2},{2,11},{3,8},{4,9},{5,6},{6,10},{7,13},{8,5},{9,14},{1... | collective-permute-start | bytes 147464 | tf_op jit(solution)/shard_map/ppermute | solution.py:350
  4.8 5.8 %collective-permute-start.2 = (bf16[24,1024]{1,0:T(8,128)(2,1)S(1)}, bf16[24,1024]{1,0:T(8,128)(2,1)S(1)}, u32[]{:S(2)}, u32[]{:S(2)}) collective-permute-start(bf16[24,1024]{1,0:T(8,128)(2,1)S(1)} %get-tuple-element.16.source.rest_0_), channel_id=1, source_target_pairs={{0,11},{1,8},{2,15},{3,4},{4,13},{5,2},{6,14},{7,9},{8,0},{9,3},{1... | collective-permute-start | bytes 147464 | tf_op jit(solution)/shard_map/ppermute | solution.py:350
  5.9 4.7 %collective-permute-start.3 = (bf16[24,1024]{1,0:T(8,128)(2,1)S(1)}, bf16[24,1024]{1,0:T(8,128)(2,1)S(1)}, u32[]{:S(2)}, u32[]{:S(2)}) collective-permute-start(bf16[24,1024]{1,0:T(8,128)(2,1)S(1)} %get-tuple-element.16.source.rest_0_), channel_id=1, source_target_pairs={{0,5},{1,12},{2,7},{3,0},{4,11},{5,14},{6,1},{7,2},{8,13},{9,6},{1... | collective-permute-start | bytes 147464 | tf_op jit(solution)/shard_map/ppermute | solution.py:350
  7.5 4.3 %collective-permute-start = (bf16[24,1024]{1,0:T(8,128)(2,1)S(1)}, bf16[24,1024]{1,0:T(8,128)(2,1)S(1)}, u32[]{:S(2)}, u32[]{:S(2)}) collective-permute-start(bf16[24,1024]{1,0:T(8,128)(2,1)S(1)} %again.1), channel_id=1, source_target_pairs={{0,14},{1,15},{2,13},{3,12},{4,1},{5,0},{6,4},{7,5},{8,10},{9,11},... | collective-permute-start | bytes 147464 | tf_op jit(solution)/shard_map/ppermute | solution.py:350
  9.9 2.0 %collective-permute-start.4 = (bf16[24,1024]{1,0:T(8,128)(2,1)S(1)}, bf16[24,1024]{1,0:T(8,128)(2,1)S(1)}, u32[]{:S(2)}, u32[]{:S(2)}) collective-permute-start(bf16[24,1024]{1,0:T(8,128)(2,1)S(1)} %collective-permute-done.1.rest_2_), channel_id=1, source_target_pairs={{0,1},{1,0},{2,3},{3,2},{4,5},{5,4},{6,7},{7,6},{8,9},{9,8},{10,11... | collective-permute-start | bytes 147464 | tf_op jit(solution)/shard_map/ppermute | solution.py:367
  10.6 1.3 %collective-permute-start.5 = (bf16[24,1024]{1,0:T(8,128)(2,1)S(1)}, bf16[24,1024]{1,0:T(8,128)(2,1)S(1)}, u32[]{:S(2)}, u32[]{:S(2)}) collective-permute-start(bf16[24,1024]{1,0:T(8,128)(2,1)S(1)} %collective-permute-done.2.rest_3_), channel_id=1, source_target_pairs={{0,1},{1,0},{2,3},{3,2},{4,5},{5,4},{6,7},{7,6},{8,9},{9,8},{10,11... | collective-permute-start | bytes 147464 | tf_op jit(solution)/shard_map/ppermute | solution.py:367
  10.6 1.4 %collective-permute-start.6 = (bf16[24,1024]{1,0:T(8,128)(2,1)S(1)}, bf16[24,1024]{1,0:T(8,128)(2,1)S(1)}, u32[]{:S(2)}, u32[]{:S(2)}) collective-permute-start(bf16[24,1024]{1,0:T(8,128)(2,1)S(1)} %collective-permute-done.3.rest_4_), channel_id=1, source_target_pairs={{0,1},{1,0},{2,3},{3,2},{4,5},{5,4},{6,7},{7,6},{8,9},{9,8},{10,11... | collective-permute-start | bytes 147464 | tf_op jit(solution)/shard_map/ppermute | solution.py:367
  13.3 1.6 %collective-permute-start.7 = (bf16[128,1024]{1,0:T(8,128)(2,1)S(1)}, bf16[128,1024]{1,0:T(8,128)(2,1)S(1)}, u32[]{:S(2)}, u32[]{:S(2)}) collective-permute-start(bf16[128,1024]{1,0:T(8,128)(2,1)S(1)} %attention.1.own), channel_id=1, source_target_pairs={{0,1},{1,0},{2,3},{3,2},{4,5},{5,4},{6,7},{7,6},{8,9},{9,8},{10,11... | collective-permute-start | bytes 786440 | tf_op jit(solution)/shard_map/ppermute | solution.py:379

commit v9 on v8

--- a/solution.py
+++ b/solution.py
@@ -269,10 +269,10 @@
 
 
 SEARCHED_ROUNDS = [
-    (7, 2, 11, 8, 9, 6, 10, 13, 5, 14, 15, 0, 4, 3, 12, 1),
-    (11, 8, 15, 4, 13, 2, 14, 9, 0, 3, 7, 12, 1, 10, 6, 5),
+    (2, 7, 11, 8, 9, 6, 10, 13, 5, 14, 15, 0, 4, 3, 12, 1),
+    (8, 11, 15, 4, 13, 2, 14, 9, 0, 3, 7, 12, 10, 1, 6, 5),
     (5, 12, 7, 0, 11, 14, 1, 2, 13, 6, 4, 9, 8, 15, 3, 10),
-    (14, 15, 13, 12, 1, 0, 4, 5, 10, 11, 3, 2, 6, 7, 9, 8),
+    (14, 15, 13, 12, 0, 1, 4, 5, 10, 11, 3, 2, 6, 7, 9, 8),
 ]
 
 

time: 15.9 us -> 15.7 us (0.987)
  no operation moved by 1% of the time
where the time goes in v9:
time: 15.7 us; the launch traced here: 15.6 us
  starting transfers between devices  9.44 us (60%)
  Pallas kernels  4.14 us (26%)
  waiting for transfers between devices  1.89 us (12%)
    ppermute x4, starting transfers between devices, direct_body(): lax.ppermute(sent, ('tok', 'head'), list(enumerate(targets)))  8.54 us
    pallas_call x1, Pallas kernels, direct_body(): pl.pallas_call(functools.partial(attention_kernel, len(blocks)), out_shap...  1.3 us
    pallas_call x1, Pallas kernels, direct_body(): pl.pallas_call(anchor_kernel, out_shape=(jax.ShapeDtypeStruct((picks, wid...  1.28 us
    ppermute x1, waiting for transfers between devices, direct_body(): other = lax.ppermute(terms, 'head', [(0, 1), (1, 0)])  1.24 us
    pallas_call x1, Pallas kernels, direct_body(): pl.pallas_call(finish_kernel, out_shape=jax.ShapeDtypeStruct((cells, loca...  0.83 us
    pallas_call x1, Pallas kernels, direct_body(): pl.pallas_call(query_kernel, out_shape=(jax.ShapeDtypeStruct((heads // 2,...  0.72 us
    ppermute x4, waiting for transfers between devices, direct_body(): lax.ppermute(sent, ('tok', 'head'), list(enumerate(targets)))  0.64 us
    ppermute x3, starting transfers between devices, direct_body(): lax.ppermute(block, 'head', [(0, 1), (1, 0)])  0.54 us
  transfers between devices with their start and end apart: 8, of which 3 were waited for; matrix products, arithmetic and copies ran while one was open for 0% of the time, Pallas kernels for 5%

profile of v9, /device:TPU:0, one launch (start us, length us, event | category | flops | bytes accessed | tf_op | source)
XLA Modules:
  0.0 15.6 jit_solution(16449703269631512418)
XLA Ops:
  0.0 1.3 %anchors.1 = (bf16[24,1024]{1,0:T(8,128)(2,1)S(1)}, bf16[128,1024]{1,0:T(8,128)(2,1)S(1)}, f32[1,1024]{1,0:T(1,128)S(1)}, f32[4,256]{1,0:T(4,128)S(1)}) custom-call(s32[16]{0:T(128)} %refs_0_.1, s32[8]{0:T(128)} %refs_1_.1, bf16[128,1024]{1,0:T(8,128)(2,1)} %refs_2_.1, bf16[32,1024]{1,0:T(8,128)(2,1)} %refs_3_.1, f32[1,1024]{1,0:T(1,128)} %bitcast.2, ...), custom_call_target="tpu_custom_call" | custom-call | tf_op jit(solution)/shard_map/anchors/pallas_call | solution.py:308
  1.3 0.0 copy-start
  1.3 0.0 copy-start.1
  1.3 0.0 copy-start.2
  1.3 0.0 copy-start.3
  1.3 3.0 %collective-permute-start.1 = (bf16[24,1024]{1,0:T(8,128)(2,1)S(1)}, bf16[24,1024]{1,0:T(8,128)(2,1)S(1)}, u32[]{:S(2)}, u32[]{:S(2)}) collective-permute-start(bf16[24,1024]{1,0:T(8,128)(2,1)S(1)} %get-tuple-element.16.source.rest_0_), channel_id=1, source_target_pairs={{0,2},{1,7},{2,11},{3,8},{4,9},{5,6},{6,10},{7,13},{8,5},{9,14},{1... | collective-permute-start | bytes 147464 | tf_op jit(solution)/shard_map/ppermute | solution.py:350
  4.3 1.2 %collective-permute-start.2 = (bf16[24,1024]{1,0:T(8,128)(2,1)S(1)}, bf16[24,1024]{1,0:T(8,128)(2,1)S(1)}, u32[]{:S(2)}, u32[]{:S(2)}) collective-permute-start(bf16[24,1024]{1,0:T(8,128)(2,1)S(1)} %get-tuple-element.16.source.rest_0_), channel_id=1, source_target_pairs={{0,8},{1,11},{2,15},{3,4},{4,13},{5,2},{6,14},{7,9},{8,0},{9,3},{1... | collective-permute-start | bytes 147464 | tf_op jit(solution)/shard_map/ppermute | solution.py:350
  5.5 2.0 %collective-permute-start.3 = (bf16[24,1024]{1,0:T(8,128)(2,1)S(1)}, bf16[24,1024]{1,0:T(8,128)(2,1)S(1)}, u32[]{:S(2)}, u32[]{:S(2)}) collective-permute-start(bf16[24,1024]{1,0:T(8,128)(2,1)S(1)} %get-tuple-element.16.source.rest_0_), channel_id=1, source_target_pairs={{0,5},{1,12},{2,7},{3,0},{4,11},{5,14},{6,1},{7,2},{8,13},{9,6},{1... | collective-permute-start | bytes 147464 | tf_op jit(solution)/shard_map/ppermute | solution.py:350
  7.5 2.3 %collective-permute-start = (bf16[24,1024]{1,0:T(8,128)(2,1)S(1)}, bf16[24,1024]{1,0:T(8,128)(2,1)S(1)}, u32[]{:S(2)}, u32[]{:S(2)}) collective-permute-start(bf16[24,1024]{1,0:T(8,128)(2,1)S(1)} %again.1), channel_id=1, source_target_pairs={{0,14},{1,15},{2,13},{3,12},{4,0},{5,1},{6,4},{7,5},{8,10},{9,11},... | collective-permute-start | bytes 147464 | tf_op jit(solution)/shard_map/ppermute | solution.py:350
  9.9 0.0 collective-permute-done.1.rest_2_
  9.9 0.0 collective-permute-start.4
  9.9 0.5 %collective-permute-done.2.rest_3_ = bf16[24,1024]{1,0:T(8,128)(2,1)S(1)} collective-permute-done((bf16[24,1024]{1,0:T(8,128)(2,1)S(1)}, bf16[24,1024]{1,0:T(8,128)(2,1)S(1)}, u32[]{:S(2)}, u32[]{:S(2)}) %collective-permute-start.2) | collective-permute-done | bytes 49184 | tf_op jit(solution)/shard_map/ppermute | solution.py:350
  10.4 0.0 collective-permute-start.5
  10.4 0.0 collective-permute-done.3.rest_4_
  10.4 0.5 %collective-permute-start.6 = (bf16[24,1024]{1,0:T(8,128)(2,1)S(1)}, bf16[24,1024]{1,0:T(8,128)(2,1)S(1)}, u32[]{:S(2)}, u32[]{:S(2)}) collective-permute-start(bf16[24,1024]{1,0:T(8,128)(2,1)S(1)} %collective-permute-done.3.rest_4_), channel_id=1, source_target_pairs={{0,1},{1,0},{2,3},{3,2},{4,5},{5,4},{6,7},{7,6},{8,9},{9,8},{10,11... | collective-permute-start | bytes 147464 | tf_op jit(solution)/shard_map/ppermute | solution.py:367
  10.9 0.7 %queries.1 = (bf16[4,128,256]{2,1,0:T(8,128)(2,1)S(1)}, bf16[512,1024]{1,0:T(8,128)(2,1)S(1)}) custom-call(bf16[128,1024]{1,0:T(8,128)(2,1)S(1)} %get-tuple-element.11.vol, f32[1,1024]{1,0:T(1,128)S(1)} %get-tuple-element.12.gain, bf16[1024,512]{1,0:T(8,128)(2,1)S(1)} %copy-done.2, bf16[1024,512]{1,0:T(8,128)(2,1)S(1)} %copy-done.3, ...), custom_call_target="tpu_custom_call" | custom-call | flops 134217728 | bytes 4194304 | tf_op jit(solution)/shard_map/queries/pallas_call | solution.py:353
  11.6 0.2 %collective-permute-done.rest_1_ = bf16[24,1024]{1,0:T(8,128)(2,1)S(1)} collective-permute-done((bf16[24,1024]{1,0:T(8,128)(2,1)S(1)}, bf16[24,1024]{1,0:T(8,128)(2,1)S(1)}, u32[]{:S(2)}, u32[]{:S(2)}) %collective-permute-start) | collective-permute-done | bytes 49184 | tf_op jit(solution)/shard_map/ppermute | solution.py:350
  11.8 0.0 collective-permute-done.4.rest_5_
  11.8 0.0 collective-permute-done.5.rest_6_
  11.8 0.0 collective-permute-done.6.rest_7_
  11.8 1.3 %attention.1.own = bf16[128,1024]{1,0:T(8,128)(2,1)S(1)} custom-call(bf16[4,128,256]{2,1,0:T(8,128)(2,1)S(1)} %get-tuple-element.13.queries, f32[4,256]{1,0:T(4,128)S(1)} %get-tuple-element.14.multiplier, bf16[1024,512]{1,0:T(8,128)(2,1)S(1)} %copy-done, bf16[512,1024]{1,0:T(8,128)(2,1)S(1)} %get-tuple-element.15.value_turned, ...), custom_call_target="tpu_custom_call" | custom-call | tf_op jit(solution)/shard_map/attention/pallas_call | solution.py:369
  13.1 0.4 %collective-permute-start.7 = (bf16[128,1024]{1,0:T(8,128)(2,1)S(1)}, bf16[128,1024]{1,0:T(8,128)(2,1)S(1)}, u32[]{:S(2)}, u32[]{:S(2)}) collective-permute-start(bf16[128,1024]{1,0:T(8,128)(2,1)S(1)} %attention.1.own), channel_id=1, source_target_pairs={{0,1},{1,0},{2,3},{3,2},{4,5},{5,4},{6,7},{7,6},{8,9},{9,8},{10,11... | collective-permute-start | bytes 786440 | tf_op jit(solution)/shard_map/ppermute | solution.py:379
  13.5 1.2 %collective-permute-done.7.other = bf16[128,1024]{1,0:T(8,128)(2,1)S(1)} collective-permute-done((bf16[128,1024]{1,0:T(8,128)(2,1)S(1)}, bf16[128,1024]{1,0:T(8,128)(2,1)S(1)}, u32[]{:S(2)}, u32[]{:S(2)}) %collective-permute-start.7) | collective-permute-done | bytes 262176 | tf_op jit(solution)/shard_map/ppermute | solution.py:379
  14.7 0.8 %finish.1 = bf16[128,512]{1,0:T(8,128)(2,1)} custom-call(bf16[128,1024]{1,0:T(8,128)(2,1)S(1)} %attention.1.own, bf16[128,1024]{1,0:T(8,128)(2,1)S(1)} %collective-permute-done.7.other), custom_call_target="tpu_custom_call" | custom-call | tf_op jit(solution)/shard_map/finish/pallas_call | solution.py:380
  (5 shorter events, 0.0 us)
Async XLA Ops:
  1.3 9.6 %copy-start = (bf16[1024,512]{1,0:T(8,128)(2,1)S(1)}, bf16[1024,512]{1,0:T(8,128)(2,1)}, u32[]{:S(2)}) copy-start(bf16[1024,512]{1,0:T(8,128)(2,1)} %lookup.3) | copy-start | bytes 3145732
  1.3 9.6 %copy-start.1 = (bf16[512,1024]{1,0:T(8,128)(2,1)S(1)}, bf16[512,1024]{1,0:T(8,128)(2,1)}, u32[]{:S(2)}) copy-start(bf16[512,1024]{1,0:T(8,128)(2,1)} %final.3) | copy-start | bytes 3145732
  1.3 9.6 %copy-start.2 = (bf16[1024,512]{1,0:T(8,128)(2,1)S(1)}, bf16[1024,512]{1,0:T(8,128)(2,1)}, u32[]{:S(2)}) copy-start(bf16[1024,512]{1,0:T(8,128)(2,1)} %projection.1) | copy-start | bytes 3145732
  1.3 9.6 %copy-start.3 = (bf16[1024,512]{1,0:T(8,128)(2,1)S(1)}, bf16[1024,512]{1,0:T(8,128)(2,1)}, u32[]{:S(2)}) copy-start(bf16[1024,512]{1,0:T(8,128)(2,1)} %value_projection.1) | copy-start | bytes 3145732
  1.3 8.6 %collective-permute-start.1 = (bf16[24,1024]{1,0:T(8,128)(2,1)S(1)}, bf16[24,1024]{1,0:T(8,128)(2,1)S(1)}, u32[]{:S(2)}, u32[]{:S(2)}) collective-permute-start(bf16[24,1024]{1,0:T(8,128)(2,1)S(1)} %get-tuple-element.16.source.rest_0_), channel_id=1, source_target_pairs={{0,2},{1,7},{2,11},{3,8},{4,9},{5,6},{6,10},{7,13},{8,5},{9,14},{1... | collective-permute-start | bytes 147464 | tf_op jit(solution)/shard_map/ppermute | solution.py:350
  4.3 6.0 %collective-permute-start.2 = (bf16[24,1024]{1,0:T(8,128)(2,1)S(1)}, bf16[24,1024]{1,0:T(8,128)(2,1)S(1)}, u32[]{:S(2)}, u32[]{:S(2)}) collective-permute-start(bf16[24,1024]{1,0:T(8,128)(2,1)S(1)} %get-tuple-element.16.source.rest_0_), channel_id=1, source_target_pairs={{0,8},{1,11},{2,15},{3,4},{4,13},{5,2},{6,14},{7,9},{8,0},{9,3},{1... | collective-permute-start | bytes 147464 | tf_op jit(solution)/shard_map/ppermute | solution.py:350
  5.5 4.9 %collective-permute-start.3 = (bf16[24,1024]{1,0:T(8,128)(2,1)S(1)}, bf16[24,1024]{1,0:T(8,128)(2,1)S(1)}, u32[]{:S(2)}, u32[]{:S(2)}) collective-permute-start(bf16[24,1024]{1,0:T(8,128)(2,1)S(1)} %get-tuple-element.16.source.rest_0_), channel_id=1, source_target_pairs={{0,5},{1,12},{2,7},{3,0},{4,11},{5,14},{6,1},{7,2},{8,13},{9,6},{1... | collective-permute-start | bytes 147464 | tf_op jit(solution)/shard_map/ppermute | solution.py:350
  7.5 4.3 %collective-permute-start = (bf16[24,1024]{1,0:T(8,128)(2,1)S(1)}, bf16[24,1024]{1,0:T(8,128)(2,1)S(1)}, u32[]{:S(2)}, u32[]{:S(2)}) collective-permute-start(bf16[24,1024]{1,0:T(8,128)(2,1)S(1)} %again.1), channel_id=1, source_target_pairs={{0,14},{1,15},{2,13},{3,12},{4,0},{5,1},{6,4},{7,5},{8,10},{9,11},... | collective-permute-start | bytes 147464 | tf_op jit(solution)/shard_map/ppermute | solution.py:350
  9.9 1.9 %collective-permute-start.4 = (bf16[24,1024]{1,0:T(8,128)(2,1)S(1)}, bf16[24,1024]{1,0:T(8,128)(2,1)S(1)}, u32[]{:S(2)}, u32[]{:S(2)}) collective-permute-start(bf16[24,1024]{1,0:T(8,128)(2,1)S(1)} %collective-permute-done.1.rest_2_), channel_id=1, source_target_pairs={{0,1},{1,0},{2,3},{3,2},{4,5},{5,4},{6,7},{7,6},{8,9},{9,8},{10,11... | collective-permute-start | bytes 147464 | tf_op jit(solution)/shard_map/ppermute | solution.py:367
  10.4 1.5 %collective-permute-start.5 = (bf16[24,1024]{1,0:T(8,128)(2,1)S(1)}, bf16[24,1024]{1,0:T(8,128)(2,1)S(1)}, u32[]{:S(2)}, u32[]{:S(2)}) collective-permute-start(bf16[24,1024]{1,0:T(8,128)(2,1)S(1)} %collective-permute-done.2.rest_3_), channel_id=1, source_target_pairs={{0,1},{1,0},{2,3},{3,2},{4,5},{5,4},{6,7},{7,6},{8,9},{9,8},{10,11... | collective-permute-start | bytes 147464 | tf_op jit(solution)/shard_map/ppermute | solution.py:367
  10.4 1.4 %collective-permute-start.6 = (bf16[24,1024]{1,0:T(8,128)(2,1)S(1)}, bf16[24,1024]{1,0:T(8,128)(2,1)S(1)}, u32[]{:S(2)}, u32[]{:S(2)}) collective-permute-start(bf16[24,1024]{1,0:T(8,128)(2,1)S(1)} %collective-permute-done.3.rest_4_), channel_id=1, source_target_pairs={{0,1},{1,0},{2,3},{3,2},{4,5},{5,4},{6,7},{7,6},{8,9},{9,8},{10,11... | collective-permute-start | bytes 147464 | tf_op jit(solution)/shard_map/ppermute | solution.py:367
  13.1 1.6 %collective-permute-start.7 = (bf16[128,1024]{1,0:T(8,128)(2,1)S(1)}, bf16[128,1024]{1,0:T(8,128)(2,1)S(1)}, u32[]{:S(2)}, u32[]{:S(2)}) collective-permute-start(bf16[128,1024]{1,0:T(8,128)(2,1)S(1)} %attention.1.own), channel_id=1, source_target_pairs={{0,1},{1,0},{2,3},{3,2},{4,5},{5,4},{6,7},{7,6},{8,9},{9,8},{10,11... | collective-permute-start | bytes 786440 | tf_op jit(solution)/shard_map/ppermute | solution.py:379

commit v10 on v9

--- a/solution.py
+++ b/solution.py
@@ -271,7 +271,7 @@
 SEARCHED_ROUNDS = [
     (2, 7, 11, 8, 9, 6, 10, 13, 5, 14, 15, 0, 4, 3, 12, 1),
     (8, 11, 15, 4, 13, 2, 14, 9, 0, 3, 7, 12, 10, 1, 6, 5),
-    (5, 12, 7, 0, 11, 14, 1, 2, 13, 6, 4, 9, 8, 15, 3, 10),
+    (5, 12, 7, 0, 11, 14, 1, 2, 13, 6, 4, 9, 15, 8, 3, 10),
     (14, 15, 13, 12, 0, 1, 4, 5, 10, 11, 3, 2, 6, 7, 9, 8),
 ]
 

time: 15.7 us -> 15.7 us (level)
  no operation moved by 1% of the time
where the time goes in v10:
time: 15.7 us; the launch traced here: 15.6 us
  starting transfers between devices  9.44 us (60%)
  Pallas kernels  4.14 us (26%)
  waiting for transfers between devices  1.89 us (12%)
    ppermute x4, starting transfers between devices, direct_body(): lax.ppermute(sent, ('tok', 'head'), list(enumerate(targets)))  8.54 us
    pallas_call x1, Pallas kernels, direct_body(): pl.pallas_call(functools.partial(attention_kernel, len(blocks)), out_shap...  1.3 us
    pallas_call x1, Pallas kernels, direct_body(): pl.pallas_call(anchor_kernel, out_shape=(jax.ShapeDtypeStruct((picks, wid...  1.28 us
    ppermute x1, waiting for transfers between devices, direct_body(): other = lax.ppermute(terms, 'head', [(0, 1), (1, 0)])  1.24 us
    pallas_call x1, Pallas kernels, direct_body(): pl.pallas_call(finish_kernel, out_shape=jax.ShapeDtypeStruct((cells, loca...  0.83 us
    pallas_call x1, Pallas kernels, direct_body(): pl.pallas_call(query_kernel, out_shape=(jax.ShapeDtypeStruct((heads // 2,...  0.72 us
    ppermute x4, waiting for transfers between devices, direct_body(): lax.ppermute(sent, ('tok', 'head'), list(enumerate(targets)))  0.64 us
    ppermute x3, starting transfers between devices, direct_body(): lax.ppermute(block, 'head', [(0, 1), (1, 0)])  0.54 us
  transfers between devices with their start and end apart: 8, of which 3 were waited for; matrix products, arithmetic and copies ran while one was open for 0% of the time, Pallas kernels for 5%

profile of v10, /device:TPU:0, one launch (start us, length us, event | category | flops | bytes accessed | tf_op | source)
XLA Modules:
  0.0 15.6 jit_solution(17600965841621633980)
XLA Ops:
  0.0 1.3 %anchors.1 = (bf16[24,1024]{1,0:T(8,128)(2,1)S(1)}, bf16[128,1024]{1,0:T(8,128)(2,1)S(1)}, f32[1,1024]{1,0:T(1,128)S(1)}, f32[4,256]{1,0:T(4,128)S(1)}) custom-call(s32[16]{0:T(128)} %refs_0_.1, s32[8]{0:T(128)} %refs_1_.1, bf16[128,1024]{1,0:T(8,128)(2,1)} %refs_2_.1, bf16[32,1024]{1,0:T(8,128)(2,1)} %refs_3_.1, f32[1,1024]{1,0:T(1,128)} %bitcast.2, ...), custom_call_target="tpu_custom_call" | custom-call | tf_op jit(solution)/shard_map/anchors/pallas_call | solution.py:308
  1.3 0.0 copy-start
  1.3 0.0 copy-start.1
  1.3 0.0 copy-start.2
  1.3 0.0 copy-start.3
  1.3 3.0 %collective-permute-start.1 = (bf16[24,1024]{1,0:T(8,128)(2,1)S(1)}, bf16[24,1024]{1,0:T(8,128)(2,1)S(1)}, u32[]{:S(2)}, u32[]{:S(2)}) collective-permute-start(bf16[24,1024]{1,0:T(8,128)(2,1)S(1)} %get-tuple-element.16.source.rest_0_), channel_id=1, source_target_pairs={{0,2},{1,7},{2,11},{3,8},{4,9},{5,6},{6,10},{7,13},{8,5},{9,14},{1... | collective-permute-start | bytes 147464 | tf_op jit(solution)/shard_map/ppermute | solution.py:350
  4.3 1.2 %collective-permute-start.2 = (bf16[24,1024]{1,0:T(8,128)(2,1)S(1)}, bf16[24,1024]{1,0:T(8,128)(2,1)S(1)}, u32[]{:S(2)}, u32[]{:S(2)}) collective-permute-start(bf16[24,1024]{1,0:T(8,128)(2,1)S(1)} %get-tuple-element.16.source.rest_0_), channel_id=1, source_target_pairs={{0,8},{1,11},{2,15},{3,4},{4,13},{5,2},{6,14},{7,9},{8,0},{9,3},{1... | collective-permute-start | bytes 147464 | tf_op jit(solution)/shard_map/ppermute | solution.py:350
  5.5 2.0 %collective-permute-start.3 = (bf16[24,1024]{1,0:T(8,128)(2,1)S(1)}, bf16[24,1024]{1,0:T(8,128)(2,1)S(1)}, u32[]{:S(2)}, u32[]{:S(2)}) collective-permute-start(bf16[24,1024]{1,0:T(8,128)(2,1)S(1)} %get-tuple-element.16.source.rest_0_), channel_id=1, source_target_pairs={{0,5},{1,12},{2,7},{3,0},{4,11},{5,14},{6,1},{7,2},{8,13},{9,6},{1... | collective-permute-start | bytes 147464 | tf_op jit(solution)/shard_map/ppermute | solution.py:350
  7.5 2.3 %collective-permute-start = (bf16[24,1024]{1,0:T(8,128)(2,1)S(1)}, bf16[24,1024]{1,0:T(8,128)(2,1)S(1)}, u32[]{:S(2)}, u32[]{:S(2)}) collective-permute-start(bf16[24,1024]{1,0:T(8,128)(2,1)S(1)} %again.1), channel_id=1, source_target_pairs={{0,14},{1,15},{2,13},{3,12},{4,0},{5,1},{6,4},{7,5},{8,10},{9,11},... | collective-permute-start | bytes 147464 | tf_op jit(solution)/shard_map/ppermute | solution.py:350
  9.9 0.0 collective-permute-done.1.rest_2_
  9.9 0.0 collective-permute-start.4
  9.9 0.5 %collective-permute-done.2.rest_3_ = bf16[24,1024]{1,0:T(8,128)(2,1)S(1)} collective-permute-done((bf16[24,1024]{1,0:T(8,128)(2,1)S(1)}, bf16[24,1024]{1,0:T(8,128)(2,1)S(1)}, u32[]{:S(2)}, u32[]{:S(2)}) %collective-permute-start.2) | collective-permute-done | bytes 49184 | tf_op jit(solution)/shard_map/ppermute | solution.py:350
  10.4 0.0 collective-permute-start.5
  10.4 0.0 collective-permute-done.3.rest_4_
  10.4 0.5 %collective-permute-start.6 = (bf16[24,1024]{1,0:T(8,128)(2,1)S(1)}, bf16[24,1024]{1,0:T(8,128)(2,1)S(1)}, u32[]{:S(2)}, u32[]{:S(2)}) collective-permute-start(bf16[24,1024]{1,0:T(8,128)(2,1)S(1)} %collective-permute-done.3.rest_4_), channel_id=1, source_target_pairs={{0,1},{1,0},{2,3},{3,2},{4,5},{5,4},{6,7},{7,6},{8,9},{9,8},{10,11... | collective-permute-start | bytes 147464 | tf_op jit(solution)/shard_map/ppermute | solution.py:367
  10.9 0.7 %queries.1 = (bf16[4,128,256]{2,1,0:T(8,128)(2,1)S(1)}, bf16[512,1024]{1,0:T(8,128)(2,1)S(1)}) custom-call(bf16[128,1024]{1,0:T(8,128)(2,1)S(1)} %get-tuple-element.11.vol, f32[1,1024]{1,0:T(1,128)S(1)} %get-tuple-element.12.gain, bf16[1024,512]{1,0:T(8,128)(2,1)S(1)} %copy-done.2, bf16[1024,512]{1,0:T(8,128)(2,1)S(1)} %copy-done.3, ...), custom_call_target="tpu_custom_call" | custom-call | flops 134217728 | bytes 4194304 | tf_op jit(solution)/shard_map/queries/pallas_call | solution.py:353
  11.6 0.2 %collective-permute-done.rest_1_ = bf16[24,1024]{1,0:T(8,128)(2,1)S(1)} collective-permute-done((bf16[24,1024]{1,0:T(8,128)(2,1)S(1)}, bf16[24,1024]{1,0:T(8,128)(2,1)S(1)}, u32[]{:S(2)}, u32[]{:S(2)}) %collective-permute-start) | collective-permute-done | bytes 49184 | tf_op jit(solution)/shard_map/ppermute | solution.py:350
  11.8 0.0 collective-permute-done.4.rest_5_
  11.8 0.0 collective-permute-done.5.rest_6_
  11.8 0.0 collective-permute-done.6.rest_7_
  11.8 1.3 %attention.1.own = bf16[128,1024]{1,0:T(8,128)(2,1)S(1)} custom-call(bf16[4,128,256]{2,1,0:T(8,128)(2,1)S(1)} %get-tuple-element.13.queries, f32[4,256]{1,0:T(4,128)S(1)} %get-tuple-element.14.multiplier, bf16[1024,512]{1,0:T(8,128)(2,1)S(1)} %copy-done, bf16[512,1024]{1,0:T(8,128)(2,1)S(1)} %get-tuple-element.15.value_turned, ...), custom_call_target="tpu_custom_call" | custom-call | tf_op jit(solution)/shard_map/attention/pallas_call | solution.py:369
  13.1 0.4 %collective-permute-start.7 = (bf16[128,1024]{1,0:T(8,128)(2,1)S(1)}, bf16[128,1024]{1,0:T(8,128)(2,1)S(1)}, u32[]{:S(2)}, u32[]{:S(2)}) collective-permute-start(bf16[128,1024]{1,0:T(8,128)(2,1)S(1)} %attention.1.own), channel_id=1, source_target_pairs={{0,1},{1,0},{2,3},{3,2},{4,5},{5,4},{6,7},{7,6},{8,9},{9,8},{10,11... | collective-permute-start | bytes 786440 | tf_op jit(solution)/shard_map/ppermute | solution.py:379
  13.5 1.2 %collective-permute-done.7.other = bf16[128,1024]{1,0:T(8,128)(2,1)S(1)} collective-permute-done((bf16[128,1024]{1,0:T(8,128)(2,1)S(1)}, bf16[128,1024]{1,0:T(8,128)(2,1)S(1)}, u32[]{:S(2)}, u32[]{:S(2)}) %collective-permute-start.7) | collective-permute-done | bytes 262176 | tf_op jit(solution)/shard_map/ppermute | solution.py:379
  14.7 0.8 %finish.1 = bf16[128,512]{1,0:T(8,128)(2,1)} custom-call(bf16[128,1024]{1,0:T(8,128)(2,1)S(1)} %attention.1.own, bf16[128,1024]{1,0:T(8,128)(2,1)S(1)} %collective-permute-done.7.other), custom_call_target="tpu_custom_call" | custom-call | tf_op jit(solution)/shard_map/finish/pallas_call | solution.py:380
  (5 shorter events, 0.0 us)
Async XLA Ops:
  1.3 9.6 %copy-start = (bf16[1024,512]{1,0:T(8,128)(2,1)S(1)}, bf16[1024,512]{1,0:T(8,128)(2,1)}, u32[]{:S(2)}) copy-start(bf16[1024,512]{1,0:T(8,128)(2,1)} %lookup.3) | copy-start | bytes 3145732
  1.3 9.6 %copy-start.1 = (bf16[512,1024]{1,0:T(8,128)(2,1)S(1)}, bf16[512,1024]{1,0:T(8,128)(2,1)}, u32[]{:S(2)}) copy-start(bf16[512,1024]{1,0:T(8,128)(2,1)} %final.3) | copy-start | bytes 3145732
  1.3 9.6 %copy-start.2 = (bf16[1024,512]{1,0:T(8,128)(2,1)S(1)}, bf16[1024,512]{1,0:T(8,128)(2,1)}, u32[]{:S(2)}) copy-start(bf16[1024,512]{1,0:T(8,128)(2,1)} %projection.1) | copy-start | bytes 3145732
  1.3 9.6 %copy-start.3 = (bf16[1024,512]{1,0:T(8,128)(2,1)S(1)}, bf16[1024,512]{1,0:T(8,128)(2,1)}, u32[]{:S(2)}) copy-start(bf16[1024,512]{1,0:T(8,128)(2,1)} %value_projection.1) | copy-start | bytes 3145732
  1.3 8.6 %collective-permute-start.1 = (bf16[24,1024]{1,0:T(8,128)(2,1)S(1)}, bf16[24,1024]{1,0:T(8,128)(2,1)S(1)}, u32[]{:S(2)}, u32[]{:S(2)}) collective-permute-start(bf16[24,1024]{1,0:T(8,128)(2,1)S(1)} %get-tuple-element.16.source.rest_0_), channel_id=1, source_target_pairs={{0,2},{1,7},{2,11},{3,8},{4,9},{5,6},{6,10},{7,13},{8,5},{9,14},{1... | collective-permute-start | bytes 147464 | tf_op jit(solution)/shard_map/ppermute | solution.py:350
  4.3 6.0 %collective-permute-start.2 = (bf16[24,1024]{1,0:T(8,128)(2,1)S(1)}, bf16[24,1024]{1,0:T(8,128)(2,1)S(1)}, u32[]{:S(2)}, u32[]{:S(2)}) collective-permute-start(bf16[24,1024]{1,0:T(8,128)(2,1)S(1)} %get-tuple-element.16.source.rest_0_), channel_id=1, source_target_pairs={{0,8},{1,11},{2,15},{3,4},{4,13},{5,2},{6,14},{7,9},{8,0},{9,3},{1... | collective-permute-start | bytes 147464 | tf_op jit(solution)/shard_map/ppermute | solution.py:350
  5.5 4.9 %collective-permute-start.3 = (bf16[24,1024]{1,0:T(8,128)(2,1)S(1)}, bf16[24,1024]{1,0:T(8,128)(2,1)S(1)}, u32[]{:S(2)}, u32[]{:S(2)}) collective-permute-start(bf16[24,1024]{1,0:T(8,128)(2,1)S(1)} %get-tuple-element.16.source.rest_0_), channel_id=1, source_target_pairs={{0,5},{1,12},{2,7},{3,0},{4,11},{5,14},{6,1},{7,2},{8,13},{9,6},{1... | collective-permute-start | bytes 147464 | tf_op jit(solution)/shard_map/ppermute | solution.py:350
  7.5 4.3 %collective-permute-start = (bf16[24,1024]{1,0:T(8,128)(2,1)S(1)}, bf16[24,1024]{1,0:T(8,128)(2,1)S(1)}, u32[]{:S(2)}, u32[]{:S(2)}) collective-permute-start(bf16[24,1024]{1,0:T(8,128)(2,1)S(1)} %again.1), channel_id=1, source_target_pairs={{0,14},{1,15},{2,13},{3,12},{4,0},{5,1},{6,4},{7,5},{8,10},{9,11},... | collective-permute-start | bytes 147464 | tf_op jit(solution)/shard_map/ppermute | solution.py:350
  9.9 1.9 %collective-permute-start.4 = (bf16[24,1024]{1,0:T(8,128)(2,1)S(1)}, bf16[24,1024]{1,0:T(8,128)(2,1)S(1)}, u32[]{:S(2)}, u32[]{:S(2)}) collective-permute-start(bf16[24,1024]{1,0:T(8,128)(2,1)S(1)} %collective-permute-done.1.rest_2_), channel_id=1, source_target_pairs={{0,1},{1,0},{2,3},{3,2},{4,5},{5,4},{6,7},{7,6},{8,9},{9,8},{10,11... | collective-permute-start | bytes 147464 | tf_op jit(solution)/shard_map/ppermute | solution.py:367
  10.4 1.5 %collective-permute-start.5 = (bf16[24,1024]{1,0:T(8,128)(2,1)S(1)}, bf16[24,1024]{1,0:T(8,128)(2,1)S(1)}, u32[]{:S(2)}, u32[]{:S(2)}) collective-permute-start(bf16[24,1024]{1,0:T(8,128)(2,1)S(1)} %collective-permute-done.2.rest_3_), channel_id=1, source_target_pairs={{0,1},{1,0},{2,3},{3,2},{4,5},{5,4},{6,7},{7,6},{8,9},{9,8},{10,11... | collective-permute-start | bytes 147464 | tf_op jit(solution)/shard_map/ppermute | solution.py:367
  10.4 1.4 %collective-permute-start.6 = (bf16[24,1024]{1,0:T(8,128)(2,1)S(1)}, bf16[24,1024]{1,0:T(8,128)(2,1)S(1)}, u32[]{:S(2)}, u32[]{:S(2)}) collective-permute-start(bf16[24,1024]{1,0:T(8,128)(2,1)S(1)} %collective-permute-done.3.rest_4_), channel_id=1, source_target_pairs={{0,1},{1,0},{2,3},{3,2},{4,5},{5,4},{6,7},{7,6},{8,9},{9,8},{10,11... | collective-permute-start | bytes 147464 | tf_op jit(solution)/shard_map/ppermute | solution.py:367
  13.1 1.6 %collective-permute-start.7 = (bf16[128,1024]{1,0:T(8,128)(2,1)S(1)}, bf16[128,1024]{1,0:T(8,128)(2,1)S(1)}, u32[]{:S(2)}, u32[]{:S(2)}) collective-permute-start(bf16[128,1024]{1,0:T(8,128)(2,1)S(1)} %attention.1.own), channel_id=1, source_target_pairs={{0,1},{1,0},{2,3},{3,2},{4,5},{5,4},{6,7},{7,6},{8,9},{9,8},{10,11... | collective-permute-start | bytes 786440 | tf_op jit(solution)/shard_map/ppermute | solution.py:379

commit v11 on v10

--- a/solution.py
+++ b/solution.py
@@ -183,7 +183,7 @@
 def anchor_kernel(*refs):
     sources, (anchors, vol, vol_gain, multiplier), rest = refs[:7], refs[7:11], refs[11:]
     vol_position, surf_position, surf, surf_gain, divisor, semaphores = rest
-    targets = (vol_position, surf_position, vol, surf, vol_gain, surf_gain, divisor)
+    targets = (vol, surf, vol_position, surf_position, vol_gain, surf_gain, divisor)
     for copy in fetch(sources, targets, semaphores):
         copy.wait()
     block_index = lax.axis_index("tok")
@@ -327,10 +327,10 @@
         name="anchors",
     )(
         *in_hbm(
+            interior_element_embedding,
+            boundary_element_embedding,
             interior_landmark_position,
             boundary_landmark_position,
-            interior_element_embedding,
-            boundary_element_embedding,
             interior_rescaling_factor.reshape(1, width),
             boundary_rescaling_factor.reshape(1, width),
             channel_logit_divisor,

time: 15.7 us -> 15.7 us (level)
  no operation moved by 1% of the time
where the time goes in v11:
time: 15.7 us; the launch traced here: 15.6 us
  starting transfers between devices  9.44 us (60%)
  Pallas kernels  4.16 us (26%)
  waiting for transfers between devices  1.89 us (12%)
    ppermute x4, starting transfers between devices, direct_body(): lax.ppermute(sent, ('tok', 'head'), list(enumerate(targets)))  8.54 us
    pallas_call x1, Pallas kernels, direct_body(): pl.pallas_call(functools.partial(attention_kernel, len(blocks)), out_shap...  1.31 us
    pallas_call x1, Pallas kernels, direct_body(): pl.pallas_call(anchor_kernel, out_shape=(jax.ShapeDtypeStruct((picks, wid...  1.29 us
    ppermute x1, waiting for transfers between devices, direct_body(): other = lax.ppermute(terms, 'head', [(0, 1), (1, 0)])  1.24 us
    pallas_call x1, Pallas kernels, direct_body(): pl.pallas_call(finish_kernel, out_shape=jax.ShapeDtypeStruct((cells, loca...  0.83 us
    pallas_call x1, Pallas kernels, direct_body(): pl.pallas_call(query_kernel, out_shape=(jax.ShapeDtypeStruct((heads // 2,...  0.72 us
    ppermute x4, waiting for transfers between devices, direct_body(): lax.ppermute(sent, ('tok', 'head'), list(enumerate(targets)))  0.64 us
    ppermute x3, starting transfers between devices, direct_body(): lax.ppermute(block, 'head', [(0, 1), (1, 0)])  0.54 us
  transfers between devices with their start and end apart: 8, of which 3 were waited for; matrix products, arithmetic and copies ran while one was open for 0% of the time, Pallas kernels for 5%

profile of v11, /device:TPU:0, one launch (start us, length us, event | category | flops | bytes accessed | tf_op | source)
XLA Modules:
  0.0 15.6 jit_solution(17586391704684172447)
XLA Ops:
  0.0 1.3 %anchors.1 = (bf16[24,1024]{1,0:T(8,128)(2,1)S(1)}, bf16[128,1024]{1,0:T(8,128)(2,1)S(1)}, f32[1,1024]{1,0:T(1,128)S(1)}, f32[4,256]{1,0:T(4,128)S(1)}) custom-call(bf16[128,1024]{1,0:T(8,128)(2,1)} %refs_0_.1, bf16[32,1024]{1,0:T(8,128)(2,1)} %refs_1_.1, s32[16]{0:T(128)} %refs_2_.1, s32[8]{0:T(128)} %refs_3_.1, f32[1,1024]{1,0:T(1,128)} %bitcast.2, ...), custom_call_target="tpu_custom_call" | custom-call | tf_op jit(solution)/shard_map/anchors/pallas_call | solution.py:308
  1.3 0.0 copy-start
  1.3 0.0 copy-start.1
  1.3 0.0 copy-start.2
  1.3 0.0 copy-start.3
  1.4 3.0 %collective-permute-start.1 = (bf16[24,1024]{1,0:T(8,128)(2,1)S(1)}, bf16[24,1024]{1,0:T(8,128)(2,1)S(1)}, u32[]{:S(2)}, u32[]{:S(2)}) collective-permute-start(bf16[24,1024]{1,0:T(8,128)(2,1)S(1)} %get-tuple-element.16.source.rest_0_), channel_id=1, source_target_pairs={{0,2},{1,7},{2,11},{3,8},{4,9},{5,6},{6,10},{7,13},{8,5},{9,14},{1... | collective-permute-start | bytes 147464 | tf_op jit(solution)/shard_map/ppermute | solution.py:350
  4.4 1.2 %collective-permute-start.2 = (bf16[24,1024]{1,0:T(8,128)(2,1)S(1)}, bf16[24,1024]{1,0:T(8,128)(2,1)S(1)}, u32[]{:S(2)}, u32[]{:S(2)}) collective-permute-start(bf16[24,1024]{1,0:T(8,128)(2,1)S(1)} %get-tuple-element.16.source.rest_0_), channel_id=1, source_target_pairs={{0,8},{1,11},{2,15},{3,4},{4,13},{5,2},{6,14},{7,9},{8,0},{9,3},{1... | collective-permute-start | bytes 147464 | tf_op jit(solution)/shard_map/ppermute | solution.py:350
  5.5 2.0 %collective-permute-start.3 = (bf16[24,1024]{1,0:T(8,128)(2,1)S(1)}, bf16[24,1024]{1,0:T(8,128)(2,1)S(1)}, u32[]{:S(2)}, u32[]{:S(2)}) collective-permute-start(bf16[24,1024]{1,0:T(8,128)(2,1)S(1)} %get-tuple-element.16.source.rest_0_), channel_id=1, source_target_pairs={{0,5},{1,12},{2,7},{3,0},{4,11},{5,14},{6,1},{7,2},{8,13},{9,6},{1... | collective-permute-start | bytes 147464 | tf_op jit(solution)/shard_map/ppermute | solution.py:350
  7.6 2.3 %collective-permute-start = (bf16[24,1024]{1,0:T(8,128)(2,1)S(1)}, bf16[24,1024]{1,0:T(8,128)(2,1)S(1)}, u32[]{:S(2)}, u32[]{:S(2)}) collective-permute-start(bf16[24,1024]{1,0:T(8,128)(2,1)S(1)} %again.1), channel_id=1, source_target_pairs={{0,14},{1,15},{2,13},{3,12},{4,0},{5,1},{6,4},{7,5},{8,10},{9,11},... | collective-permute-start | bytes 147464 | tf_op jit(solution)/shard_map/ppermute | solution.py:350
  9.9 0.0 collective-permute-done.1.rest_2_
  9.9 0.0 collective-permute-start.4
  9.9 0.5 %collective-permute-done.2.rest_3_ = bf16[24,1024]{1,0:T(8,128)(2,1)S(1)} collective-permute-done((bf16[24,1024]{1,0:T(8,128)(2,1)S(1)}, bf16[24,1024]{1,0:T(8,128)(2,1)S(1)}, u32[]{:S(2)}, u32[]{:S(2)}) %collective-permute-start.2) | collective-permute-done | bytes 49184 | tf_op jit(solution)/shard_map/ppermute | solution.py:350
  10.4 0.0 collective-permute-start.5
  10.4 0.0 collective-permute-done.3.rest_4_
  10.4 0.5 %collective-permute-start.6 = (bf16[24,1024]{1,0:T(8,128)(2,1)S(1)}, bf16[24,1024]{1,0:T(8,128)(2,1)S(1)}, u32[]{:S(2)}, u32[]{:S(2)}) collective-permute-start(bf16[24,1024]{1,0:T(8,128)(2,1)S(1)} %collective-permute-done.3.rest_4_), channel_id=1, source_target_pairs={{0,1},{1,0},{2,3},{3,2},{4,5},{5,4},{6,7},{7,6},{8,9},{9,8},{10,11... | collective-permute-start | bytes 147464 | tf_op jit(solution)/shard_map/ppermute | solution.py:367
  10.9 0.7 %queries.1 = (bf16[4,128,256]{2,1,0:T(8,128)(2,1)S(1)}, bf16[512,1024]{1,0:T(8,128)(2,1)S(1)}) custom-call(bf16[128,1024]{1,0:T(8,128)(2,1)S(1)} %get-tuple-element.11.vol, f32[1,1024]{1,0:T(1,128)S(1)} %get-tuple-element.12.gain, bf16[1024,512]{1,0:T(8,128)(2,1)S(1)} %copy-done.2, bf16[1024,512]{1,0:T(8,128)(2,1)S(1)} %copy-done.3, ...), custom_call_target="tpu_custom_call" | custom-call | flops 134217728 | bytes 4194304 | tf_op jit(solution)/shard_map/queries/pallas_call | solution.py:353
  11.7 0.2 %collective-permute-done.rest_1_ = bf16[24,1024]{1,0:T(8,128)(2,1)S(1)} collective-permute-done((bf16[24,1024]{1,0:T(8,128)(2,1)S(1)}, bf16[24,1024]{1,0:T(8,128)(2,1)S(1)}, u32[]{:S(2)}, u32[]{:S(2)}) %collective-permute-start) | collective-permute-done | bytes 49184 | tf_op jit(solution)/shard_map/ppermute | solution.py:350
  11.8 0.0 collective-permute-done.4.rest_5_
  11.8 0.0 collective-permute-done.5.rest_6_
  11.8 0.0 collective-permute-done.6.rest_7_
  11.8 1.3 %attention.1.own = bf16[128,1024]{1,0:T(8,128)(2,1)S(1)} custom-call(bf16[4,128,256]{2,1,0:T(8,128)(2,1)S(1)} %get-tuple-element.13.queries, f32[4,256]{1,0:T(4,128)S(1)} %get-tuple-element.14.multiplier, bf16[1024,512]{1,0:T(8,128)(2,1)S(1)} %copy-done, bf16[512,1024]{1,0:T(8,128)(2,1)S(1)} %get-tuple-element.15.value_turned, ...), custom_call_target="tpu_custom_call" | custom-call | tf_op jit(solution)/shard_map/attention/pallas_call | solution.py:369
  13.1 0.4 %collective-permute-start.7 = (bf16[128,1024]{1,0:T(8,128)(2,1)S(1)}, bf16[128,1024]{1,0:T(8,128)(2,1)S(1)}, u32[]{:S(2)}, u32[]{:S(2)}) collective-permute-start(bf16[128,1024]{1,0:T(8,128)(2,1)S(1)} %attention.1.own), channel_id=1, source_target_pairs={{0,1},{1,0},{2,3},{3,2},{4,5},{5,4},{6,7},{7,6},{8,9},{9,8},{10,11... | collective-permute-start | bytes 786440 | tf_op jit(solution)/shard_map/ppermute | solution.py:379
  13.5 1.2 %collective-permute-done.7.other = bf16[128,1024]{1,0:T(8,128)(2,1)S(1)} collective-permute-done((bf16[128,1024]{1,0:T(8,128)(2,1)S(1)}, bf16[128,1024]{1,0:T(8,128)(2,1)S(1)}, u32[]{:S(2)}, u32[]{:S(2)}) %collective-permute-start.7) | collective-permute-done | bytes 262176 | tf_op jit(solution)/shard_map/ppermute | solution.py:379
  14.7 0.8 %finish.1 = bf16[128,512]{1,0:T(8,128)(2,1)} custom-call(bf16[128,1024]{1,0:T(8,128)(2,1)S(1)} %attention.1.own, bf16[128,1024]{1,0:T(8,128)(2,1)S(1)} %collective-permute-done.7.other), custom_call_target="tpu_custom_call" | custom-call | tf_op jit(solution)/shard_map/finish/pallas_call | solution.py:380
  (5 shorter events, 0.0 us)
Async XLA Ops:
  1.3 9.6 %copy-start = (bf16[1024,512]{1,0:T(8,128)(2,1)S(1)}, bf16[1024,512]{1,0:T(8,128)(2,1)}, u32[]{:S(2)}) copy-start(bf16[1024,512]{1,0:T(8,128)(2,1)} %lookup.3) | copy-start | bytes 3145732
  1.3 9.6 %copy-start.1 = (bf16[512,1024]{1,0:T(8,128)(2,1)S(1)}, bf16[512,1024]{1,0:T(8,128)(2,1)}, u32[]{:S(2)}) copy-start(bf16[512,1024]{1,0:T(8,128)(2,1)} %final.3) | copy-start | bytes 3145732
  1.3 9.6 %copy-start.2 = (bf16[1024,512]{1,0:T(8,128)(2,1)S(1)}, bf16[1024,512]{1,0:T(8,128)(2,1)}, u32[]{:S(2)}) copy-start(bf16[1024,512]{1,0:T(8,128)(2,1)} %projection.1) | copy-start | bytes 3145732
  1.3 9.6 %copy-start.3 = (bf16[1024,512]{1,0:T(8,128)(2,1)S(1)}, bf16[1024,512]{1,0:T(8,128)(2,1)}, u32[]{:S(2)}) copy-start(bf16[1024,512]{1,0:T(8,128)(2,1)} %value_projection.1) | copy-start | bytes 3145732
  1.4 8.6 %collective-permute-start.1 = (bf16[24,1024]{1,0:T(8,128)(2,1)S(1)}, bf16[24,1024]{1,0:T(8,128)(2,1)S(1)}, u32[]{:S(2)}, u32[]{:S(2)}) collective-permute-start(bf16[24,1024]{1,0:T(8,128)(2,1)S(1)} %get-tuple-element.16.source.rest_0_), channel_id=1, source_target_pairs={{0,2},{1,7},{2,11},{3,8},{4,9},{5,6},{6,10},{7,13},{8,5},{9,14},{1... | collective-permute-start | bytes 147464 | tf_op jit(solution)/shard_map/ppermute | solution.py:350
  4.4 6.0 %collective-permute-start.2 = (bf16[24,1024]{1,0:T(8,128)(2,1)S(1)}, bf16[24,1024]{1,0:T(8,128)(2,1)S(1)}, u32[]{:S(2)}, u32[]{:S(2)}) collective-permute-start(bf16[24,1024]{1,0:T(8,128)(2,1)S(1)} %get-tuple-element.16.source.rest_0_), channel_id=1, source_target_pairs={{0,8},{1,11},{2,15},{3,4},{4,13},{5,2},{6,14},{7,9},{8,0},{9,3},{1... | collective-permute-start | bytes 147464 | tf_op jit(solution)/shard_map/ppermute | solution.py:350
  5.5 4.9 %collective-permute-start.3 = (bf16[24,1024]{1,0:T(8,128)(2,1)S(1)}, bf16[24,1024]{1,0:T(8,128)(2,1)S(1)}, u32[]{:S(2)}, u32[]{:S(2)}) collective-permute-start(bf16[24,1024]{1,0:T(8,128)(2,1)S(1)} %get-tuple-element.16.source.rest_0_), channel_id=1, source_target_pairs={{0,5},{1,12},{2,7},{3,0},{4,11},{5,14},{6,1},{7,2},{8,13},{9,6},{1... | collective-permute-start | bytes 147464 | tf_op jit(solution)/shard_map/ppermute | solution.py:350
  7.6 4.3 %collective-permute-start = (bf16[24,1024]{1,0:T(8,128)(2,1)S(1)}, bf16[24,1024]{1,0:T(8,128)(2,1)S(1)}, u32[]{:S(2)}, u32[]{:S(2)}) collective-permute-start(bf16[24,1024]{1,0:T(8,128)(2,1)S(1)} %again.1), channel_id=1, source_target_pairs={{0,14},{1,15},{2,13},{3,12},{4,0},{5,1},{6,4},{7,5},{8,10},{9,11},... | collective-permute-start | bytes 147464 | tf_op jit(solution)/shard_map/ppermute | solution.py:350
  9.9 1.9 %collective-permute-start.4 = (bf16[24,1024]{1,0:T(8,128)(2,1)S(1)}, bf16[24,1024]{1,0:T(8,128)(2,1)S(1)}, u32[]{:S(2)}, u32[]{:S(2)}) collective-permute-start(bf16[24,1024]{1,0:T(8,128)(2,1)S(1)} %collective-permute-done.1.rest_2_), channel_id=1, source_target_pairs={{0,1},{1,0},{2,3},{3,2},{4,5},{5,4},{6,7},{7,6},{8,9},{9,8},{10,11... | collective-permute-start | bytes 147464 | tf_op jit(solution)/shard_map/ppermute | solution.py:367
  10.4 1.5 %collective-permute-start.5 = (bf16[24,1024]{1,0:T(8,128)(2,1)S(1)}, bf16[24,1024]{1,0:T(8,128)(2,1)S(1)}, u32[]{:S(2)}, u32[]{:S(2)}) collective-permute-start(bf16[24,1024]{1,0:T(8,128)(2,1)S(1)} %collective-permute-done.2.rest_3_), channel_id=1, source_target_pairs={{0,1},{1,0},{2,3},{3,2},{4,5},{5,4},{6,7},{7,6},{8,9},{9,8},{10,11... | collective-permute-start | bytes 147464 | tf_op jit(solution)/shard_map/ppermute | solution.py:367
  10.4 1.4 %collective-permute-start.6 = (bf16[24,1024]{1,0:T(8,128)(2,1)S(1)}, bf16[24,1024]{1,0:T(8,128)(2,1)S(1)}, u32[]{:S(2)}, u32[]{:S(2)}) collective-permute-start(bf16[24,1024]{1,0:T(8,128)(2,1)S(1)} %collective-permute-done.3.rest_4_), channel_id=1, source_target_pairs={{0,1},{1,0},{2,3},{3,2},{4,5},{5,4},{6,7},{7,6},{8,9},{9,8},{10,11... | collective-permute-start | bytes 147464 | tf_op jit(solution)/shard_map/ppermute | solution.py:367
  13.1 1.6 %collective-permute-start.7 = (bf16[128,1024]{1,0:T(8,128)(2,1)S(1)}, bf16[128,1024]{1,0:T(8,128)(2,1)S(1)}, u32[]{:S(2)}, u32[]{:S(2)}) collective-permute-start(bf16[128,1024]{1,0:T(8,128)(2,1)S(1)} %attention.1.own), channel_id=1, source_target_pairs={{0,1},{1,0},{2,3},{3,2},{4,5},{5,4},{6,7},{7,6},{8,9},{9,8},{10,11... | collective-permute-start | bytes 786440 | tf_op jit(solution)/shard_map/ppermute | solution.py:379
